TPU v7x, 256 devices: a whole 4x4x8 slice. The times are simulated.
256 devices in a mesh: pool: 32 (over x, z_hi, y), tp: 8 (over z_lo, core).
Axes of the slice: x: 4, y: 4, z: 8 (z_hi: 2, z_lo: 4; z = z_hi * 4 + z_lo), core: 2. Of those that a mesh axis runs over, the one named last changes fastest.
Arguments:
- prefill_pages: bfloat16 [1024, 128, 2, 1024], P('pool', None, None, 'tp'), may hold values from -6 to 6
- page_owner: int32 [32, 32], P('pool'), may hold values from 0 to 31, as said below
- queries: bfloat16 [8192, 8192], P('pool', 'tp'), may hold values from -8 to 8
- suffix_cache: bfloat16 [8192, 16, 2, 1024], P('pool', None, None, 'tp'), may hold values from -10 to 10
- suffix_len: int32 [8192], P('pool'), may hold values from 1 to 16
- prefix_id: int32 [8192, 1], P('pool'), may hold values from 0 to 31; in each aligned block of 256 rows (0 to 255, 256 to 511, ...) at most 16 rows name the same one
- out_weight: bfloat16 [8192, 4096], P('tp'), may hold values from -0.25 to 0.25
Outputs:
- attended: bfloat16 [8192, 4096], P(('pool', 'tp'))
Inputs may be any that keep to these rules, and one draw needn't show every extreme that they name: Page j of device p becomes page j of the receptor cache of device page_owner[p, j]; every page of every receptor comes from exactly one device; pages 2k and 2k + 1 of a device go to the same device, so one device sends at most 2 pages to another. `prefix_id`: at most 16 of the sequences of one device name the same receptor, and on some device one receptor is named by exactly 16.
All inputs are finite; a program needn't handle non-finite values.
Results may differ from a plain program's by a relative error of at most 0.019.
Values may be sent and summed in bfloat16 or wider, within the bound.
No kernel may reach another device: no remote copies, remote signals or barrier semaphores. Data moves between devices by JAX's collectives and lax.ppermute only.
A program may use at most 64 MiB of HBM per device.

v0:
```python
import jax
import jax.numpy as jnp
from jax import lax
from jax.sharding import PartitionSpec as P

HD = 128
PAGE_CAP = 2
G = 8


def shared_attend(query_block, key_rows, value_rows, score_scale):
    scores = (
        jnp.einsum("rkgd,tkd->rkgt", query_block, key_rows, preferred_element_type=jnp.float32)
        * score_scale
    )
    highest = jnp.max(scores, axis=-1)
    exp_terms = jnp.exp(scores - highest[..., None])
    totals = jnp.sum(exp_terms, axis=-1)
    weights = exp_terms.astype(jnp.bfloat16)
    output = (
        jnp.einsum("rkgt,tkd->rkgd", weights, value_rows, preferred_element_type=jnp.float32)
        / totals[..., None]
    )
    return (output.astype(jnp.bfloat16), highest + jnp.log(totals))


def local(prefill_pages, page_owner, queries, suffix_cache, suffix_len, prefix_id, out_weight):
    pool_size = lax.axis_size("pool")
    pages_here = prefill_pages.shape[0]
    page_rows = prefill_pages.shape[1]
    kv_width = prefill_pages.shape[3]
    kv_local = kv_width // HD
    seq_here = queries.shape[0]
    query_width = queries.shape[1]
    score_scale = HD ** (-0.5)
    destination = page_owner[0]
    page_index = jnp.arange(pages_here, dtype=jnp.int32)
    earlier_same = jnp.sum(
        (
            (destination[None, :] == destination[:, None])
            & (page_index[None, :] < page_index[:, None])
        ).astype(jnp.int32),
        axis=1,
    )
    page_slot = destination * PAGE_CAP + earlier_same
    slot_index = jnp.arange(pool_size * PAGE_CAP, dtype=jnp.int32)
    page_pick = slot_index[:, None] == page_slot[None, :]
    outgoing = jnp.dot(
        page_pick.astype(jnp.bfloat16),
        prefill_pages.reshape(pages_here, -1),
        preferred_element_type=jnp.float32,
    ).astype(jnp.bfloat16)
    slot_anchor = jnp.sum(jnp.where(page_pick, page_index[None, :] + 1, 0), axis=1) - 1
    incoming, arrived_from = (
        lax.all_to_all(outgoing, "pool", split_axis=0, concat_axis=0, tiled=True),
        lax.all_to_all(slot_anchor, "pool", split_axis=0, concat_axis=0, tiled=True),
    )
    placing = (page_index[:, None] == arrived_from[None, :]).astype(jnp.bfloat16)
    receptor = jnp.dot(placing, incoming, preferred_element_type=jnp.float32).astype(jnp.bfloat16)
    receptor = receptor.reshape(pages_here * page_rows, 2, kv_local, HD)
    receptor_keys = receptor[:, 0]
    receptor_values = receptor[:, 1]
    routed = prefix_id[:, 0]
    seq_index = jnp.arange(seq_here, dtype=jnp.int32)
    query_rank = jnp.sum(
        ((routed[None, :] == routed[:, None]) & (seq_index[None, :] < seq_index[:, None])).astype(
            jnp.int32
        ),
        axis=1,
    )
    capacity = max(2, (2 * seq_here + pool_size - 1) // pool_size)
    query_slot = routed * capacity + query_rank
    query_pick = (
        jnp.arange(pool_size * capacity, dtype=jnp.int32)[:, None] == query_slot[None, :]
    ).astype(jnp.bfloat16)
    dispatched = jnp.dot(query_pick, queries, preferred_element_type=jnp.float32).astype(
        jnp.bfloat16
    )
    dispatched = dispatched.reshape(pool_size, capacity, query_width)
    arrived = lax.all_to_all(dispatched, "pool", split_axis=0, concat_axis=0, tiled=True)
    peer_count = arrived.shape[0]
    item_count = arrived.shape[1]
    grouped = arrived.reshape(peer_count // 4, 4 * item_count, kv_local, G, HD)

    def one_group(group_rows):
        return shared_attend(group_rows, receptor_keys, receptor_values, score_scale)

    outputs, lse_rows = lax.map(one_group, grouped)
    replies = outputs.astype(jnp.float32).reshape(peer_count, item_count, query_width)
    reply_lse = lse_rows.reshape(peer_count, item_count, kv_local * G)
    returned = lax.all_to_all(replies, "pool", split_axis=0, concat_axis=0, tiled=True)
    returned_lse = lax.all_to_all(reply_lse, "pool", split_axis=0, concat_axis=0, tiled=True)
    prefix_part = jnp.take(returned.reshape(pool_size * capacity, query_width), query_slot, axis=0)
    prefix_part = prefix_part.reshape(seq_here, kv_local, G, HD)
    prefix_lse = jnp.take(
        returned_lse.reshape(pool_size * capacity, kv_local * G), query_slot, axis=0
    )
    prefix_lse = prefix_lse.reshape(seq_here, kv_local, G)
    suffix_rows = suffix_cache.shape[1]
    own_queries = queries.reshape(seq_here, kv_local, G, HD)
    suffix_split = suffix_cache.reshape(seq_here, suffix_rows, 2, kv_local, HD)
    scores = (
        jnp.einsum(
            "skgd,stkd->skgt",
            own_queries,
            suffix_split[:, :, 0],
            preferred_element_type=jnp.float32,
        )
        * score_scale
    )
    in_length = (jnp.arange(suffix_rows, dtype=jnp.int32)[None, :] < suffix_len[:, None])[
        :, None, None, :
    ]
    scores = jnp.where(in_length, scores, -1e30)
    highest = jnp.max(scores, axis=-1)
    exp_terms = jnp.where(in_length, jnp.exp(scores - highest[..., None]), 0.0)
    totals = jnp.sum(exp_terms, axis=-1)
    weights = exp_terms.astype(jnp.bfloat16)
    suffix_part = (
        jnp.einsum(
            "skgt,stkd->skgd", weights, suffix_split[:, :, 1], preferred_element_type=jnp.float32
        )
        / totals[..., None]
    )
    suffix_lse = highest + jnp.log(totals)
    merged_top = jnp.maximum(prefix_lse, suffix_lse)
    prefix_share = jnp.exp(prefix_lse - merged_top)
    suffix_share = jnp.exp(suffix_lse - merged_top)
    attention = (prefix_share[..., None] * prefix_part + suffix_share[..., None] * suffix_part) / (
        prefix_share + suffix_share
    )[..., None]
    attention = attention.astype(jnp.bfloat16).reshape(seq_here, query_width)
    return lax.psum_scatter(
        jnp.dot(attention, out_weight, preferred_element_type=jnp.float32).astype(jnp.bfloat16),
        "tp",
        scatter_dimension=0,
        tiled=True,
    )


def solution(mesh):
    in_specs = (
        P("pool", None, None, "tp"),
        P("pool", None),
        P("pool", "tp"),
        P("pool", None, None, "tp"),
        P("pool"),
        P("pool", None),
        P("tp", None),
    )
    out_specs = P(("pool", "tp"), None)
    return jax.shard_map(local, mesh=mesh, in_specs=in_specs, out_specs=out_specs, check_vma=False)
```

profile of v0, /device:TPU:1, one launch (start us, length us, event | category | flops | bytes accessed | tf_op | source)
XLA Modules:
  0.0 357.0 jit_solution(10910022565209062524)
XLA Ops:
  8.9 14.5 %all-to-all-start.1 = ((s32[32,2,1]{1,2,0:T(1,128)}), s32[32,2,1]{1,2,0:T(1,128)S(1)}, u32[]{:S(2)}, u32[]{:S(2)}) async-start(s32[32,2,1]{1,2,0:T(1,128)} %bitcast.22), calls=%async_computation.1 | async-start | bytes 32768 | tf_op jit(solution)/shard_map/all_to_all | solution.py:56
  25.1 2.6 convolution_convert_fusion.3
  27.6 6.8 %all-to-all-done.1 = s32[32,2,1]{1,2,0:T(1,128)S(1)} async-done(((s32[32,2,1]{1,2,0:T(1,128)}), s32[32,2,1]{1,2,0:T(1,128)S(1)}, u32[]{:S(2)}, u32[]{:S(2)}) %all-to-all-start.1) | async-done | bytes 288 | tf_op jit(solution)/shard_map/all_to_all | solution.py:56
  34.4 4.8 %all-to-all-start = ((bf16[32,16,1024]{2,1,0:T(8,128)(2,1)}), bf16[32,16,1024]{2,1,0:T(8,128)(2,1)S(1)}, u32[]{:S(2)}, u32[]{:S(2)}) async-start(bf16[32,16,1024]{2,1,0:T(8,128)(2,1)} %bitcast.18), calls=%async_computation | async-start | bytes 2097152 | tf_op jit(solution)/shard_map/all_to_all | solution.py:80
  39.3 3.3 reshape.289
  42.6 3.3 convolution_convert_fusion
  45.9 7.6 %all_to_all.23 = bf16[32,2,32768]{2,1,0:T(2,128)(2,1)} reshape(bf16[64,32768]{1,0:T(8,128)(2,1)} %convolution_convert_fusion) | data formatting | bytes 8388608 | tf_op jit(solution)/shard_map/all_to_all | solution.py:55
  53.5 7.0 %all-to-all-done = bf16[32,16,1024]{2,1,0:T(8,128)(2,1)S(1)} async-done(((bf16[32,16,1024]{2,1,0:T(8,128)(2,1)}), bf16[32,16,1024]{2,1,0:T(8,128)(2,1)S(1)}, u32[]{:S(2)}, u32[]{:S(2)}) %all-to-all-start) | async-done | bytes 1048608 | tf_op jit(solution)/shard_map/all_to_all | solution.py:80
  60.5 4.9 %all-to-all-start.2 = ((bf16[32,2,32768]{2,1,0:T(2,128)(2,1)}), bf16[32,2,32768]{2,1,0:T(2,128)(2,1)}, u32[]{:S(2)}, u32[]{:S(2)}) async-start(bf16[32,2,32768]{2,1,0:T(2,128)(2,1)} %all_to_all.23), calls=%async_computation.2 | async-start | bytes 8388608 | tf_op jit(solution)/shard_map/all_to_all | solution.py:55
  68.1 44.8 %all-to-all-done.2 = bf16[32,2,32768]{2,1,0:T(2,128)(2,1)} async-done(((bf16[32,2,32768]{2,1,0:T(2,128)(2,1)}), bf16[32,2,32768]{2,1,0:T(2,128)(2,1)}, u32[]{:S(2)}, u32[]{:S(2)}) %all-to-all-start.2) | async-done | bytes 4194336 | tf_op jit(solution)/shard_map/all_to_all | solution.py:55
  112.9 7.2 %all_to_all.25 = bf16[64,32768]{1,0:T(8,128)(2,1)} reshape(bf16[32,2,32768]{2,1,0:T(2,128)(2,1)} %all-to-all-done.2) | data formatting | bytes 8388608 | tf_op jit(solution)/shard_map/all_to_all | solution.py:55
  120.1 4.2 %convolution_convert_fusion.1 = bf16[32,32768]{1,0:T(8,128)(2,1)} fusion(bf16[64,32768]{1,0:T(8,128)(2,1)} %all_to_all.25, s32[64]{0:T(128)S(1)} %eq.89), kind=kOutput, calls=%fused_computation.23 | convolution fusion | flops 135268352 | bytes 6291712 | tf_op jit(solution)/shard_map/dot_general | solution.py:59
  124.3 3.2 reshape.290
  127.6 3.0 fusion.54
  131.8 42.1 %while.12 = (s32[]{:T(128)}, bf16[8,64,1,8,128]{4,3,1,2,0:T(8,128)(2,1)S(1)}, f32[8,64,1,8]{3,1,2,0:T(8,128)S(1)}, bf16[8,64,1,8,128]{4,3,1,2,0:T(8,128)(2,1)}, ...) while((s32[]{:T(128)}, bf16[8,64,1,8,128]{4,3,1,2,0:T(8,128)(2,1)S(1)}, ...), condition=%wide.region_6.7_spmd, body=%wide.region_3.6_spmd.sunk | while | flops 1090649600 | bytes 27695700 | solution.py:88
  131.8 2.2 bitcast_reduce_fusion.2
  134.0 1.5 fusion.67
  135.5 1.5 fusion.68
  137.0 2.2 bitcast_reduce_fusion.2
  139.3 1.5 fusion.67
  140.8 1.5 fusion.68
  142.3 2.2 bitcast_reduce_fusion.2
  144.5 1.5 fusion.67
  146.1 1.5 fusion.68
  147.6 2.2 bitcast_reduce_fusion.2
  149.8 1.5 fusion.67
  151.3 1.5 fusion.68
  152.8 2.2 bitcast_reduce_fusion.2
  155.1 1.5 fusion.67
  156.6 1.5 fusion.68
  158.1 2.2 bitcast_reduce_fusion.2
  160.3 1.5 fusion.67
  161.9 1.5 fusion.68
  163.4 2.2 bitcast_reduce_fusion.2
  165.6 1.5 fusion.67
  167.1 1.5 fusion.68
  168.6 2.2 bitcast_reduce_fusion.2
  170.9 1.5 fusion.67
  172.4 1.5 fusion.68
  174.8 12.1 %all-to-all-start.3 = ((f32[32,1,128]{2,1,0:T(1,128)}), f32[32,1,128]{2,1,0:T(1,128)S(1)}, u32[]{:S(2)}, u32[]{:S(2)}) async-start(f32[32,1,128]{2,1,0:T(1,128)} %reshape.331), calls=%async_computation.3 | async-start | bytes 32768 | tf_op jit(solution)/shard_map/all_to_all | solution.py:92
  186.8 1.5 reshape.302
  188.4 9.2 %all-to-all-done.3 = f32[32,1,128]{2,1,0:T(1,128)S(1)} async-done(((f32[32,1,128]{2,1,0:T(1,128)}), f32[32,1,128]{2,1,0:T(1,128)S(1)}, u32[]{:S(2)}, u32[]{:S(2)}) %all-to-all-start.3) | async-done | bytes 16416 | tf_op jit(solution)/shard_map/all_to_all | solution.py:92
  197.6 4.0 %all-to-all-start.4 = ((f32[32,16,1024]{2,1,0:T(8,128)}), f32[32,16,1024]{2,1,0:T(8,128)S(1)}, u32[]{:S(2)}, u32[]{:S(2)}) async-start(f32[32,16,1024]{2,1,0:T(8,128)} %reshape.302), calls=%async_computation.4 | async-start | bytes 4194304 | tf_op jit(solution)/shard_map/all_to_all | solution.py:91
  201.7 1.9 copy.74
  214.0 8.2 %all-to-all-done.4 = f32[32,16,1024]{2,1,0:T(8,128)S(1)} async-done(((f32[32,16,1024]{2,1,0:T(8,128)}), f32[32,16,1024]{2,1,0:T(8,128)S(1)}, u32[]{:S(2)}, u32[]{:S(2)}) %all-to-all-start.4) | async-done | bytes 2097184 | tf_op jit(solution)/shard_map/all_to_all | solution.py:91
  225.4 1.5 fusion.32
  226.9 7.1 %convolution_convert_fusion.2 = bf16[256,4096]{1,0:T(8,128)(2,1)} fusion(bf16[1024,4096]{1,0:T(8,128)(2,1)} %param.15, bf16[32,8,8,128]{3,2,1,0:T(8,128)(2,1)S(1)} %bitcast.169), kind=kOutput, calls=%fused_computation.24 | convolution fusion | flops 2148532224 | bytes 11010048 | tf_op jit(solution)/shard_map/dot_general | solution.py:134
  234.0 116.1 %reduce-scatter.2.cloned.1.call-done = bf16[32,4096]{1,0:T(8,128)(2,1)} async-done(((bf16[256,4096]{1,0:T(8,128)(2,1)}), bf16[32,4096]{1,0:T(8,128)(2,1)}) %reduce-scatter.2.cloned.1.call-update) | async-done | bytes 262160 | tf_op jit(solution)/shard_map/reduce_scatter | solution.py:133
  (74 shorter events, 22.4 us)
Async XLA Ops:
  8.9 25.5 %all-to-all-start.1 = ((s32[32,2,1]{1,2,0:T(1,128)}), s32[32,2,1]{1,2,0:T(1,128)S(1)}, u32[]{:S(2)}, u32[]{:S(2)}) async-start(s32[32,2,1]{1,2,0:T(1,128)} %bitcast.22), calls=%async_computation.1 | async-start | bytes 32768 | tf_op jit(solution)/shard_map/all_to_all | solution.py:56
  34.4 26.1 %all-to-all-start = ((bf16[32,16,1024]{2,1,0:T(8,128)(2,1)}), bf16[32,16,1024]{2,1,0:T(8,128)(2,1)S(1)}, u32[]{:S(2)}, u32[]{:S(2)}) async-start(bf16[32,16,1024]{2,1,0:T(8,128)(2,1)} %bitcast.18), calls=%async_computation | async-start | bytes 2097152 | tf_op jit(solution)/shard_map/all_to_all | solution.py:80
  60.5 52.3 %all-to-all-start.2 = ((bf16[32,2,32768]{2,1,0:T(2,128)(2,1)}), bf16[32,2,32768]{2,1,0:T(2,128)(2,1)}, u32[]{:S(2)}, u32[]{:S(2)}) async-start(bf16[32,2,32768]{2,1,0:T(2,128)(2,1)} %all_to_all.23), calls=%async_computation.2 | async-start | bytes 8388608 | tf_op jit(solution)/shard_map/all_to_all | solution.py:55
  130.5 1.2 copy-start.5
  174.8 22.9 %all-to-all-start.3 = ((f32[32,1,128]{2,1,0:T(1,128)}), f32[32,1,128]{2,1,0:T(1,128)S(1)}, u32[]{:S(2)}, u32[]{:S(2)}) async-start(f32[32,1,128]{2,1,0:T(1,128)} %reshape.331), calls=%async_computation.3 | async-start | bytes 32768 | tf_op jit(solution)/shard_map/all_to_all | solution.py:92
  188.4 15.2 %copy-start.4 = (bf16[256,1024]{1,0:T(8,128)(2,1)S(1)}, bf16[256,1024]{1,0:T(8,128)(2,1)}, u32[]{:S(2)}) copy-start(bf16[256,1024]{1,0:T(8,128)(2,1)} %param.11) | copy-start | bytes 1572868
  188.4 15.3 %copy-start.12 = (s32[256]{0:T(256)S(1)}, s32[256]{0:T(256)}, u32[]{:S(2)}) copy-start(s32[256]{0:T(256)} %param.13) | copy-start | bytes 3076
  197.6 24.5 %all-to-all-start.4 = ((f32[32,16,1024]{2,1,0:T(8,128)}), f32[32,16,1024]{2,1,0:T(8,128)S(1)}, u32[]{:S(2)}, u32[]{:S(2)}) async-start(f32[32,16,1024]{2,1,0:T(8,128)} %reshape.302), calls=%async_computation.4 | async-start | bytes 4194304 | tf_op jit(solution)/shard_map/all_to_all | solution.py:91
  201.7 6.2 %copy-start.10 = (s32[256,1]{0,1:T(1,128)S(1)}, s32[256,1]{0,1:T(1,128)}, u32[]{:S(2)}) copy-start(s32[256,1]{0,1:T(1,128)} %param.14) | copy-start | bytes 3076
  201.7 148.4 %reduce-scatter.2.cloned.1.call-start = ((), (), s32[]{:S(2)}) async-start(), calls=%async_computation.6 | async-start | bytes 2359296 | tf_op jit(solution)/shard_map/reduce_scatter | solution.py:133
  203.6 1.3 copy-start
  203.8 5.8 %copy-start.6 = (pred[256,16]{1,0:T(8,128)(4,1)}, pred[256,16]{1,0:T(8,128)(4,1)S(1)}, u32[]{:S(2)}) copy-start(pred[256,16]{1,0:T(8,128)(4,1)S(1)} %iota_compare_fusion.3) | copy-start | bytes 12292
  205.7 4.8 %copy-start.2 = (f32[256,8,16]{2,1,0:T(8,128)}, f32[256,8,16]{2,1,0:T(8,128)S(1)}, u32[]{:S(2)}) copy-start(f32[256,8,16]{2,1,0:T(8,128)S(1)} %get-tuple-element.62) | copy-start | bytes 393220
  222.2 1.6 copy-start.11
  223.5 1.6 copy-start.1
  223.5 1.8 copy-start.3
  223.5 1.8 copy-start.7
  223.5 1.8 copy-start.8
  223.5 1.9 copy-start.9
Sparse Core Ops, SparseCore 0:
  234.1 115.9 reduce-scatter.1
where the time goes:
time: 360 us; the launch traced here: 357 us
  waiting for transfers between devices  192 us (53%)
  matrix products  49.2 us (14%)
  local copies, waits for them, and re-layouts  40.6 us (11%)
  starting transfers between devices  40.3 us (11%)
  other arithmetic  20.7 us (6%)
  between operations  13.7 us (4%)
    reduce_scatter x1, waiting for transfers between devices, local(): lax.psum_scatter(jnp.dot(attention, out_weight, preferred_element_type=jn...  116 us
    all_to_all x1, waiting for transfers between devices, local(): lax.all_to_all(outgoing, 'pool', split_axis=0, concat_axis=0, tiled=True)  44.8 us
    dot_general x8, matrix products, shared_attend(): jnp.einsum('rkgd,tkd->rkgt', query_block, key_rows, preferred_element_typ...  17.9 us
    all_to_all x2, local copies, waits for them, and re-layouts, local(): lax.all_to_all(outgoing, 'pool', split_axis=0, concat_axis=0, tiled=True)  14.8 us
    all_to_all x1, starting transfers between devices, local(): lax.all_to_all(slot_anchor, 'pool', split_axis=0, concat_axis=0, tiled=True)  14.5 us
    all_to_all x1, starting transfers between devices, local(): lax.all_to_all(reply_lse, 'pool', split_axis=0, concat_axis=0, tiled=True)  12.1 us
    reduce_sum x8, other arithmetic, shared_attend(): totals = jnp.sum(exp_terms, axis=-1)  11.9 us
    dot_general x8, matrix products, shared_attend(): jnp.einsum('rkgt,tkd->rkgd', weights, value_rows, preferred_element_type=...  11.9 us
  transfers between devices with their start and end apart: 6, of which 6 were waited for; matrix products, arithmetic and copies ran while one was open for 7% of the time, Pallas kernels for 0%

commit v1 on v0

v1 whole, which is shorter than its diff:
```python
import functools

import jax
import jax.numpy as jnp
from jax import lax
from jax.experimental import pallas as pl
from jax.experimental.pallas import tpu as pltpu
from jax.sharding import Mesh
from jax.sharding import PartitionSpec as P

HD = 128
G = 8
CAP = 16
PLANE = ("x", "y")
SCALE = HD**-0.5
LOG2E = 1.4426950408889634
MARK = 16384.0
LOW = -1e30
F32 = jnp.float32
BF16 = jnp.bfloat16


def slot_base(ids):
    return (((ids >> 3) * 4 + (ids & 3)) * 2 + ((ids >> 2) & 1)) * CAP


def slots_as_row(ids_col, ids_row):
    n = ids_row.shape[1]
    i = lax.broadcasted_iota(jnp.int32, (n, n), 0)
    j = lax.broadcasted_iota(jnp.int32, (n, n), 1)
    earlier = jnp.where((ids_col == ids_row) & (i < j), 1.0, 0.0)
    rank = jnp.sum(earlier, axis=0, keepdims=True).astype(jnp.int32)
    return slot_base(ids_row) + rank


def slots_as_col(ids_col, ids_row):
    n = ids_row.shape[1]
    i = lax.broadcasted_iota(jnp.int32, (n, n), 0)
    j = lax.broadcasted_iota(jnp.int32, (n, n), 1)
    earlier = jnp.where((ids_col == ids_row) & (j < i), 1.0, 0.0)
    rank = jnp.sum(earlier, axis=1, keepdims=True).astype(jnp.int32)
    return slot_base(ids_col) + rank


def dispatch_kernel(col_ref, row_ref, q_ref, out_ref):
    slot = slots_as_row(col_ref[...], row_ref[...])
    rows, n = out_ref.shape[0], slot.shape[1]
    pick = jnp.where(lax.broadcasted_iota(jnp.int32, (rows, n), 0) == slot, 1.0, 0.0)
    out_ref[...] = jnp.dot(pick.astype(BF16), q_ref[...], preferred_element_type=F32).astype(BF16)


def dispatch(ids_col, ids_row, queries, rows):
    return pl.pallas_call(
        dispatch_kernel,
        out_shape=jax.ShapeDtypeStruct((rows, queries.shape[1]), BF16),
        compiler_params=pltpu.CompilerParams(vmem_limit_bytes=32 * 2**20),
        cost_estimate=pl.CostEstimate(
            flops=2 * rows * queries.shape[0] * queries.shape[1], bytes_accessed=2**21, transcendentals=0
        ),
        name="dispatch",
    )(ids_col, ids_row, queries)


def place_kernel(pick_ref, pages_ref, out_ref, sem):
    copies = [
        pltpu.make_async_copy(pages_ref.at[pick_ref[s]], out_ref.at[s], sem.at[s])
        for s in range(out_ref.shape[0])
    ]
    for copy in copies:
        copy.start()
    for copy in copies:
        copy.wait()


def place(pick, pages, slots):
    return pl.pallas_call(
        place_kernel,
        out_shape=jax.ShapeDtypeStruct((slots,) + pages.shape[1:], BF16),
        in_specs=[
            pl.BlockSpec(memory_space=pltpu.SMEM),
            pl.BlockSpec(memory_space=pl.ANY),
        ],
        out_specs=pl.BlockSpec(memory_space=pl.ANY),
        scratch_shapes=[pltpu.SemaphoreType.DMA((slots,))],
        cost_estimate=pl.CostEstimate(flops=0, bytes_accessed=2**23, transcendentals=0),
        name="place",
    )(pick, pages)


def attend_kernel(width, q_ref, kv_ref, out_ref, list_ref, s_ref, acc_ref):
    sub = pl.program_id(0)
    peers, span = kv_ref.shape[0], kv_ref.shape[1] // 4
    group, cap = q_ref.shape[0], q_ref.shape[1]
    key_at = pl.multiple_of(sub * 2 * span, 2 * span)

    @pl.when(pl.program_id(1) == 0)
    def _():
        def scan(src, n):
            tile = kv_ref[src, pl.ds(key_at, 16), :].astype(F32)
            list_ref[n] = src
            return n + (jnp.max(tile) < MARK / 2).astype(jnp.int32)

        list_ref[peers] = lax.fori_loop(0, peers, scan, 0)

    count = list_ref[peers]
    heads = [(j, h) for j in range(group) for h in range(G)]
    q = jnp.concatenate([q_ref[j, :, h * HD : (h + 1) * HD] for j, h in heads], axis=0)

    def score(i, top):
        key = kv_ref[list_ref[i], pl.ds(key_at, span), :]
        s = lax.dot_general(q, key, (((1,), (1,)), ((), ())), preferred_element_type=F32)
        s_ref[i] = s
        for c in range(0, span, HD):
            top = jnp.maximum(top, s[:, c : c + HD])
        return top

    top = lax.fori_loop(0, count, score, jnp.full(q.shape, LOW, F32))
    top = jnp.max(top, axis=1, keepdims=True)
    acc_ref[...] = jnp.zeros_like(acc_ref)
    ones = jnp.ones((span, HD), BF16)

    def gather(i, carry):
        value = kv_ref[list_ref[i], pl.ds(key_at + span, span), :]
        p = jnp.exp2((s_ref[i] - top) * (SCALE * LOG2E)).astype(BF16)
        acc_ref[...] += jnp.dot(
            p, jnp.concatenate([value, ones], axis=1), preferred_element_type=F32
        )
        return carry

    lax.fori_loop(0, count, gather, 0)
    total = acc_ref[:, HD:]
    some = total > 0.0
    total = jnp.where(some, total, 1.0)
    out = (acc_ref[:, :HD] / total).astype(BF16)
    lse = jnp.where(some, top * SCALE + jnp.log(total), LOW)
    lane = lax.broadcasted_iota(jnp.int32, (cap, HD), 1)
    for j in range(group):
        packed = jnp.zeros((cap, HD), F32)
        for h in range(G):
            at = (j * G + h) * cap
            out_ref[j, :, h * HD : (h + 1) * HD] = out[at : at + cap]
            packed = jnp.where((lane & 7) == h, lse[at : at + cap], packed)
        first = packed.astype(BF16).astype(F32)
        second = (packed - first).astype(BF16).astype(F32)
        third = packed - first - second
        part = jnp.where(lane < 8, first, jnp.where(lane < 16, second, third))
        out_ref[j, :, width:] = jnp.where(lane < 24, part, 0.0).astype(BF16)


def attend(q, kv, name):
    peers, rows, width = q.shape
    group = 4
    span = kv.shape[1] // 4
    m = group * CAP * G
    return pl.pallas_call(
        functools.partial(attend_kernel, width),
        grid=(2, peers // group),
        out_shape=jax.ShapeDtypeStruct((peers, rows, width + HD), BF16),
        in_specs=[
            pl.BlockSpec((group, CAP, width), lambda s, i: (i, s, 0)),
            pl.BlockSpec(memory_space=pltpu.VMEM),
        ],
        out_specs=pl.BlockSpec((group, CAP, width + HD), lambda s, i: (i, s, 0)),
        scratch_shapes=[
            pltpu.SMEM((peers + 1,), jnp.int32),
            pltpu.VMEM((peers, m, span), F32),
            pltpu.VMEM((m, 2 * HD), F32),
        ],
        compiler_params=pltpu.CompilerParams(vmem_limit_bytes=40 * 2**20),
        cost_estimate=pl.CostEstimate(
            flops=4 * peers * rows * G * 8 * span * HD,
            bytes_accessed=6 * 2**20,
            transcendentals=peers * rows * G * 8 * span,
        ),
        name=name,
    )(q, kv)


def collect_kernel(col_ref, row_ref, replies_ref, out_ref):
    slot = slots_as_col(col_ref[...], row_ref[...])
    n, width = slot.shape[0], replies_ref.shape[1]
    pick = jnp.where(lax.broadcasted_iota(jnp.int32, (n, replies_ref.shape[0]), 1) == slot, 1.0, 0.0)
    rows = jnp.dot(pick.astype(BF16), replies_ref[...], preferred_element_type=F32).astype(BF16)
    out_ref[:, :width] = rows[: n // 2]
    out_ref[:, width:] = rows[n // 2 :]


def collect(ids_col, ids_row, replies):
    n = ids_col.shape[0]
    return pl.pallas_call(
        collect_kernel,
        out_shape=jax.ShapeDtypeStruct((n // 2, 2 * replies.shape[1]), BF16),
        compiler_params=pltpu.CompilerParams(vmem_limit_bytes=32 * 2**20),
        cost_estimate=pl.CostEstimate(
            flops=2 * n * replies.shape[0] * replies.shape[1], bytes_accessed=2**21, transcendentals=0
        ),
        name="collect",
    )(ids_col, ids_row, replies)


def merge_kernel(me_ref, col_ref, row_ref, own_ref, far_ref, suf_ref, suf_lse_ref, w_ref, send_ref, keep_ref, att_ref):
    @pl.when(pl.program_id(0) == 0)
    def _():
        n, width = suf_ref.shape
        slot = slots_as_col(col_ref[...], row_ref[...])
        pick = jnp.where(lax.broadcasted_iota(jnp.int32, (n, own_ref.shape[0]), 1) == slot, 1.0, 0.0)
        own = jnp.dot(pick.astype(BF16), own_ref[...], preferred_element_type=F32)
        far = jnp.concatenate([far_ref[:, : width + HD], far_ref[:, width + HD :]], axis=0)
        i = lax.broadcasted_iota(jnp.int32, (HD, width), 0)
        c = lax.broadcasted_iota(jnp.int32, (HD, width), 1)
        spread = jnp.where((i < 24) & ((i & 7) == (c >> 7)), 1.0, 0.0).astype(BF16)
        own_lse = jnp.dot(own[:, width:].astype(BF16), spread, preferred_element_type=F32)
        far_lse = jnp.dot(far[:, width:], spread, preferred_element_type=F32)
        suf_lse = suf_lse_ref[...]
        top = jnp.maximum(jnp.maximum(own_lse, far_lse), suf_lse)
        a = jnp.exp(own_lse - top)
        b = jnp.exp(far_lse - top)
        s = jnp.exp(suf_lse - top)
        att = (a * own[:, :width] + b * far[:, :width].astype(F32) + s * suf_ref[...]) / (a + b + s)
        att_ref[0] = att.astype(BF16)
        me = me_ref[0]
        step = n // 8
        for q in range(8):
            flip = (1 - q // 4) + 2 * (1 - (q // 2) % 2) + 4 * (1 - q % 2)
            at = pl.multiple_of((me ^ flip) * step, step)
            att_ref[1, q * step : (q + 1) * step] = att_ref[0, pl.ds(at, step), :]

    half = send_ref.shape[0]
    out = jnp.dot(att_ref[1], w_ref[...], preferred_element_type=F32).astype(BF16)
    send_ref[...] = out[:half]
    keep_ref[...] = out[half:]


def merge_project(me, ids_col, ids_row, own, far, suf, suf_lse, weight):
    n, width = suf.shape
    columns = weight.shape[1]
    tile = 512
    whole = pl.BlockSpec(memory_space=pltpu.VMEM)
    shape = jax.ShapeDtypeStruct((n // 2, columns), BF16)
    block = pl.BlockSpec((n // 2, tile), lambda c: (0, c))
    return pl.pallas_call(
        merge_kernel,
        grid=(columns // tile,),
        out_shape=(shape, shape),
        in_specs=[pl.BlockSpec(memory_space=pltpu.SMEM)]
        + [whole] * 6
        + [pl.BlockSpec((width, tile), lambda c: (0, c))],
        out_specs=(block, block),
        scratch_shapes=[pltpu.VMEM((2, n, width), BF16)],
        compiler_params=pltpu.CompilerParams(vmem_limit_bytes=40 * 2**20),
        cost_estimate=pl.CostEstimate(
            flops=2 * n * width * columns, bytes_accessed=16 * 2**20, transcendentals=3 * n * width
        ),
        name="merge_project",
    )(me, ids_col, ids_row, own, far, suf, suf_lse, weight)


def suffix_attend(queries, suffix_cache, suffix_len):
    seq, width = queries.shape
    rows = suffix_cache.shape[1]
    heads = queries.reshape(seq, width // HD, HD)
    scores = (
        jnp.einsum("sgd,std->sgt", heads, suffix_cache[:, :, 0], preferred_element_type=F32) * SCALE
    )
    in_length = (jnp.arange(rows, dtype=jnp.int32)[None, :] < suffix_len[:, None])[:, None, :]
    scores = jnp.where(in_length, scores, LOW)
    highest = jnp.max(scores, axis=-1)
    exp_terms = jnp.where(in_length, jnp.exp(scores - highest[..., None]), 0.0)
    totals = jnp.sum(exp_terms, axis=-1)
    out = (
        jnp.einsum("sgt,std->sgd", exp_terms.astype(BF16), suffix_cache[:, :, 1], preferred_element_type=F32)
        / totals[..., None]
    )
    lse = jnp.broadcast_to((highest + jnp.log(totals))[..., None], out.shape)
    return out.reshape(seq, width), lse.reshape(seq, width)


def swap(value, axis, bit):
    size = lax.axis_size(axis)
    return lax.ppermute(value, axis, [(i, i ^ bit) for i in range(size)])


def local(prefill_pages, page_owner, queries, suffix_cache, suffix_len, prefix_id, out_weight):
    plane = lax.axis_size("x") * lax.axis_size("y")
    pages, page = prefill_pages.shape[:2]
    seq, width = queries.shape
    pairs = pages // 2
    ids_col, ids_row = prefix_id, prefix_id.reshape(1, seq)
    far_row = swap(ids_row, "zh", 1)
    far_col = far_row.reshape(seq, 1)

    sent = dispatch(ids_col, ids_row, queries, plane * 2 * CAP).reshape(plane, 2 * CAP, width)
    own_q = lax.all_to_all(sent, PLANE, 0, 0, tiled=True)

    owner = page_owner[0, ::2]
    slot = slot_base(owner) // CAP
    here = jnp.arange(2 * plane, dtype=jnp.int32)[:, None] == slot[None, :]
    pick = pairs + jnp.sum(jnp.where(here, jnp.arange(pairs, dtype=jnp.int32)[None, :] - pairs, 0), axis=1)
    paired = jnp.swapaxes(prefill_pages.reshape(pairs, 2 * page, 2, HD), 1, 2)
    paired = paired.reshape(pairs, 4 * page, HD)
    paired = jnp.pad(paired, ((0, 1), (0, 0), (0, 0)), constant_values=MARK)
    placed = place(pick, paired, 2 * plane).reshape(plane, 8 * page, HD)
    placed, own_q = lax.optimization_barrier((placed, own_q))
    kv = lax.all_to_all(placed, PLANE, 0, 0, tiled=True)
    far_q = swap(own_q, "zh", 1)

    suf, suf_lse = suffix_attend(queries, suffix_cache, suffix_len)

    far_out = attend(far_q, kv, "attend_far")
    far_back = lax.all_to_all(far_out, PLANE, 0, 0, tiled=True)
    own_out = attend(own_q, kv, "attend_own")
    far_back, own_out = lax.optimization_barrier((far_back, own_out))
    own_back = lax.all_to_all(own_out, PLANE, 0, 0, tiled=True)
    far_part = collect(far_col, far_row, far_back.reshape(plane * 2 * CAP, width + HD))
    far_part = swap(far_part, "zh", 1)

    me = (lax.axis_index("zl") * 2 + lax.axis_index("core")).astype(jnp.int32).reshape(1)
    send, keep = merge_project(
        me, ids_col, ids_row, own_back.reshape(plane * 2 * CAP, width + HD), far_part, suf, suf_lse, out_weight
    )

    def add(a, b):
        return (a.astype(F32) + b.astype(F32)).astype(BF16)

    got = swap(send, "core", 1)
    half = seq // 4
    send, keep = add(keep[:half], got[:half]), add(keep[half:], got[half:])
    got = swap(send, "zl", 1)
    half = seq // 8
    send, keep = add(keep[:half], got[:half]), add(keep[half:], got[half:])
    return add(keep, swap(send, "zl", 2))


def solution(mesh):
    x, zh, y, zl, core = 4, 2, 4, 4, 2
    names = ("x", "zh", "y", "zl", "core")
    fine = Mesh(mesh.devices.reshape(x, zh, y, zl, core), names)
    pool, tp = ("x", "zh", "y"), ("zl", "core")
    in_specs = (
        P(pool, None, None, tp),
        P(pool, None),
        P(pool, tp),
        P(pool, None, None, tp),
        P(pool),
        P(pool, None),
        P(tp, None),
    )
    out_specs = P(pool + tp, None)
    return jax.shard_map(local, mesh=fine, in_specs=in_specs, out_specs=out_specs, check_vma=False)
```

time: 360 us -> 396 us (1.10)
  Pallas kernels: 0 us -> 225 us
  waiting for transfers between devices: 192 us -> 78.1 us
  matrix products: 49.2 us -> 5.03 us
  local copies, waits for them, and re-layouts: 40.6 us -> 17.7 us
  starting transfers between devices: 40.3 us -> 62.6 us
  other arithmetic: 20.7 us -> 4.09 us
  between operations: 13.7 us -> 0.24 us
    pallas_call x0 -> x6, Pallas kernels: none -> 225 us  [the longest x1 129 us: place(): pl.pallas_call(place_kernel, out_shape=jax.ShapeDtypeStruct((slots,) + pa...]
    reduce_scatter x1 -> x0, waiting for transfers between devices: 116 us -> none  [local(): lax.psum_scatter(jnp.dot(attention, out_weight, preferred_element_type=jn...]
    ppermute x0 -> x6, waiting for transfers between devices: none -> 61.2 us  [swap(): return lax.ppermute(value, axis, [(i, i ^ bit) for i in range(size)])]
    all_to_all x5 -> x4, waiting for transfers between devices: 76 us -> 16.9 us  [the longest x1 16.9 us: local(): kv = lax.all_to_all(placed, PLANE, 0, 0, tiled=True)]
    dot_general x22 -> x2, matrix products: 49.2 us -> 5.03 us  [the longest x1 3.64 us: suffix_attend(): jnp.einsum('sgt,std->sgd', exp_terms.astype(BF16), suffix_cache[:, :, 1],...]
    ppermute x0 -> x6, starting transfers between devices: none -> 31.4 us  [swap(): return lax.ppermute(value, axis, [(i, i ^ bit) for i in range(size)])]
    all_to_all x5 -> x0, local copies, waits for them, and re-layouts: 16.1 us -> none  [the longest x2 14.8 us: local(): lax.all_to_all(outgoing, 'pool', split_axis=0, concat_axis=0, tiled=True)]
    reduce_sum x12 -> x2, other arithmetic: 14.6 us -> 2.3 us  [the longest x1 2.21 us: suffix_attend(): totals = jnp.sum(exp_terms, axis=-1)]
  transfers between devices with their start and end apart: 6 -> 10, of which waited for: 6 -> 6; matrix products, arithmetic and copies ran while one was open for 7% -> 5% of each run, Pallas kernels for 0% -> 55%
where the time goes in v1:
time: 396 us; the launch traced here: 393 us
  Pallas kernels  225 us (57%)
  waiting for transfers between devices  78.1 us (20%)
  starting transfers between devices  62.6 us (16%)
  local copies, waits for them, and re-layouts  17.7 us (4%)
  matrix products  5.03 us (1%)
  other arithmetic  4.09 us (1%)
    pallas_call x1, Pallas kernels, place(): pl.pallas_call(place_kernel, out_shape=jax.ShapeDtypeStruct((slots,) + pa...  129 us
    pallas_call x2, Pallas kernels, attend(): pl.pallas_call(functools.partial(attend_kernel, width), grid=(2, peers //...  85.3 us
    ppermute x6, waiting for transfers between devices, swap(): return lax.ppermute(value, axis, [(i, i ^ bit) for i in range(size)])  61.2 us
    ppermute x6, starting transfers between devices, swap(): return lax.ppermute(value, axis, [(i, i ^ bit) for i in range(size)])  31.4 us
    all_to_all x1, waiting for transfers between devices, local(): kv = lax.all_to_all(placed, PLANE, 0, 0, tiled=True)  16.9 us
    all_to_all x1, starting transfers between devices, local(): far_back = lax.all_to_all(far_out, PLANE, 0, 0, tiled=True)  10.2 us
    unnamed x30, local copies, waits for them, and re-layouts  7.93 us
  transfers between devices with their start and end apart: 10, of which 6 were waited for; matrix products, arithmetic and copies ran while one was open for 5% of the time, Pallas kernels for 55%

profile of v1, /device:TPU:1, one launch (start us, length us, event | category | flops | bytes accessed | tf_op | source)
XLA Modules:
  0.0 392.6 jit_solution(7413824653529253808)
XLA Ops:
  0.0 0.8 copy.24.col_ref
  0.8 0.0 copy-start.1
  0.8 1.0 copy-done.1
  1.9 0.7 copy-done.4
  2.6 1.5 dispatch.1
  4.1 7.6 %all-to-all-start = ((bf16[16,32,1024]{2,1,0:T(8,128)(2,1)}), bf16[16,32,1024]{2,1,0:T(8,128)(2,1)S(1)}, u32[]{:S(2)}, u32[]{:S(2)}) async-start(bf16[16,32,1024]{2,1,0:T(8,128)(2,1)} %bitcast.7), calls=%async_computation | async-start | bytes 2097152 | tf_op jit(solution)/shard_map/all_to_all | solution.py:293
  11.7 0.1 slice.33
  11.8 0.5 copy.19
  12.3 1.7 pad.4.pages_ref
  14.0 0.1 select_reduce_fusion
  14.1 0.5 broadcast_add_fusion.pick_ref
  14.6 129.1 %place.1 = bf16[32,512,128]{2,1,0:T(8,128)(2,1)} custom-call(s32[32]{0:T(128)} %broadcast_add_fusion.pick_ref, bf16[17,512,128]{2,1,0:T(8,128)(2,1)} %pad.4.pages_ref), custom_call_target="tpu_custom_call" | custom-call | bytes 8388608 | tf_op jit(solution)/shard_map/place/pallas_call | solution.py:76
  143.7 0.0 copy-start.5
  143.7 6.7 %all-to-all-start.1 = ((bf16[16,1024,128]{2,1,0:T(8,128)(2,1)}), bf16[16,1024,128]{2,1,0:T(8,128)(2,1)}, u32[]{:S(2)}, u32[]{:S(2)}) async-start(bf16[16,1024,128]{2,1,0:T(8,128)(2,1)} %bitcast.37), calls=%async_computation.1 | async-start | bytes 8388608 | tf_op jit(solution)/shard_map/all_to_all | solution.py:304
  150.5 7.0 %collective-permute-start = (bf16[16,32,1024]{2,1,0:T(8,128)(2,1)S(1)}, bf16[16,32,1024]{2,1,0:T(8,128)(2,1)S(1)}, u32[]{:S(2)}, u32[]{:S(2)}) collective-permute-start(bf16[16,32,1024]{2,1,0:T(8,128)(2,1)S(1)} %all-to-all-done.q_ref), channel_id=1, source_target_pairs={{0,32},{32,0},{1,33},{33,1},{2,34},{34,2},{3,35},{35,3},{4,36},{36... | collective-permute-start | bytes 3145736 | tf_op jit(solution)/shard_map/ppermute | solution.py:280
  157.5 0.1 collective-permute-start.1
  157.6 27.8 %collective-permute-done.q_ref = bf16[16,32,1024]{2,1,0:T(8,128)(2,1)S(1)} collective-permute-done((bf16[16,32,1024]{2,1,0:T(8,128)(2,1)S(1)}, bf16[16,32,1024]{2,1,0:T(8,128)(2,1)S(1)}, u32[]{:S(2)}, u32[]{:S(2)}) %collective-permute-start) | collective-permute-done | bytes 1048608 | tf_op jit(solution)/shard_map/ppermute | solution.py:280
  185.4 16.9 %all-to-all-done.1.kv_ref = bf16[16,1024,128]{2,1,0:T(8,128)(2,1)} async-done(((bf16[16,1024,128]{2,1,0:T(8,128)(2,1)}), bf16[16,1024,128]{2,1,0:T(8,128)(2,1)}, u32[]{:S(2)}, u32[]{:S(2)}) %all-to-all-start.1) | async-done | bytes 4194336 | tf_op jit(solution)/shard_map/all_to_all | solution.py:304
  202.3 42.8 %attend_far.1 = bf16[16,32,1152]{2,1,0:T(8,128)(2,1)} custom-call(bf16[16,32,1024]{2,1,0:T(8,128)(2,1)S(1)} %collective-permute-done.q_ref, bf16[16,1024,128]{2,1,0:T(8,128)(2,1)} %all-to-all-done.1.kv_ref), custom_call_target="tpu_custom_call" | custom-call | flops 4294967296 | bytes 6291456 | tf_op jit(solution)/shard_map/attend_far/pallas_call | solution.py:155
  245.1 10.2 %all-to-all-start.2 = ((bf16[16,32,1152]{2,1,0:T(8,128)(2,1)}), bf16[16,32,1152]{2,1,0:T(8,128)(2,1)S(1)}, u32[]{:S(2)}, u32[]{:S(2)}) async-start(bf16[16,32,1152]{2,1,0:T(8,128)(2,1)} %attend_far.1), calls=%async_computation.2 | async-start | bytes 2359296 | tf_op jit(solution)/shard_map/all_to_all | solution.py:310
  255.3 0.0 copy-start.2
  255.3 6.6 %fusion.9 = (bf16[256,16,1,128]{3,2,1,0:T(2,128)(2,1)S(1)}, bf16[256,16,1,128]{3,2,1,0:T(2,128)(2,1)}) fusion(bf16[256,16,2,128]{3,2,1,0:T(2,128)(2,1)} %param.10), kind=kLoop, calls=%fused_computation.30 | loop fusion | bytes 4194304 | tf_op jit(solution)/shard_map/slice | solution.py:263
  262.0 0.1 copy.27
  262.1 0.1 iota_compare_fusion
  262.2 1.4 fusion.10
  263.6 42.5 %attend_own.1 = bf16[16,32,1152]{2,1,0:T(8,128)(2,1)S(1)} custom-call(bf16[16,32,1024]{2,1,0:T(8,128)(2,1)S(1)} %all-to-all-done.q_ref, bf16[16,1024,128]{2,1,0:T(8,128)(2,1)} %all-to-all-done.1.kv_ref), custom_call_target="tpu_custom_call" | custom-call | flops 4294967296 | bytes 6291456 | tf_op jit(solution)/shard_map/attend_own/pallas_call | solution.py:155
  306.1 1.0 copy-done.3
  307.1 6.7 %all-to-all-start.3 = ((bf16[16,32,1152]{2,1,0:T(8,128)(2,1)}), bf16[16,32,1152]{2,1,0:T(8,128)(2,1)S(1)}, u32[]{:S(2)}, u32[]{:S(2)}) async-start(bf16[16,32,1152]{2,1,0:T(8,128)(2,1)} %copy-done.3), calls=%async_computation.3 | async-start | bytes 2359296 | tf_op jit(solution)/shard_map/all_to_all | solution.py:313
  313.8 2.2 fusion.1
  316.0 0.1 copy.21.col_ref
  316.2 1.7 collect.1
  317.8 6.5 %collective-permute-start.2 = (bf16[128,2304]{1,0:T(8,128)(2,1)}, bf16[128,2304]{1,0:T(8,128)(2,1)}, u32[]{:S(2)}, u32[]{:S(2)}) collective-permute-start(bf16[128,2304]{1,0:T(8,128)(2,1)} %collect.1), channel_id=1, source_target_pairs={{0,32},{32,0},{1,33},{33,1},{2,34},{34,2},{3,35},{35,3},{4,36},{36... | collective-permute-start | bytes 1769480 | tf_op jit(solution)/shard_map/ppermute | solution.py:280
  324.4 3.6 convolution_divide_fusion
  328.0 0.3 broadcast_in_dim.49
  328.4 0.9 copy-done.9
  329.2 0.5 copy_bitcast_fusion
  329.7 7.3 %collective-permute-done.2.far_ref = bf16[128,2304]{1,0:T(8,128)(2,1)} collective-permute-done((bf16[128,2304]{1,0:T(8,128)(2,1)}, bf16[128,2304]{1,0:T(8,128)(2,1)}, u32[]{:S(2)}, u32[]{:S(2)}) %collective-permute-start.2) | collective-permute-done | bytes 589856 | tf_op jit(solution)/shard_map/ppermute | solution.py:280
  337.0 3.4 copy-done
  340.4 7.2 %merge_project.1 = (bf16[128,4096]{1,0:T(8,128)(2,1)S(1)}, bf16[128,4096]{1,0:T(8,128)(2,1)S(1)}) custom-call(s32[1]{0:T(128)} %bitcast.me_ref, s32[256,1]{1,0:T(8,128)S(1)} %copy.24.col_ref, s32[1,256]{1,0:T(1,128)S(1)} %bitcast.35, bf16[512,1152]{1,0:T(8,128)(2,1)S(1)} %bitcast.30, bf16[128,2304]{1,0:T(8,128)(2,1)} %collective-permute-done.2.far_ref, ...), custom_call_target="tpu_custom_call" | custom-call | flops 2147483648 | bytes 16777216 | tf_op jit(solution)/shard_map/merge_project/pallas_call | solution.py:241
  347.6 13.7 %collective-permute-start.3 = (bf16[128,4096]{1,0:T(8,128)(2,1)S(1)}, bf16[128,4096]{1,0:T(8,128)(2,1)S(1)}, u32[]{:S(2)}, u32[]{:S(2)}) collective-permute-start(bf16[128,4096]{1,0:T(8,128)(2,1)S(1)} %get-tuple-element.16), channel_id=1, source_target_pairs={{0,1},{1,0},{2,3},{3,2},{4,5},{5,4},{6,7},{7,6},{8,9},{9,8},{10,11... | collective-permute-start | bytes 3145736 | tf_op jit(solution)/shard_map/ppermute | solution.py:280
  361.3 2.3 collective-permute-done.3
  363.6 0.3 add_convert_fusion.1
  363.8 2.0 collective-permute-start.4
  365.8 12.0 %collective-permute-done.4 = bf16[64,4096]{1,0:T(8,128)(2,1)S(1)} collective-permute-done((bf16[64,4096]{1,0:T(8,128)(2,1)S(1)}, bf16[64,4096]{1,0:T(8,128)(2,1)S(1)}, u32[]{:S(2)}, u32[]{:S(2)}) %collective-permute-start.4) | collective-permute-done | bytes 524320 | tf_op jit(solution)/shard_map/ppermute | solution.py:280
  377.8 0.1 add_convert_fusion.3
  377.9 2.2 collective-permute-start.5
  380.1 11.8 %collective-permute-done.5 = bf16[32,4096]{1,0:T(8,128)(2,1)S(1)} collective-permute-done((bf16[32,4096]{1,0:T(8,128)(2,1)S(1)}, bf16[32,4096]{1,0:T(8,128)(2,1)S(1)}, u32[]{:S(2)}, u32[]{:S(2)}) %collective-permute-start.5) | collective-permute-done | bytes 262176 | tf_op jit(solution)/shard_map/ppermute | solution.py:280
  391.8 0.8 add_convert_fusion.2
  (27 shorter events, 0.1 us)
Async XLA Ops:
  0.0 11.7 %copy-start.13 = (s32[1,32]{1,0:T(1,128)S(1)}, s32[1,32]{1,0:T(1,128)}, u32[]{:S(2)}) copy-start(s32[1,32]{1,0:T(1,128)} %param.8) | copy-start | bytes 388
  0.8 1.0 copy-start.1
  1.9 0.7 copy-start.4
  2.6 9.2 %copy-start.7 = (bf16[32,128,2,128]{3,2,1,0:T(2,128)(2,1)S(1)}, bf16[32,128,2,128]{3,2,1,0:T(2,128)(2,1)}, u32[]{:S(2)}) copy-start(bf16[32,128,2,128]{3,2,1,0:T(2,128)(2,1)} %param.7) | copy-start | bytes 6291460
  4.1 139.6 %all-to-all-start = ((bf16[16,32,1024]{2,1,0:T(8,128)(2,1)}), bf16[16,32,1024]{2,1,0:T(8,128)(2,1)S(1)}, u32[]{:S(2)}, u32[]{:S(2)}) async-start(bf16[16,32,1024]{2,1,0:T(8,128)(2,1)} %bitcast.7), calls=%async_computation | async-start | bytes 2097152 | tf_op jit(solution)/shard_map/all_to_all | solution.py:293
  143.7 13.7 %copy-start.5 = (s32[256,1]{0,1:T(1,128)S(1)}, s32[256,1]{0,1:T(1,128)}, u32[]{:S(2)}) copy-start(s32[256,1]{0,1:T(1,128)} %param.12) | copy-start | bytes 3076
  143.7 58.6 %all-to-all-start.1 = ((bf16[16,1024,128]{2,1,0:T(8,128)(2,1)}), bf16[16,1024,128]{2,1,0:T(8,128)(2,1)}, u32[]{:S(2)}, u32[]{:S(2)}) async-start(bf16[16,1024,128]{2,1,0:T(8,128)(2,1)} %bitcast.37), calls=%async_computation.1 | async-start | bytes 8388608 | tf_op jit(solution)/shard_map/all_to_all | solution.py:304
  150.5 34.9 %collective-permute-start = (bf16[16,32,1024]{2,1,0:T(8,128)(2,1)S(1)}, bf16[16,32,1024]{2,1,0:T(8,128)(2,1)S(1)}, u32[]{:S(2)}, u32[]{:S(2)}) collective-permute-start(bf16[16,32,1024]{2,1,0:T(8,128)(2,1)S(1)} %all-to-all-done.q_ref), channel_id=1, source_target_pairs={{0,32},{32,0},{1,33},{33,1},{2,34},{34,2},{3,35},{35,3},{4,36},{36... | collective-permute-start | bytes 3145736 | tf_op jit(solution)/shard_map/ppermute | solution.py:280
  157.5 158.6 %collective-permute-start.1 = (s32[1,256]{1,0:T(1,128)S(1)}, s32[1,256]{1,0:T(1,128)S(1)}, u32[]{:S(2)}, u32[]{:S(2)}) collective-permute-start(s32[1,256]{1,0:T(1,128)S(1)} %bitcast.34), channel_id=1, source_target_pairs={{0,32},{32,0},{1,33},{33,1},{2,34},{34,2},{3,35},{35,3},{4,36},{36... | collective-permute-start | bytes 3080 | tf_op jit(solution)/shard_map/ppermute | solution.py:280
  245.1 62.0 %all-to-all-start.2 = ((bf16[16,32,1152]{2,1,0:T(8,128)(2,1)}), bf16[16,32,1152]{2,1,0:T(8,128)(2,1)S(1)}, u32[]{:S(2)}, u32[]{:S(2)}) async-start(bf16[16,32,1152]{2,1,0:T(8,128)(2,1)} %attend_far.1), calls=%async_computation.2 | async-start | bytes 2359296 | tf_op jit(solution)/shard_map/all_to_all | solution.py:310
  255.3 6.6 %copy-start.2 = (bf16[256,1024]{1,0:T(8,128)(2,1)S(1)}, bf16[256,1024]{1,0:T(8,128)(2,1)}, u32[]{:S(2)}) copy-start(bf16[256,1024]{1,0:T(8,128)(2,1)} %q_ref.1) | copy-start | bytes 1572868
  255.3 6.7 %copy-start.12 = (s32[256]{0:T(256)S(1)}, s32[256]{0:T(256)}, u32[]{:S(2)}) copy-start(s32[256]{0:T(256)} %param.11) | copy-start | bytes 3076
  262.2 43.9 %copy-start.11 = (pred[256,16]{1,0:T(8,128)(4,1)}, pred[256,16]{1,0:T(8,128)(4,1)S(1)}, u32[]{:S(2)}) copy-start(pred[256,16]{1,0:T(8,128)(4,1)S(1)} %iota_compare_fusion) | copy-start | bytes 12292
  263.6 50.2 %copy-start.6 = (f32[256,8,16]{2,1,0:T(8,128)}, f32[256,8,16]{2,1,0:T(8,128)S(1)}, u32[]{:S(2)}) copy-start(f32[256,8,16]{2,1,0:T(8,128)S(1)} %get-tuple-element.22) | copy-start | bytes 393220
  306.1 1.0 copy-start.3
  307.1 29.9 %all-to-all-start.3 = ((bf16[16,32,1152]{2,1,0:T(8,128)(2,1)}), bf16[16,32,1152]{2,1,0:T(8,128)(2,1)S(1)}, u32[]{:S(2)}, u32[]{:S(2)}) async-start(bf16[16,32,1152]{2,1,0:T(8,128)(2,1)} %copy-done.3), calls=%async_computation.3 | async-start | bytes 2359296 | tf_op jit(solution)/shard_map/all_to_all | solution.py:313
  317.8 19.2 %collective-permute-start.2 = (bf16[128,2304]{1,0:T(8,128)(2,1)}, bf16[128,2304]{1,0:T(8,128)(2,1)}, u32[]{:S(2)}, u32[]{:S(2)}) collective-permute-start(bf16[128,2304]{1,0:T(8,128)(2,1)} %collect.1), channel_id=1, source_target_pairs={{0,32},{32,0},{1,33},{33,1},{2,34},{34,2},{3,35},{35,3},{4,36},{36... | collective-permute-start | bytes 1769480 | tf_op jit(solution)/shard_map/ppermute | solution.py:280
  324.4 3.6 copy-start.8
  324.4 3.6 copy-start.10
  328.0 1.2 copy-start.9
  337.0 3.4 copy-start
  347.6 15.9 %collective-permute-start.3 = (bf16[128,4096]{1,0:T(8,128)(2,1)S(1)}, bf16[128,4096]{1,0:T(8,128)(2,1)S(1)}, u32[]{:S(2)}, u32[]{:S(2)}) collective-permute-start(bf16[128,4096]{1,0:T(8,128)(2,1)S(1)} %get-tuple-element.16), channel_id=1, source_target_pairs={{0,1},{1,0},{2,3},{3,2},{4,5},{5,4},{6,7},{7,6},{8,9},{9,8},{10,11... | collective-permute-start | bytes 3145736 | tf_op jit(solution)/shard_map/ppermute | solution.py:280
  363.8 14.0 %collective-permute-start.4 = (bf16[64,4096]{1,0:T(8,128)(2,1)S(1)}, bf16[64,4096]{1,0:T(8,128)(2,1)S(1)}, u32[]{:S(2)}, u32[]{:S(2)}) collective-permute-start(bf16[64,4096]{1,0:T(8,128)(2,1)S(1)} %get-tuple-element.18), channel_id=1, source_target_pairs={{0,2},{2,0},{4,6},{6,4},{1,3},{3,1},{5,7},{7,5},{8,10},{10,8},{12,... | collective-permute-start | bytes 1572872 | tf_op jit(solution)/shard_map/ppermute | solution.py:280
  377.9 13.9 %collective-permute-start.5 = (bf16[32,4096]{1,0:T(8,128)(2,1)S(1)}, bf16[32,4096]{1,0:T(8,128)(2,1)S(1)}, u32[]{:S(2)}, u32[]{:S(2)}) collective-permute-start(bf16[32,4096]{1,0:T(8,128)(2,1)S(1)} %add_convert_fusion.3), channel_id=1, source_target_pairs={{0,4},{2,6},{4,0},{6,2},{1,5},{3,7},{5,1},{7,3},{8,12},{10,14},{12... | collective-permute-start | bytes 786440 | tf_op jit(solution)/shard_map/ppermute | solution.py:280

commit v2 on v1

--- a/solution.py
+++ b/solution.py
@@ -14,7 +14,6 @@
 PLANE = ("x", "y")
 SCALE = HD**-0.5
 LOG2E = 1.4426950408889634
-MARK = 16384.0
 LOW = -1e30
 F32 = jnp.float32
 BF16 = jnp.bfloat16
@@ -61,119 +60,144 @@
     )(ids_col, ids_row, queries)
 
 
-def place_kernel(pick_ref, pages_ref, out_ref, sem):
-    copies = [
-        pltpu.make_async_copy(pages_ref.at[pick_ref[s]], out_ref.at[s], sem.at[s])
-        for s in range(out_ref.shape[0])
-    ]
-    for copy in copies:
-        copy.start()
-    for copy in copies:
-        copy.wait()
+def place_kernel(pick_ref, pages_ref, out_ref):
+    def one(slot, carry):
+        out_ref[slot] = pages_ref[pick_ref[slot]]
+        return carry
+
+    lax.fori_loop(0, out_ref.shape[0], one, 0)
 
 
 def place(pick, pages, slots):
+    whole = pl.BlockSpec(memory_space=pltpu.VMEM)
     return pl.pallas_call(
         place_kernel,
         out_shape=jax.ShapeDtypeStruct((slots,) + pages.shape[1:], BF16),
-        in_specs=[
-            pl.BlockSpec(memory_space=pltpu.SMEM),
-            pl.BlockSpec(memory_space=pl.ANY),
-        ],
-        out_specs=pl.BlockSpec(memory_space=pl.ANY),
-        scratch_shapes=[pltpu.SemaphoreType.DMA((slots,))],
-        cost_estimate=pl.CostEstimate(flops=0, bytes_accessed=2**23, transcendentals=0),
+        in_specs=[pl.BlockSpec(memory_space=pltpu.SMEM), whole],
+        out_specs=whole,
+        compiler_params=pltpu.CompilerParams(vmem_limit_bytes=32 * 2**20),
+        cost_estimate=pl.CostEstimate(flops=0, bytes_accessed=6 * 2**20, transcendentals=0),
         name="place",
     )(pick, pages)
 
 
-def attend_kernel(width, q_ref, kv_ref, out_ref, list_ref, s_ref, acc_ref):
+def attend_kernel(width, list_ref, count_ref, q_ref, kv_ref, out_ref, key_ref, value_ref, s_ref, acc_ref):
     sub = pl.program_id(0)
-    peers, span = kv_ref.shape[0], kv_ref.shape[1] // 4
+    span = kv_ref.shape[1] // 4
     group, cap = q_ref.shape[0], q_ref.shape[1]
     key_at = pl.multiple_of(sub * 2 * span, 2 * span)
+    count = count_ref[sub]
+    even = ((count + 1) // 2) * 2
 
     @pl.when(pl.program_id(1) == 0)
     def _():
-        def scan(src, n):
-            tile = kv_ref[src, pl.ds(key_at, 16), :].astype(F32)
-            list_ref[n] = src
-            return n + (jnp.max(tile) < MARK / 2).astype(jnp.int32)
-
-        list_ref[peers] = lax.fori_loop(0, peers, scan, 0)
-
-    count = list_ref[peers]
+        def pack(n, carry):
+            src = list_ref[sub, n]
+            at = pl.multiple_of(n * span, span)
+            weight = jnp.where(n < count, 1.0, 0.0).astype(BF16)
+            key_ref[pl.ds(at, span), :] = kv_ref[src, pl.ds(key_at, span), :]
+            value_ref[pl.ds(at, span), :HD] = kv_ref[src, pl.ds(key_at + span, span), :] * weight
+            value_ref[pl.ds(at, span), HD:] = jnp.full((span, HD), 1.0, BF16) * weight
+            return carry
+
+        lax.fori_loop(0, even, pack, 0)
+
     heads = [(j, h) for j in range(group) for h in range(G)]
     q = jnp.concatenate([q_ref[j, :, h * HD : (h + 1) * HD] for j, h in heads], axis=0)
-
-    def score(i, top):
-        key = kv_ref[list_ref[i], pl.ds(key_at, span), :]
+    fours = even // 4
+
+    def score(at, size, top):
+        key = key_ref[pl.ds(at, size), :]
         s = lax.dot_general(q, key, (((1,), (1,)), ((), ())), preferred_element_type=F32)
-        s_ref[i] = s
-        for c in range(0, span, HD):
+        s_ref[:, pl.ds(at, size)] = s
+        for c in range(0, size, HD):
             top = jnp.maximum(top, s[:, c : c + HD])
         return top
 
-    top = lax.fori_loop(0, count, score, jnp.full(q.shape, LOW, F32))
+    def four(i):
+        return pl.multiple_of(i * 4 * span, 4 * span)
+
+    def two(i):
+        return pl.multiple_of(i * 2 * span, 2 * span)
+
+    top = lax.fori_loop(
+        0, fours, lambda i, t: score(four(i), 4 * span, t), jnp.full(q.shape, LOW, F32)
+    )
+    top = lax.fori_loop(2 * fours, even // 2, lambda i, t: score(two(i), 2 * span, t), top)
     top = jnp.max(top, axis=1, keepdims=True)
     acc_ref[...] = jnp.zeros_like(acc_ref)
-    ones = jnp.ones((span, HD), BF16)
-
-    def gather(i, carry):
-        value = kv_ref[list_ref[i], pl.ds(key_at + span, span), :]
-        p = jnp.exp2((s_ref[i] - top) * (SCALE * LOG2E)).astype(BF16)
-        acc_ref[...] += jnp.dot(
-            p, jnp.concatenate([value, ones], axis=1), preferred_element_type=F32
-        )
+
+    def weigh(at, size, carry):
+        p = jnp.exp2((s_ref[:, pl.ds(at, size)] - top) * (SCALE * LOG2E)).astype(BF16)
+        acc_ref[...] += jnp.dot(p, value_ref[pl.ds(at, size), :], preferred_element_type=F32)
         return carry
 
-    lax.fori_loop(0, count, gather, 0)
+    lax.fori_loop(0, fours, lambda i, c: weigh(four(i), 4 * span, c), 0)
+    lax.fori_loop(2 * fours, even // 2, lambda i, c: weigh(two(i), 2 * span, c), 0)
     total = acc_ref[:, HD:]
-    some = total > 0.0
-    total = jnp.where(some, total, 1.0)
+    total = jnp.where(total > 0.0, total, 1.0)
     out = (acc_ref[:, :HD] / total).astype(BF16)
-    lse = jnp.where(some, top * SCALE + jnp.log(total), LOW)
     lane = lax.broadcasted_iota(jnp.int32, (cap, HD), 1)
     for j in range(group):
-        packed = jnp.zeros((cap, HD), F32)
+        packed_total = jnp.ones((cap, HD), F32)
+        packed_top = jnp.zeros((cap, HD), F32)
         for h in range(G):
             at = (j * G + h) * cap
             out_ref[j, :, h * HD : (h + 1) * HD] = out[at : at + cap]
-            packed = jnp.where((lane & 7) == h, lse[at : at + cap], packed)
-        first = packed.astype(BF16).astype(F32)
-        second = (packed - first).astype(BF16).astype(F32)
-        third = packed - first - second
+            packed_total = jnp.where((lane & 7) == h, total[at : at + cap], packed_total)
+            packed_top = jnp.where((lane & 7) == h, top[at : at + cap], packed_top)
+        lse = jnp.where(count > 0, packed_top * SCALE + jnp.log(packed_total), LOW)
+        first = lse.astype(BF16).astype(F32)
+        second = (lse - first).astype(BF16).astype(F32)
+        third = lse - first - second
         part = jnp.where(lane < 8, first, jnp.where(lane < 16, second, third))
         out_ref[j, :, width:] = jnp.where(lane < 24, part, 0.0).astype(BF16)
 
 
-def attend(q, kv, name):
+def attend(listed, count, q, kv, name):
     peers, rows, width = q.shape
-    group = 4
+    group = 8
     span = kv.shape[1] // 4
     m = group * CAP * G
+    smem = pl.BlockSpec(memory_space=pltpu.SMEM)
     return pl.pallas_call(
         functools.partial(attend_kernel, width),
         grid=(2, peers // group),
         out_shape=jax.ShapeDtypeStruct((peers, rows, width + HD), BF16),
         in_specs=[
+            smem,
+            smem,
             pl.BlockSpec((group, CAP, width), lambda s, i: (i, s, 0)),
             pl.BlockSpec(memory_space=pltpu.VMEM),
         ],
         out_specs=pl.BlockSpec((group, CAP, width + HD), lambda s, i: (i, s, 0)),
         scratch_shapes=[
-            pltpu.SMEM((peers + 1,), jnp.int32),
-            pltpu.VMEM((peers, m, span), F32),
+            pltpu.VMEM((peers * span, HD), BF16),
+            pltpu.VMEM((peers * span, 2 * HD), BF16),
+            pltpu.VMEM((m, peers * span), F32),
             pltpu.VMEM((m, 2 * HD), F32),
         ],
-        compiler_params=pltpu.CompilerParams(vmem_limit_bytes=40 * 2**20),
+        compiler_params=pltpu.CompilerParams(vmem_limit_bytes=48 * 2**20),
         cost_estimate=pl.CostEstimate(
             flops=4 * peers * rows * G * 8 * span * HD,
             bytes_accessed=6 * 2**20,
             transcendentals=peers * rows * G * 8 * span,
         ),
         name=name,
-    )(q, kv)
+    )(listed, count, q, kv)
+
+
+def pages_here(owner):
+    plane = owner.shape[0]
+    mine = lax.axis_index("x") * 8 + lax.axis_index("y") + 4 * jnp.arange(2, dtype=jnp.int32)
+    there = jnp.max((owner[None] == mine[:, None, None]).astype(jnp.int32), axis=2)
+    peer = jnp.arange(plane, dtype=jnp.int32)
+    rank = jnp.sum(there[:, None, :] * (peer[None, :] < peer[:, None]).astype(jnp.int32)[None], axis=2)
+    hit = (there[:, None, :] == 1) & (rank[:, None, :] == peer[None, :, None])
+    listed = jnp.sum(jnp.where(hit, peer[None, None, :], 0), axis=2)
+    count = jnp.sum(there, axis=1)
+    listed = jnp.where(peer[None, :] < count[:, None], listed, listed[:, :1])
+    return listed.astype(jnp.int32), count.astype(jnp.int32)
 
 
 def collect_kernel(col_ref, row_ref, replies_ref, out_ref):
@@ -293,22 +317,24 @@
     own_q = lax.all_to_all(sent, PLANE, 0, 0, tiled=True)
 
     owner = page_owner[0, ::2]
+    listed, count = pages_here(lax.all_gather(owner, PLANE))
     slot = slot_base(owner) // CAP
     here = jnp.arange(2 * plane, dtype=jnp.int32)[:, None] == slot[None, :]
-    pick = pairs + jnp.sum(jnp.where(here, jnp.arange(pairs, dtype=jnp.int32)[None, :] - pairs, 0), axis=1)
+    pick = jnp.sum(jnp.where(here, jnp.arange(pairs, dtype=jnp.int32)[None, :], 0), axis=1)
     paired = jnp.swapaxes(prefill_pages.reshape(pairs, 2 * page, 2, HD), 1, 2)
     paired = paired.reshape(pairs, 4 * page, HD)
-    paired = jnp.pad(paired, ((0, 1), (0, 0), (0, 0)), constant_values=MARK)
     placed = place(pick, paired, 2 * plane).reshape(plane, 8 * page, HD)
     placed, own_q = lax.optimization_barrier((placed, own_q))
     kv = lax.all_to_all(placed, PLANE, 0, 0, tiled=True)
     far_q = swap(own_q, "zh", 1)
 
     suf, suf_lse = suffix_attend(queries, suffix_cache, suffix_len)
-
-    far_out = attend(far_q, kv, "attend_far")
+    far_q, suf, suf_lse, listed, count = lax.optimization_barrier((far_q, suf, suf_lse, listed, count))
+
+    far_out = attend(listed, count, far_q, kv, "attend_far")
+    far_out, own_q = lax.optimization_barrier((far_out, own_q))
     far_back = lax.all_to_all(far_out, PLANE, 0, 0, tiled=True)
-    own_out = attend(own_q, kv, "attend_own")
+    own_out = attend(listed, count, own_q, kv, "attend_own")
     far_back, own_out = lax.optimization_barrier((far_back, own_out))
     own_back = lax.all_to_all(own_out, PLANE, 0, 0, tiled=True)
     far_part = collect(far_col, far_row, far_back.reshape(plane * 2 * CAP, width + HD))

time: 396 us -> 291 us (0.73); the launches traced: 393 us -> 293 us
  Pallas kernels: 225 us -> 47.5 us
  blocking collectives: 0 us -> 61.3 us
  starting transfers between devices: 62.6 us -> 86.9 us
  waiting for transfers between devices: 78.1 us -> 69.1 us
  local copies, waits for them, and re-layouts: 17.7 us -> 23.1 us
    pallas_call x1, Pallas kernels: 129 us -> 0.97 us  [place(): pl.pallas_call(place_kernel, out_shape=jax.ShapeDtypeStruct((slots,) + pa...]
    all_gather x0 -> x1, blocking collectives: none -> 61.3 us  [local(): listed, count = pages_here(lax.all_gather(owner, PLANE))]
    pallas_call x2, Pallas kernels: 85.3 us -> 37.2 us  [attend(): pl.pallas_call(functools.partial(attend_kernel, width), grid=(2, peers //...]
    ppermute x6, starting transfers between devices: 31.4 us -> 55.9 us  [swap(): return lax.ppermute(value, axis, [(i, i ^ bit) for i in range(size)])]
    all_to_all x1, waiting for transfers between devices: 16.9 us -> 0.01 us  [local(): kv = lax.all_to_all(placed, PLANE, 0, 0, tiled=True)]
    all_to_all x1, waiting for transfers between devices: 0.01 us -> 10.2 us  [local(): own_q = lax.all_to_all(sent, PLANE, 0, 0, tiled=True)]
    unnamed x30 -> x28, local copies, waits for them, and re-layouts: 7.93 us -> 12.4 us
  transfers between devices with their start and end apart: 10 -> 10, of which waited for: 6 -> 7; matrix products, arithmetic and copies ran while one was open for 5% -> 5% of each run, Pallas kernels for 55% -> 7%
where the time goes in v2:
time: 291 us; the launch traced here: 293 us
  starting transfers between devices  86.9 us (30%)
  waiting for transfers between devices  69.1 us (24%)
  blocking collectives  61.3 us (21%)
  Pallas kernels  47.5 us (16%)
  local copies, waits for them, and re-layouts  23.1 us (8%)
    all_gather x1, blocking collectives, local(): listed, count = pages_here(lax.all_gather(owner, PLANE))  61.3 us
    ppermute x6, waiting for transfers between devices, swap(): return lax.ppermute(value, axis, [(i, i ^ bit) for i in range(size)])  58.8 us
    ppermute x6, starting transfers between devices, swap(): return lax.ppermute(value, axis, [(i, i ^ bit) for i in range(size)])  55.9 us
    pallas_call x2, Pallas kernels, attend(): pl.pallas_call(functools.partial(attend_kernel, width), grid=(2, peers //...  37.2 us
    unnamed x28, local copies, waits for them, and re-layouts  12.4 us
    all_to_all x1, starting transfers between devices, local(): own_back = lax.all_to_all(own_out, PLANE, 0, 0, tiled=True)  10.5 us
    all_to_all x1, waiting for transfers between devices, local(): own_q = lax.all_to_all(sent, PLANE, 0, 0, tiled=True)  10.2 us
    all_to_all x1, starting transfers between devices, local(): far_back = lax.all_to_all(far_out, PLANE, 0, 0, tiled=True)  8.19 us
  transfers between devices with their start and end apart: 10, of which 7 were waited for; matrix products, arithmetic and copies ran while one was open for 5% of the time, Pallas kernels for 7%

profile of v2, /device:TPU:1, one launch (start us, length us, event | category | flops | bytes accessed | tf_op | source)
XLA Modules:
  0.0 292.6 jit_solution(3635039815208386198)
XLA Ops:
  0.0 0.8 copy.30.col_ref
  0.8 1.0 copy-done.3
  1.9 0.7 copy-done.9
  2.6 1.5 dispatch.1
  4.0 7.6 %all-to-all-start = ((bf16[16,32,1024]{2,1,0:T(8,128)(2,1)}), bf16[16,32,1024]{2,1,0:T(8,128)(2,1)S(1)}, u32[]{:S(2)}, u32[]{:S(2)}) async-start(bf16[16,32,1024]{2,1,0:T(8,128)(2,1)} %bitcast.7), calls=%async_computation | async-start | bytes 2097152 | tf_op jit(solution)/shard_map/all_to_all | solution.py:317
  11.6 0.1 slice.36
  11.8 2.1 copy.25
  14.0 1.0 place.1
  14.9 2.0 copy-done
  16.9 10.2 %all-to-all-done.q_ref = bf16[16,32,1024]{2,1,0:T(8,128)(2,1)S(1)} async-done(((bf16[16,32,1024]{2,1,0:T(8,128)(2,1)}), bf16[16,32,1024]{2,1,0:T(8,128)(2,1)S(1)}, u32[]{:S(2)}, u32[]{:S(2)}) %all-to-all-start) | async-done | bytes 1048608 | tf_op jit(solution)/shard_map/all_to_all | solution.py:317
  27.2 4.7 %all-to-all-start.1 = ((bf16[16,1024,128]{2,1,0:T(8,128)(2,1)}), bf16[16,1024,128]{2,1,0:T(8,128)(2,1)}, u32[]{:S(2)}, u32[]{:S(2)}) async-start(bf16[16,1024,128]{2,1,0:T(8,128)(2,1)} %bitcast.32), calls=%async_computation.1 | async-start | bytes 8388608 | tf_op jit(solution)/shard_map/all_to_all | solution.py:328
  32.0 61.3 %all-gather = s32[16,1,16]{2,1,0:T(1,128)S(1)} all-gather(s32[1,1,16]{2,1,0:T(1,128)S(1)} %bitcast.46), channel_id=1, replica_groups=mesh['x'=4,'zh'=2,'y'=4,'zl'=4,'core'=2] {'x','y'}, dimensions={0}, use_global_device_ids=true | all-gather | bytes 1088 | tf_op jit(solution)/shard_map/all_gather | solution.py:320
  93.2 0.2 convert_reduce_fusion
  93.4 0.1 reduce_sum.47.count_ref
  93.5 0.1 multiply_reduce_fusion
  93.7 0.1 select_reduce_fusion
  93.8 0.1 slice_reduce_fusion
  94.0 0.1 iota_compare_fusion
  94.1 5.7 %fusion.11 = (bf16[256,16,1,128]{3,2,1,0:T(2,128)(2,1)S(1)}, bf16[256,16,1,128]{3,2,1,0:T(2,128)(2,1)S(1)}) fusion(bf16[256,16,2,128]{3,2,1,0:T(2,128)(2,1)} %param.10), kind=kLoop, calls=%fused_computation.39 | loop fusion | bytes 4194304 | tf_op jit(solution)/shard_map/slice | solution.py:287
  99.8 0.7 fusion.12
  100.6 7.0 %collective-permute-start = (bf16[16,32,1024]{2,1,0:T(8,128)(2,1)S(1)}, bf16[16,32,1024]{2,1,0:T(8,128)(2,1)S(1)}, u32[]{:S(2)}, u32[]{:S(2)}) collective-permute-start(bf16[16,32,1024]{2,1,0:T(8,128)(2,1)S(1)} %all-to-all-done.q_ref), channel_id=1, source_target_pairs={{0,32},{32,0},{1,33},{33,1},{2,34},{34,2},{3,35},{35,3},{4,36},{36... | collective-permute-start | bytes 3145736 | tf_op jit(solution)/shard_map/ppermute | solution.py:304
  107.6 0.7 fusion.1
  108.3 1.2 convolution_divide_fusion
  109.6 0.3 broadcast_in_dim.83
  109.9 1.5 copy_bitcast_fusion
  111.4 20.3 %collective-permute-done.q_ref = bf16[16,32,1024]{2,1,0:T(8,128)(2,1)S(1)} collective-permute-done((bf16[16,32,1024]{2,1,0:T(8,128)(2,1)S(1)}, bf16[16,32,1024]{2,1,0:T(8,128)(2,1)S(1)}, u32[]{:S(2)}, u32[]{:S(2)}) %collective-permute-start) | collective-permute-done | bytes 1048608 | tf_op jit(solution)/shard_map/ppermute | solution.py:304
  131.7 18.9 %attend_far.1 = bf16[16,32,1152]{2,1,0:T(8,128)(2,1)} custom-call(s32[2,16]{1,0:T(2,128)S(1)} %compare_select_fusion.list_ref, s32[2]{0:T(128)S(1)} %reduce_sum.47.count_ref, bf16[16,32,1024]{2,1,0:T(8,128)(2,1)S(1)} %collective-permute-done.q_ref, bf16[16,1024,128]{2,1,0:T(8,128)(2,1)} %all-to-all-done.1.kv_ref), custom_call_target="tpu_custom_call" | custom-call | flops 4294967296 | bytes 6291456 | tf_op jit(solution)/shard_map/attend_far/pallas_call | solution.py:163
  150.7 8.2 %all-to-all-start.2 = ((bf16[16,32,1152]{2,1,0:T(8,128)(2,1)}), bf16[16,32,1152]{2,1,0:T(8,128)(2,1)S(1)}, u32[]{:S(2)}, u32[]{:S(2)}) async-start(bf16[16,32,1152]{2,1,0:T(8,128)(2,1)} %attend_far.1), calls=%async_computation.2 | async-start | bytes 2359296 | tf_op jit(solution)/shard_map/all_to_all | solution.py:336
  158.9 1.2 copy-done.7
  160.1 18.2 %attend_own.1 = bf16[16,32,1152]{2,1,0:T(8,128)(2,1)S(1)} custom-call(s32[2,16]{1,0:T(2,128)S(1)} %compare_select_fusion.list_ref, s32[2]{0:T(128)S(1)} %reduce_sum.47.count_ref, bf16[16,32,1024]{2,1,0:T(8,128)(2,1)S(1)} %copy-done.7, bf16[16,1024,128]{2,1,0:T(8,128)(2,1)} %all-to-all-done.1.kv_ref), custom_call_target="tpu_custom_call" | custom-call | flops 4294967296 | bytes 6291456 | tf_op jit(solution)/shard_map/attend_own/pallas_call | solution.py:163
  178.3 1.0 copy-done.5
  179.4 10.5 %all-to-all-start.3 = ((bf16[16,32,1152]{2,1,0:T(8,128)(2,1)}), bf16[16,32,1152]{2,1,0:T(8,128)(2,1)S(1)}, u32[]{:S(2)}, u32[]{:S(2)}) async-start(bf16[16,32,1152]{2,1,0:T(8,128)(2,1)} %copy-done.5), calls=%async_computation.3 | async-start | bytes 2359296 | tf_op jit(solution)/shard_map/all_to_all | solution.py:339
  189.9 6.3 %collective-permute-start.1 = (s32[1,256]{1,0:T(1,128)S(1)}, s32[1,256]{1,0:T(1,128)S(1)}, u32[]{:S(2)}, u32[]{:S(2)}) collective-permute-start(s32[1,256]{1,0:T(1,128)S(1)} %bitcast.38), channel_id=1, source_target_pairs={{0,32},{32,0},{1,33},{33,1},{2,34},{34,2},{3,35},{35,3},{4,36},{36... | collective-permute-start | bytes 3080 | tf_op jit(solution)/shard_map/ppermute | solution.py:304
  196.2 1.0 collective-permute-done.1.row_ref
  197.2 0.8 copy.29.col_ref
  198.0 0.9 copy-done.8
  198.9 1.7 collect.1
  200.6 5.4 %collective-permute-start.2 = (bf16[128,2304]{1,0:T(8,128)(2,1)}, bf16[128,2304]{1,0:T(8,128)(2,1)S(1)}, u32[]{:S(2)}, u32[]{:S(2)}) collective-permute-start(bf16[128,2304]{1,0:T(8,128)(2,1)} %collect.1), channel_id=1, source_target_pairs={{0,32},{32,0},{1,33},{33,1},{2,34},{34,2},{3,35},{35,3},{4,36},{36... | collective-permute-start | bytes 1769480 | tf_op jit(solution)/shard_map/ppermute | solution.py:304
  205.9 7.5 %collective-permute-done.2.far_ref = bf16[128,2304]{1,0:T(8,128)(2,1)S(1)} collective-permute-done((bf16[128,2304]{1,0:T(8,128)(2,1)}, bf16[128,2304]{1,0:T(8,128)(2,1)S(1)}, u32[]{:S(2)}, u32[]{:S(2)}) %collective-permute-start.2) | collective-permute-done | bytes 589856 | tf_op jit(solution)/shard_map/ppermute | solution.py:304
  213.4 3.4 %copy-done.1 = bf16[1024,4096]{1,0:T(8,128)(2,1)S(1)} copy-done((bf16[1024,4096]{1,0:T(8,128)(2,1)S(1)}, bf16[1024,4096]{1,0:T(8,128)(2,1)}, u32[]{:S(2)}) %copy-start.1) | copy-done | bytes 8388632
  216.8 1.2 copy-done.2
  218.0 6.2 %merge_project.1 = (bf16[128,4096]{1,0:T(8,128)(2,1)S(1)}, bf16[128,4096]{1,0:T(8,128)(2,1)S(1)}) custom-call(s32[1]{0:T(128)} %bitcast.me_ref, s32[256,1]{1,0:T(8,128)S(1)} %copy.30.col_ref, s32[1,256]{1,0:T(1,128)S(1)} %bitcast.39, bf16[512,1152]{1,0:T(8,128)(2,1)S(1)} %bitcast.34, bf16[128,2304]{1,0:T(8,128)(2,1)S(1)} %collective-permute-done.2.far_ref, ...), custom_call_target="tpu_custom_call" | custom-call | flops 2147483648 | bytes 16777216 | tf_op jit(solution)/shard_map/merge_project/pallas_call | solution.py:265
  224.2 37.0 %collective-permute-start.3 = (bf16[128,4096]{1,0:T(8,128)(2,1)S(1)}, bf16[128,4096]{1,0:T(8,128)(2,1)S(1)}, u32[]{:S(2)}, u32[]{:S(2)}) collective-permute-start(bf16[128,4096]{1,0:T(8,128)(2,1)S(1)} %get-tuple-element.30), channel_id=1, source_target_pairs={{0,1},{1,0},{2,3},{3,2},{4,5},{5,4},{6,7},{7,6},{8,9},{9,8},{10,11... | collective-permute-start | bytes 3145736 | tf_op jit(solution)/shard_map/ppermute | solution.py:304
  261.2 2.3 collective-permute-done.3
  263.5 0.3 add_convert_fusion.1
  263.9 13.1 %collective-permute-done.4 = bf16[64,4096]{1,0:T(8,128)(2,1)S(1)} collective-permute-done((bf16[64,4096]{1,0:T(8,128)(2,1)S(1)}, bf16[64,4096]{1,0:T(8,128)(2,1)S(1)}, u32[]{:S(2)}, u32[]{:S(2)}) %collective-permute-start.4) | collective-permute-done | bytes 524320 | tf_op jit(solution)/shard_map/ppermute | solution.py:304
  277.2 14.7 %collective-permute-done.5 = bf16[32,4096]{1,0:T(8,128)(2,1)S(1)} collective-permute-done((bf16[32,4096]{1,0:T(8,128)(2,1)S(1)}, bf16[32,4096]{1,0:T(8,128)(2,1)S(1)}, u32[]{:S(2)}, u32[]{:S(2)}) %collective-permute-start.5) | collective-permute-done | bytes 262176 | tf_op jit(solution)/shard_map/ppermute | solution.py:304
  291.8 0.8 add_convert_fusion.2
  (32 shorter events, 0.6 us)
Async XLA Ops:
  0.0 11.6 %copy-start.12 = (s32[1,32]{1,0:T(1,128)S(1)}, s32[1,32]{1,0:T(1,128)}, u32[]{:S(2)}) copy-start(s32[1,32]{1,0:T(1,128)} %param.8) | copy-start | bytes 388
  0.8 1.0 copy-start.3
  1.9 0.7 copy-start.9
  4.0 23.1 %all-to-all-start = ((bf16[16,32,1024]{2,1,0:T(8,128)(2,1)}), bf16[16,32,1024]{2,1,0:T(8,128)(2,1)S(1)}, u32[]{:S(2)}, u32[]{:S(2)}) async-start(bf16[16,32,1024]{2,1,0:T(8,128)(2,1)} %bitcast.7), calls=%async_computation | async-start | bytes 2097152 | tf_op jit(solution)/shard_map/all_to_all | solution.py:317
  14.9 2.0 copy-start
  27.1 73.4 %copy-start.6 = (bf16[16,32,1024]{2,1,0:T(8,128)(2,1)}, bf16[16,32,1024]{2,1,0:T(8,128)(2,1)S(1)}, u32[]{:S(2)}) copy-start(bf16[16,32,1024]{2,1,0:T(8,128)(2,1)S(1)} %all-to-all-done.q_ref) | copy-start | bytes 3145732
  27.1 4.7 %copy-start.4 = (bf16[256,1024]{1,0:T(8,128)(2,1)S(1)}, bf16[256,1024]{1,0:T(8,128)(2,1)}, u32[]{:S(2)}) copy-start(bf16[256,1024]{1,0:T(8,128)(2,1)} %q_ref.1) | copy-start | bytes 1572868
  27.2 66.8 %copy-start.11 = (s32[256]{0:T(256)S(1)}, s32[256]{0:T(256)}, u32[]{:S(2)}) copy-start(s32[256]{0:T(256)} %param.11) | copy-start | bytes 3076
  27.2 104.6 %all-to-all-start.1 = ((bf16[16,1024,128]{2,1,0:T(8,128)(2,1)}), bf16[16,1024,128]{2,1,0:T(8,128)(2,1)}, u32[]{:S(2)}, u32[]{:S(2)}) async-start(bf16[16,1024,128]{2,1,0:T(8,128)(2,1)} %bitcast.32), calls=%async_computation.1 | async-start | bytes 8388608 | tf_op jit(solution)/shard_map/all_to_all | solution.py:328
  100.6 31.2 %collective-permute-start = (bf16[16,32,1024]{2,1,0:T(8,128)(2,1)S(1)}, bf16[16,32,1024]{2,1,0:T(8,128)(2,1)S(1)}, u32[]{:S(2)}, u32[]{:S(2)}) collective-permute-start(bf16[16,32,1024]{2,1,0:T(8,128)(2,1)S(1)} %all-to-all-done.q_ref), channel_id=1, source_target_pairs={{0,32},{32,0},{1,33},{33,1},{2,34},{34,2},{3,35},{35,3},{4,36},{36... | collective-permute-start | bytes 3145736 | tf_op jit(solution)/shard_map/ppermute | solution.py:304
  150.7 28.7 %all-to-all-start.2 = ((bf16[16,32,1152]{2,1,0:T(8,128)(2,1)}), bf16[16,32,1152]{2,1,0:T(8,128)(2,1)S(1)}, u32[]{:S(2)}, u32[]{:S(2)}) async-start(bf16[16,32,1152]{2,1,0:T(8,128)(2,1)} %attend_far.1), calls=%async_computation.2 | async-start | bytes 2359296 | tf_op jit(solution)/shard_map/all_to_all | solution.py:336
  158.9 1.2 copy-start.7
  178.3 1.0 copy-start.5
  179.4 10.5 %copy-start.10 = (s32[256,1]{0,1:T(1,128)S(1)}, s32[256,1]{0,1:T(1,128)}, u32[]{:S(2)}) copy-start(s32[256,1]{0,1:T(1,128)} %param.12) | copy-start | bytes 3076
  179.4 34.0 %all-to-all-start.3 = ((bf16[16,32,1152]{2,1,0:T(8,128)(2,1)}), bf16[16,32,1152]{2,1,0:T(8,128)(2,1)S(1)}, u32[]{:S(2)}, u32[]{:S(2)}) async-start(bf16[16,32,1152]{2,1,0:T(8,128)(2,1)} %copy-done.5), calls=%async_computation.3 | async-start | bytes 2359296 | tf_op jit(solution)/shard_map/all_to_all | solution.py:339
  189.9 7.3 %collective-permute-start.1 = (s32[1,256]{1,0:T(1,128)S(1)}, s32[1,256]{1,0:T(1,128)S(1)}, u32[]{:S(2)}, u32[]{:S(2)}) collective-permute-start(s32[1,256]{1,0:T(1,128)S(1)} %bitcast.38), channel_id=1, source_target_pairs={{0,32},{32,0},{1,33},{33,1},{2,34},{34,2},{3,35},{35,3},{4,36},{36... | collective-permute-start | bytes 3080 | tf_op jit(solution)/shard_map/ppermute | solution.py:304
  198.0 0.9 copy-start.8
  200.6 12.9 %collective-permute-start.2 = (bf16[128,2304]{1,0:T(8,128)(2,1)}, bf16[128,2304]{1,0:T(8,128)(2,1)S(1)}, u32[]{:S(2)}, u32[]{:S(2)}) collective-permute-start(bf16[128,2304]{1,0:T(8,128)(2,1)} %collect.1), channel_id=1, source_target_pairs={{0,32},{32,0},{1,33},{33,1},{2,34},{34,2},{3,35},{35,3},{4,36},{36... | collective-permute-start | bytes 1769480 | tf_op jit(solution)/shard_map/ppermute | solution.py:304
  213.4 3.4 %copy-start.1 = (bf16[1024,4096]{1,0:T(8,128)(2,1)S(1)}, bf16[1024,4096]{1,0:T(8,128)(2,1)}, u32[]{:S(2)}) copy-start(bf16[1024,4096]{1,0:T(8,128)(2,1)} %w_ref.1) | copy-start | bytes 25165828
  216.8 1.2 copy-start.2
  224.2 39.3 %collective-permute-start.3 = (bf16[128,4096]{1,0:T(8,128)(2,1)S(1)}, bf16[128,4096]{1,0:T(8,128)(2,1)S(1)}, u32[]{:S(2)}, u32[]{:S(2)}) collective-permute-start(bf16[128,4096]{1,0:T(8,128)(2,1)S(1)} %get-tuple-element.30), channel_id=1, source_target_pairs={{0,1},{1,0},{2,3},{3,2},{4,5},{5,4},{6,7},{7,6},{8,9},{9,8},{10,11... | collective-permute-start | bytes 3145736 | tf_op jit(solution)/shard_map/ppermute | solution.py:304
  263.8 13.2 %collective-permute-start.4 = (bf16[64,4096]{1,0:T(8,128)(2,1)S(1)}, bf16[64,4096]{1,0:T(8,128)(2,1)S(1)}, u32[]{:S(2)}, u32[]{:S(2)}) collective-permute-start(bf16[64,4096]{1,0:T(8,128)(2,1)S(1)} %get-tuple-element.32), channel_id=1, source_target_pairs={{0,2},{2,0},{4,6},{6,4},{1,3},{3,1},{5,7},{7,5},{8,10},{10,8},{12,... | collective-permute-start | bytes 1572872 | tf_op jit(solution)/shard_map/ppermute | solution.py:304
  277.1 14.8 %collective-permute-start.5 = (bf16[32,4096]{1,0:T(8,128)(2,1)S(1)}, bf16[32,4096]{1,0:T(8,128)(2,1)S(1)}, u32[]{:S(2)}, u32[]{:S(2)}) collective-permute-start(bf16[32,4096]{1,0:T(8,128)(2,1)S(1)} %add_convert_fusion.3), channel_id=1, source_target_pairs={{0,4},{2,6},{4,0},{6,2},{1,5},{3,7},{5,1},{7,3},{8,12},{10,14},{12... | collective-permute-start | bytes 786440 | tf_op jit(solution)/shard_map/ppermute | solution.py:304

commit v3 on v2

--- a/solution.py
+++ b/solution.py
@@ -15,6 +15,7 @@
 SCALE = HD**-0.5
 LOG2E = 1.4426950408889634
 LOW = -1e30
+MARK = 16384.0
 F32 = jnp.float32
 BF16 = jnp.bfloat16
 
@@ -62,7 +63,13 @@
 
 def place_kernel(pick_ref, pages_ref, out_ref):
     def one(slot, carry):
-        out_ref[slot] = pages_ref[pick_ref[slot]]
+        src = pick_ref[slot]
+        out_ref[slot] = pages_ref[jnp.maximum(src, 0)]
+
+        @pl.when(src < 0)
+        def _():
+            out_ref[slot, :16, :] = jnp.full((16, HD), MARK, BF16)
+
         return carry
 
     lax.fori_loop(0, out_ref.shape[0], one, 0)
@@ -81,18 +88,28 @@
     )(pick, pages)
 
 
-def attend_kernel(width, list_ref, count_ref, q_ref, kv_ref, out_ref, key_ref, value_ref, s_ref, acc_ref):
+def attend_kernel(width, q_ref, kv_ref, out_ref, list_ref, key_ref, value_ref, s_ref, acc_ref):
     sub = pl.program_id(0)
-    span = kv_ref.shape[1] // 4
+    peers, span = kv_ref.shape[0], kv_ref.shape[1] // 4
     group, cap = q_ref.shape[0], q_ref.shape[1]
     key_at = pl.multiple_of(sub * 2 * span, 2 * span)
-    count = count_ref[sub]
-    even = ((count + 1) // 2) * 2
 
     @pl.when(pl.program_id(1) == 0)
     def _():
+        there = [
+            (jnp.max(kv_ref[src, pl.ds(key_at, 16), :].astype(F32)) < MARK / 2).astype(jnp.int32)
+            for src in range(peers)
+        ]
+        count = jnp.int32(0)
+        for src in range(peers):
+            list_ref[count] = src
+            count = count + there[src]
+        list_ref[count] = list_ref[0]
+        list_ref[peers + 1] = count
+        even = ((count + 1) // 2) * 2
+
         def pack(n, carry):
-            src = list_ref[sub, n]
+            src = list_ref[n]
             at = pl.multiple_of(n * span, span)
             weight = jnp.where(n < count, 1.0, 0.0).astype(BF16)
             key_ref[pl.ds(at, span), :] = kv_ref[src, pl.ds(key_at, span), :]
@@ -102,6 +119,8 @@
 
         lax.fori_loop(0, even, pack, 0)
 
+    count = list_ref[peers + 1]
+    even = ((count + 1) // 2) * 2
     heads = [(j, h) for j in range(group) for h in range(G)]
     q = jnp.concatenate([q_ref[j, :, h * HD : (h + 1) * HD] for j, h in heads], axis=0)
     fours = even // 4
@@ -154,24 +173,22 @@
         out_ref[j, :, width:] = jnp.where(lane < 24, part, 0.0).astype(BF16)
 
 
-def attend(listed, count, q, kv, name):
+def attend(q, kv, name):
     peers, rows, width = q.shape
     group = 8
     span = kv.shape[1] // 4
     m = group * CAP * G
-    smem = pl.BlockSpec(memory_space=pltpu.SMEM)
     return pl.pallas_call(
         functools.partial(attend_kernel, width),
         grid=(2, peers // group),
         out_shape=jax.ShapeDtypeStruct((peers, rows, width + HD), BF16),
         in_specs=[
-            smem,
-            smem,
             pl.BlockSpec((group, CAP, width), lambda s, i: (i, s, 0)),
             pl.BlockSpec(memory_space=pltpu.VMEM),
         ],
         out_specs=pl.BlockSpec((group, CAP, width + HD), lambda s, i: (i, s, 0)),
         scratch_shapes=[
+            pltpu.SMEM((peers + 2,), jnp.int32),
             pltpu.VMEM((peers * span, HD), BF16),
             pltpu.VMEM((peers * span, 2 * HD), BF16),
             pltpu.VMEM((m, peers * span), F32),
@@ -184,20 +201,7 @@
             transcendentals=peers * rows * G * 8 * span,
         ),
         name=name,
-    )(listed, count, q, kv)
-
-
-def pages_here(owner):
-    plane = owner.shape[0]
-    mine = lax.axis_index("x") * 8 + lax.axis_index("y") + 4 * jnp.arange(2, dtype=jnp.int32)
-    there = jnp.max((owner[None] == mine[:, None, None]).astype(jnp.int32), axis=2)
-    peer = jnp.arange(plane, dtype=jnp.int32)
-    rank = jnp.sum(there[:, None, :] * (peer[None, :] < peer[:, None]).astype(jnp.int32)[None], axis=2)
-    hit = (there[:, None, :] == 1) & (rank[:, None, :] == peer[None, :, None])
-    listed = jnp.sum(jnp.where(hit, peer[None, None, :], 0), axis=2)
-    count = jnp.sum(there, axis=1)
-    listed = jnp.where(peer[None, :] < count[:, None], listed, listed[:, :1])
-    return listed.astype(jnp.int32), count.astype(jnp.int32)
+    )(q, kv)
 
 
 def collect_kernel(col_ref, row_ref, replies_ref, out_ref):
@@ -222,56 +226,67 @@
     )(ids_col, ids_row, replies)
 
 
-def merge_kernel(me_ref, col_ref, row_ref, own_ref, far_ref, suf_ref, suf_lse_ref, w_ref, send_ref, keep_ref, att_ref):
-    @pl.when(pl.program_id(0) == 0)
-    def _():
-        n, width = suf_ref.shape
-        slot = slots_as_col(col_ref[...], row_ref[...])
-        pick = jnp.where(lax.broadcasted_iota(jnp.int32, (n, own_ref.shape[0]), 1) == slot, 1.0, 0.0)
-        own = jnp.dot(pick.astype(BF16), own_ref[...], preferred_element_type=F32)
-        far = jnp.concatenate([far_ref[:, : width + HD], far_ref[:, width + HD :]], axis=0)
-        i = lax.broadcasted_iota(jnp.int32, (HD, width), 0)
-        c = lax.broadcasted_iota(jnp.int32, (HD, width), 1)
-        spread = jnp.where((i < 24) & ((i & 7) == (c >> 7)), 1.0, 0.0).astype(BF16)
-        own_lse = jnp.dot(own[:, width:].astype(BF16), spread, preferred_element_type=F32)
-        far_lse = jnp.dot(far[:, width:], spread, preferred_element_type=F32)
-        suf_lse = suf_lse_ref[...]
-        top = jnp.maximum(jnp.maximum(own_lse, far_lse), suf_lse)
-        a = jnp.exp(own_lse - top)
-        b = jnp.exp(far_lse - top)
-        s = jnp.exp(suf_lse - top)
-        att = (a * own[:, :width] + b * far[:, :width].astype(F32) + s * suf_ref[...]) / (a + b + s)
-        att_ref[0] = att.astype(BF16)
-        me = me_ref[0]
-        step = n // 8
-        for q in range(8):
-            flip = (1 - q // 4) + 2 * (1 - (q // 2) % 2) + 4 * (1 - q % 2)
-            at = pl.multiple_of((me ^ flip) * step, step)
-            att_ref[1, q * step : (q + 1) * step] = att_ref[0, pl.ds(at, step), :]
-
+def merge_kernel(me_ref, col_ref, row_ref, own_ref, far_ref, suf_ref, suf_lse_ref, w_ref, send_ref, keep_ref, att_ref, w_buf, sem):
+    tile = w_ref.shape[1] // sem.shape[0]
+    fetches = [
+        pltpu.make_async_copy(
+            w_ref.at[:, pl.ds(t * tile, tile)], w_buf.at[:, pl.ds(t * tile, tile)], sem.at[t]
+        )
+        for t in range(sem.shape[0])
+    ]
+    for fetch in fetches:
+        fetch.start()
+    n, width = suf_ref.shape
+    slot = slots_as_col(col_ref[...], row_ref[...])
+    pick = jnp.where(lax.broadcasted_iota(jnp.int32, (n, own_ref.shape[0]), 1) == slot, 1.0, 0.0)
+    own = jnp.dot(pick.astype(BF16), own_ref[...], preferred_element_type=F32)
+    far = jnp.concatenate([far_ref[:, : width + HD], far_ref[:, width + HD :]], axis=0)
+    i = lax.broadcasted_iota(jnp.int32, (HD, width), 0)
+    c = lax.broadcasted_iota(jnp.int32, (HD, width), 1)
+    spread = jnp.where((i < 24) & ((i & 7) == (c >> 7)), 1.0, 0.0).astype(BF16)
+    own_lse = jnp.dot(own[:, width:].astype(BF16), spread, preferred_element_type=F32)
+    far_lse = jnp.dot(far[:, width:], spread, preferred_element_type=F32)
+    suf_lse = suf_lse_ref[...]
+    top = jnp.maximum(jnp.maximum(own_lse, far_lse), suf_lse)
+    a = jnp.exp(own_lse - top)
+    b = jnp.exp(far_lse - top)
+    s = jnp.exp(suf_lse - top)
+    att = (a * own[:, :width] + b * far[:, :width].astype(F32) + s * suf_ref[...]) / (a + b + s)
+    att_ref[0] = att.astype(BF16)
+    me = me_ref[0]
+    step = n // 8
+    for q in range(8):
+        flip = (1 - q // 4) + 2 * (1 - (q // 2) % 2) + 4 * (1 - q % 2)
+        at = pl.multiple_of((me ^ flip) * step, step)
+        att_ref[1, q * step : (q + 1) * step] = att_ref[0, pl.ds(at, step), :]
     half = send_ref.shape[0]
-    out = jnp.dot(att_ref[1], w_ref[...], preferred_element_type=F32).astype(BF16)
-    send_ref[...] = out[:half]
-    keep_ref[...] = out[half:]
+    for t, fetch in enumerate(fetches):
+        fetch.wait()
+        out = jnp.dot(
+            att_ref[1], w_buf[:, t * tile : (t + 1) * tile], preferred_element_type=F32
+        ).astype(BF16)
+        send_ref[:, t * tile : (t + 1) * tile] = out[:half]
+        keep_ref[:, t * tile : (t + 1) * tile] = out[half:]
 
 
 def merge_project(me, ids_col, ids_row, own, far, suf, suf_lse, weight):
     n, width = suf.shape
     columns = weight.shape[1]
-    tile = 512
     whole = pl.BlockSpec(memory_space=pltpu.VMEM)
     shape = jax.ShapeDtypeStruct((n // 2, columns), BF16)
-    block = pl.BlockSpec((n // 2, tile), lambda c: (0, c))
     return pl.pallas_call(
         merge_kernel,
-        grid=(columns // tile,),
         out_shape=(shape, shape),
         in_specs=[pl.BlockSpec(memory_space=pltpu.SMEM)]
         + [whole] * 6
-        + [pl.BlockSpec((width, tile), lambda c: (0, c))],
-        out_specs=(block, block),
-        scratch_shapes=[pltpu.VMEM((2, n, width), BF16)],
-        compiler_params=pltpu.CompilerParams(vmem_limit_bytes=40 * 2**20),
+        + [pl.BlockSpec(memory_space=pl.ANY)],
+        out_specs=(whole, whole),
+        scratch_shapes=[
+            pltpu.VMEM((2, n, width), BF16),
+            pltpu.VMEM(weight.shape, BF16),
+            pltpu.SemaphoreType.DMA((8,)),
+        ],
+        compiler_params=pltpu.CompilerParams(vmem_limit_bytes=48 * 2**20),
         cost_estimate=pl.CostEstimate(
             flops=2 * n * width * columns, bytes_accessed=16 * 2**20, transcendentals=3 * n * width
         ),
@@ -311,30 +326,29 @@
     pairs = pages // 2
     ids_col, ids_row = prefix_id, prefix_id.reshape(1, seq)
     far_row = swap(ids_row, "zh", 1)
-    far_col = far_row.reshape(seq, 1)
 
     sent = dispatch(ids_col, ids_row, queries, plane * 2 * CAP).reshape(plane, 2 * CAP, width)
     own_q = lax.all_to_all(sent, PLANE, 0, 0, tiled=True)
 
     owner = page_owner[0, ::2]
-    listed, count = pages_here(lax.all_gather(owner, PLANE))
     slot = slot_base(owner) // CAP
     here = jnp.arange(2 * plane, dtype=jnp.int32)[:, None] == slot[None, :]
-    pick = jnp.sum(jnp.where(here, jnp.arange(pairs, dtype=jnp.int32)[None, :], 0), axis=1)
+    pick = jnp.sum(jnp.where(here, jnp.arange(pairs, dtype=jnp.int32)[None, :] + 1, 0), axis=1) - 1
     paired = jnp.swapaxes(prefill_pages.reshape(pairs, 2 * page, 2, HD), 1, 2)
     paired = paired.reshape(pairs, 4 * page, HD)
     placed = place(pick, paired, 2 * plane).reshape(plane, 8 * page, HD)
-    placed, own_q = lax.optimization_barrier((placed, own_q))
+    placed, own_q, far_row, later = lax.optimization_barrier((placed, own_q, far_row, queries))
+    far_col = far_row.reshape(seq, 1)
     kv = lax.all_to_all(placed, PLANE, 0, 0, tiled=True)
     far_q = swap(own_q, "zh", 1)
 
-    suf, suf_lse = suffix_attend(queries, suffix_cache, suffix_len)
-    far_q, suf, suf_lse, listed, count = lax.optimization_barrier((far_q, suf, suf_lse, listed, count))
-
-    far_out = attend(listed, count, far_q, kv, "attend_far")
+    suf, suf_lse = suffix_attend(later, suffix_cache, suffix_len)
+    far_q, suf, suf_lse = lax.optimization_barrier((far_q, suf, suf_lse))
+
+    far_out = attend(far_q, kv, "attend_far")
     far_out, own_q = lax.optimization_barrier((far_out, own_q))
     far_back = lax.all_to_all(far_out, PLANE, 0, 0, tiled=True)
-    own_out = attend(listed, count, own_q, kv, "attend_own")
+    own_out = attend(own_q, kv, "attend_own")
     far_back, own_out = lax.optimization_barrier((far_back, own_out))
     own_back = lax.all_to_all(own_out, PLANE, 0, 0, tiled=True)
     far_part = collect(far_col, far_row, far_back.reshape(plane * 2 * CAP, width + HD))

time: 291 us -> 218 us (0.75)
  blocking collectives: 61.3 us -> 0 us
  local copies, waits for them, and re-layouts: 23.1 us -> 18.4 us
  Pallas kernels: 47.5 us -> 43.4 us
  starting transfers between devices: 86.9 us -> 83.9 us
    all_gather x1 -> x0, blocking collectives: 61.3 us -> none  [local(): listed, count = pages_here(lax.all_gather(owner, PLANE))]
    ppermute x6, starting transfers between devices: 55.9 us -> 44.6 us  [swap(): return lax.ppermute(value, axis, [(i, i ^ bit) for i in range(size)])]
    all_to_all x1, waiting for transfers between devices: 0.01 us -> 9.77 us  [local(): kv = lax.all_to_all(placed, PLANE, 0, 0, tiled=True)]
    all_to_all x1, waiting for transfers between devices: 10.2 us -> 2.99 us  [local(): own_q = lax.all_to_all(sent, PLANE, 0, 0, tiled=True)]
    all_to_all x1, starting transfers between devices: 8.19 us -> 13.7 us  [local(): far_back = lax.all_to_all(far_out, PLANE, 0, 0, tiled=True)]
    unnamed x28 -> x22, local copies, waits for them, and re-layouts: 12.4 us -> 7.84 us
    pallas_call x2, Pallas kernels: 37.2 us -> 33.6 us  [attend(): pl.pallas_call(functools.partial(attend_kernel, width), grid=(2, peers //...]
  transfers between devices with their start and end apart: 10 -> 10, of which waited for: 7 -> 7; matrix products, arithmetic and copies ran while one was open for 5% -> 6% of each run, Pallas kernels for 7% -> 9%
where the time goes in v3:
time: 218 us; the launch traced here: 220 us
  starting transfers between devices  83.9 us (38%)
  waiting for transfers between devices  69.6 us (32%)
  Pallas kernels  43.4 us (20%)
  local copies, waits for them, and re-layouts  18.4 us (8%)
    ppermute x6, waiting for transfers between devices, swap(): return lax.ppermute(value, axis, [(i, i ^ bit) for i in range(size)])  56.8 us
    ppermute x6, starting transfers between devices, swap(): return lax.ppermute(value, axis, [(i, i ^ bit) for i in range(size)])  44.6 us
    pallas_call x2, Pallas kernels, attend(): pl.pallas_call(functools.partial(attend_kernel, width), grid=(2, peers //...  33.6 us
    all_to_all x1, starting transfers between devices, local(): far_back = lax.all_to_all(far_out, PLANE, 0, 0, tiled=True)  13.7 us
    all_to_all x1, starting transfers between devices, local(): own_back = lax.all_to_all(own_out, PLANE, 0, 0, tiled=True)  13.3 us
    all_to_all x1, waiting for transfers between devices, local(): kv = lax.all_to_all(placed, PLANE, 0, 0, tiled=True)  9.77 us
    unnamed x22, local copies, waits for them, and re-layouts  7.84 us
    all_to_all x1, starting transfers between devices, local(): own_q = lax.all_to_all(sent, PLANE, 0, 0, tiled=True)  7.58 us
  transfers between devices with their start and end apart: 10, of which 7 were waited for; matrix products, arithmetic and copies ran while one was open for 6% of the time, Pallas kernels for 9%

profile of v3, /device:TPU:1, one launch (start us, length us, event | category | flops | bytes accessed | tf_op | source)
XLA Modules:
  0.0 219.5 jit_solution(5768269972418503978)
XLA Ops:
  0.0 0.9 copy.24.col_ref
  0.9 0.0 copy-start.2
  0.9 1.0 copy-done.2
  1.9 0.7 copy-done.6
  2.6 1.5 dispatch.1
  4.1 7.6 %all-to-all-start = ((bf16[16,32,1024]{2,1,0:T(8,128)(2,1)}), bf16[16,32,1024]{2,1,0:T(8,128)(2,1)S(1)}, u32[]{:S(2)}, u32[]{:S(2)}) async-start(bf16[16,32,1024]{2,1,0:T(8,128)(2,1)} %bitcast.7), calls=%async_computation | async-start | bytes 2097152 | tf_op jit(solution)/shard_map/all_to_all | solution.py:331
  11.7 7.0 %collective-permute-start = (s32[1,256]{1,0:T(1,128)S(1)}, s32[1,256]{1,0:T(1,128)S(1)}, u32[]{:S(2)}, u32[]{:S(2)}) collective-permute-start(s32[1,256]{1,0:T(1,128)S(1)} %bitcast.36), channel_id=1, source_target_pairs={{0,32},{32,0},{1,33},{33,1},{2,34},{34,2},{3,35},{35,3},{4,36},{36... | collective-permute-start | bytes 3080 | tf_op jit(solution)/shard_map/ppermute | solution.py:319
  18.7 0.1 slice.33
  18.9 0.1 select_reduce_fusion
  19.0 2.1 copy.19
  21.1 1.2 place.1
  22.3 2.0 copy-done
  24.2 0.0 collective-permute-done.row_ref
  24.2 3.0 %all-to-all-done.q_ref = bf16[16,32,1024]{2,1,0:T(8,128)(2,1)S(1)} async-done(((bf16[16,32,1024]{2,1,0:T(8,128)(2,1)}), bf16[16,32,1024]{2,1,0:T(8,128)(2,1)S(1)}, u32[]{:S(2)}, u32[]{:S(2)}) %all-to-all-start) | async-done | bytes 1048608 | tf_op jit(solution)/shard_map/all_to_all | solution.py:331
  27.2 4.7 %all-to-all-start.1 = ((bf16[16,1024,128]{2,1,0:T(8,128)(2,1)}), bf16[16,1024,128]{2,1,0:T(8,128)(2,1)}, u32[]{:S(2)}, u32[]{:S(2)}) async-start(bf16[16,1024,128]{2,1,0:T(8,128)(2,1)} %bitcast.30), calls=%async_computation.1 | async-start | bytes 8388608 | tf_op jit(solution)/shard_map/all_to_all | solution.py:342
  31.9 0.1 iota_compare_fusion
  32.0 0.0 copy-start.3
  32.0 5.7 %fusion.9 = (bf16[256,16,1,128]{3,2,1,0:T(2,128)(2,1)S(1)}, bf16[256,16,1,128]{3,2,1,0:T(2,128)(2,1)S(1)}) fusion(bf16[256,16,2,128]{3,2,1,0:T(2,128)(2,1)} %param.10), kind=kLoop, calls=%fused_computation.30 | loop fusion | bytes 4194304 | tf_op jit(solution)/shard_map/slice | solution.py:302
  37.8 0.1 copy.27
  37.9 7.0 %collective-permute-start.1 = (bf16[16,32,1024]{2,1,0:T(8,128)(2,1)S(1)}, bf16[16,32,1024]{2,1,0:T(8,128)(2,1)S(1)}, u32[]{:S(2)}, u32[]{:S(2)}) collective-permute-start(bf16[16,32,1024]{2,1,0:T(8,128)(2,1)S(1)} %all-to-all-done.q_ref), channel_id=1, source_target_pairs={{0,32},{32,0},{1,33},{33,1},{2,34},{34,2},{3,35},{35,3},{4,36},{36... | collective-permute-start | bytes 3145736 | tf_op jit(solution)/shard_map/ppermute | solution.py:319
  44.9 0.7 fusion.10
  45.6 0.7 fusion.1
  46.4 1.2 convolution_divide_fusion
  47.6 0.3 broadcast_in_dim.49
  47.9 1.6 copy_bitcast_fusion
  49.5 20.3 %collective-permute-done.1.q_ref = bf16[16,32,1024]{2,1,0:T(8,128)(2,1)S(1)} collective-permute-done((bf16[16,32,1024]{2,1,0:T(8,128)(2,1)S(1)}, bf16[16,32,1024]{2,1,0:T(8,128)(2,1)S(1)}, u32[]{:S(2)}, u32[]{:S(2)}) %collective-permute-start.1) | collective-permute-done | bytes 1048608 | tf_op jit(solution)/shard_map/ppermute | solution.py:319
  69.8 9.8 %all-to-all-done.1.kv_ref = bf16[16,1024,128]{2,1,0:T(8,128)(2,1)} async-done(((bf16[16,1024,128]{2,1,0:T(8,128)(2,1)}), bf16[16,1024,128]{2,1,0:T(8,128)(2,1)}, u32[]{:S(2)}, u32[]{:S(2)}) %all-to-all-start.1) | async-done | bytes 4194336 | tf_op jit(solution)/shard_map/all_to_all | solution.py:342
  79.6 17.1 %attend_far.1 = bf16[16,32,1152]{2,1,0:T(8,128)(2,1)} custom-call(bf16[16,32,1024]{2,1,0:T(8,128)(2,1)S(1)} %collective-permute-done.1.q_ref, bf16[16,1024,128]{2,1,0:T(8,128)(2,1)} %all-to-all-done.1.kv_ref), custom_call_target="tpu_custom_call" | custom-call | flops 4294967296 | bytes 6291456 | tf_op jit(solution)/shard_map/attend_far/pallas_call | solution.py:181
  96.7 13.7 %all-to-all-start.2 = ((bf16[16,32,1152]{2,1,0:T(8,128)(2,1)}), bf16[16,32,1152]{2,1,0:T(8,128)(2,1)S(1)}, u32[]{:S(2)}, u32[]{:S(2)}) async-start(bf16[16,32,1152]{2,1,0:T(8,128)(2,1)} %attend_far.1), calls=%async_computation.2 | async-start | bytes 2359296 | tf_op jit(solution)/shard_map/all_to_all | solution.py:350
  110.4 16.5 %attend_own.1 = bf16[16,32,1152]{2,1,0:T(8,128)(2,1)S(1)} custom-call(bf16[16,32,1024]{2,1,0:T(8,128)(2,1)S(1)} %all-to-all-done.q_ref, bf16[16,1024,128]{2,1,0:T(8,128)(2,1)} %all-to-all-done.1.kv_ref), custom_call_target="tpu_custom_call" | custom-call | flops 4294967296 | bytes 6291456 | tf_op jit(solution)/shard_map/attend_own/pallas_call | solution.py:181
  126.9 1.0 copy-done.4
  128.0 13.3 %all-to-all-start.3 = ((bf16[16,32,1152]{2,1,0:T(8,128)(2,1)}), bf16[16,32,1152]{2,1,0:T(8,128)(2,1)S(1)}, u32[]{:S(2)}, u32[]{:S(2)}) async-start(bf16[16,32,1152]{2,1,0:T(8,128)(2,1)} %copy-done.4), calls=%async_computation.3 | async-start | bytes 2359296 | tf_op jit(solution)/shard_map/all_to_all | solution.py:353
  141.3 0.8 copy.23.col_ref
  142.1 0.9 copy-done.5
  143.0 1.7 collect.1
  144.6 8.4 %collective-permute-start.2 = (bf16[128,2304]{1,0:T(8,128)(2,1)}, bf16[128,2304]{1,0:T(8,128)(2,1)S(1)}, u32[]{:S(2)}, u32[]{:S(2)}) collective-permute-start(bf16[128,2304]{1,0:T(8,128)(2,1)} %collect.1), channel_id=1, source_target_pairs={{0,32},{32,0},{1,33},{33,1},{2,34},{34,2},{3,35},{35,3},{4,36},{36... | collective-permute-start | bytes 1769480 | tf_op jit(solution)/shard_map/ppermute | solution.py:319
  153.0 7.8 %collective-permute-done.2.far_ref = bf16[128,2304]{1,0:T(8,128)(2,1)S(1)} collective-permute-done((bf16[128,2304]{1,0:T(8,128)(2,1)}, bf16[128,2304]{1,0:T(8,128)(2,1)S(1)}, u32[]{:S(2)}, u32[]{:S(2)}) %collective-permute-start.2) | collective-permute-done | bytes 589856 | tf_op jit(solution)/shard_map/ppermute | solution.py:319
  160.8 1.2 copy-done.1
  162.0 5.4 %merge_project.1 = (bf16[128,4096]{1,0:T(8,128)(2,1)S(1)}, bf16[128,4096]{1,0:T(8,128)(2,1)S(1)}) custom-call(s32[1]{0:T(128)} %bitcast.me_ref, s32[256,1]{1,0:T(8,128)S(1)} %copy.24.col_ref, s32[1,256]{1,0:T(1,128)S(1)} %bitcast.37, bf16[512,1152]{1,0:T(8,128)(2,1)S(1)} %bitcast.32, bf16[128,2304]{1,0:T(8,128)(2,1)S(1)} %collective-permute-done.2.far_ref, ...), custom_call_target="tpu_custom_call" | custom-call | flops 2147483648 | bytes 16777216 | tf_op jit(solution)/shard_map/merge_project/pallas_call | solution.py:277
  167.5 20.7 %collective-permute-start.3 = (bf16[128,4096]{1,0:T(8,128)(2,1)S(1)}, bf16[128,4096]{1,0:T(8,128)(2,1)S(1)}, u32[]{:S(2)}, u32[]{:S(2)}) collective-permute-start(bf16[128,4096]{1,0:T(8,128)(2,1)S(1)} %get-tuple-element.30), channel_id=1, source_target_pairs={{0,1},{1,0},{2,3},{3,2},{4,5},{5,4},{6,7},{7,6},{8,9},{9,8},{10,11... | collective-permute-start | bytes 3145736 | tf_op jit(solution)/shard_map/ppermute | solution.py:319
  188.2 2.3 %collective-permute-done.3 = bf16[128,4096]{1,0:T(8,128)(2,1)S(1)} collective-permute-done((bf16[128,4096]{1,0:T(8,128)(2,1)S(1)}, bf16[128,4096]{1,0:T(8,128)(2,1)S(1)}, u32[]{:S(2)}, u32[]{:S(2)}) %collective-permute-start.3) | collective-permute-done | bytes 1048608 | tf_op jit(solution)/shard_map/ppermute | solution.py:319
  190.5 0.3 add_convert_fusion.1
  190.7 0.5 collective-permute-start.4
  191.3 12.7 %collective-permute-done.4 = bf16[64,4096]{1,0:T(8,128)(2,1)S(1)} collective-permute-done((bf16[64,4096]{1,0:T(8,128)(2,1)S(1)}, bf16[64,4096]{1,0:T(8,128)(2,1)S(1)}, u32[]{:S(2)}, u32[]{:S(2)}) %collective-permute-start.4) | collective-permute-done | bytes 524320 | tf_op jit(solution)/shard_map/ppermute | solution.py:319
  204.0 0.1 add_convert_fusion.3
  204.0 1.0 collective-permute-start.5
  205.0 13.7 %collective-permute-done.5 = bf16[32,4096]{1,0:T(8,128)(2,1)S(1)} collective-permute-done((bf16[32,4096]{1,0:T(8,128)(2,1)S(1)}, bf16[32,4096]{1,0:T(8,128)(2,1)S(1)}, u32[]{:S(2)}, u32[]{:S(2)}) %collective-permute-start.5) | collective-permute-done | bytes 262176 | tf_op jit(solution)/shard_map/ppermute | solution.py:319
  218.7 0.8 add_convert_fusion.2
  (18 shorter events, 0.1 us)
Async XLA Ops:
  0.0 11.7 %copy-start.7 = (s32[256,1]{0,1:T(1,128)S(1)}, s32[256,1]{0,1:T(1,128)}, u32[]{:S(2)}) copy-start(s32[256,1]{0,1:T(1,128)} %param.12) | copy-start | bytes 3076
  0.0 18.7 %copy-start.9 = (s32[1,32]{1,0:T(1,128)S(1)}, s32[1,32]{1,0:T(1,128)}, u32[]{:S(2)}) copy-start(s32[1,32]{1,0:T(1,128)} %param.8) | copy-start | bytes 388
  0.9 1.0 copy-start.2
  1.9 0.7 copy-start.6
  4.1 23.1 %all-to-all-start = ((bf16[16,32,1024]{2,1,0:T(8,128)(2,1)}), bf16[16,32,1024]{2,1,0:T(8,128)(2,1)S(1)}, u32[]{:S(2)}, u32[]{:S(2)}) async-start(bf16[16,32,1024]{2,1,0:T(8,128)(2,1)} %bitcast.7), calls=%async_computation | async-start | bytes 2097152 | tf_op jit(solution)/shard_map/all_to_all | solution.py:331
  11.7 12.5 %collective-permute-start = (s32[1,256]{1,0:T(1,128)S(1)}, s32[1,256]{1,0:T(1,128)S(1)}, u32[]{:S(2)}, u32[]{:S(2)}) collective-permute-start(s32[1,256]{1,0:T(1,128)S(1)} %bitcast.36), channel_id=1, source_target_pairs={{0,32},{32,0},{1,33},{33,1},{2,34},{34,2},{3,35},{35,3},{4,36},{36... | collective-permute-start | bytes 3080 | tf_op jit(solution)/shard_map/ppermute | solution.py:319
  22.3 2.0 copy-start
  27.2 4.7 %copy-start.8 = (s32[256]{0:T(256)S(1)}, s32[256]{0:T(256)}, u32[]{:S(2)}) copy-start(s32[256]{0:T(256)} %param.11) | copy-start | bytes 3076
  27.2 52.3 %all-to-all-start.1 = ((bf16[16,1024,128]{2,1,0:T(8,128)(2,1)}), bf16[16,1024,128]{2,1,0:T(8,128)(2,1)}, u32[]{:S(2)}, u32[]{:S(2)}) async-start(bf16[16,1024,128]{2,1,0:T(8,128)(2,1)} %bitcast.30), calls=%async_computation.1 | async-start | bytes 8388608 | tf_op jit(solution)/shard_map/all_to_all | solution.py:342
  32.0 5.7 %copy-start.3 = (bf16[256,1024]{1,0:T(8,128)(2,1)S(1)}, bf16[256,1024]{1,0:T(8,128)(2,1)}, u32[]{:S(2)}) copy-start(bf16[256,1024]{1,0:T(8,128)(2,1)} %q_ref.1) | copy-start | bytes 1572868
  37.9 31.9 %collective-permute-start.1 = (bf16[16,32,1024]{2,1,0:T(8,128)(2,1)S(1)}, bf16[16,32,1024]{2,1,0:T(8,128)(2,1)S(1)}, u32[]{:S(2)}, u32[]{:S(2)}) collective-permute-start(bf16[16,32,1024]{2,1,0:T(8,128)(2,1)S(1)} %all-to-all-done.q_ref), channel_id=1, source_target_pairs={{0,32},{32,0},{1,33},{33,1},{2,34},{34,2},{3,35},{35,3},{4,36},{36... | collective-permute-start | bytes 3145736 | tf_op jit(solution)/shard_map/ppermute | solution.py:319
  96.7 31.2 %all-to-all-start.2 = ((bf16[16,32,1152]{2,1,0:T(8,128)(2,1)}), bf16[16,32,1152]{2,1,0:T(8,128)(2,1)S(1)}, u32[]{:S(2)}, u32[]{:S(2)}) async-start(bf16[16,32,1152]{2,1,0:T(8,128)(2,1)} %attend_far.1), calls=%async_computation.2 | async-start | bytes 2359296 | tf_op jit(solution)/shard_map/all_to_all | solution.py:350
  126.9 1.0 copy-start.4
  128.0 32.8 %all-to-all-start.3 = ((bf16[16,32,1152]{2,1,0:T(8,128)(2,1)}), bf16[16,32,1152]{2,1,0:T(8,128)(2,1)S(1)}, u32[]{:S(2)}, u32[]{:S(2)}) async-start(bf16[16,32,1152]{2,1,0:T(8,128)(2,1)} %copy-done.4), calls=%async_computation.3 | async-start | bytes 2359296 | tf_op jit(solution)/shard_map/all_to_all | solution.py:353
  142.1 0.9 copy-start.5
  144.6 16.1 %collective-permute-start.2 = (bf16[128,2304]{1,0:T(8,128)(2,1)}, bf16[128,2304]{1,0:T(8,128)(2,1)S(1)}, u32[]{:S(2)}, u32[]{:S(2)}) collective-permute-start(bf16[128,2304]{1,0:T(8,128)(2,1)} %collect.1), channel_id=1, source_target_pairs={{0,32},{32,0},{1,33},{33,1},{2,34},{34,2},{3,35},{35,3},{4,36},{36... | collective-permute-start | bytes 1769480 | tf_op jit(solution)/shard_map/ppermute | solution.py:319
  160.8 1.2 copy-start.1
  167.5 23.0 %collective-permute-start.3 = (bf16[128,4096]{1,0:T(8,128)(2,1)S(1)}, bf16[128,4096]{1,0:T(8,128)(2,1)S(1)}, u32[]{:S(2)}, u32[]{:S(2)}) collective-permute-start(bf16[128,4096]{1,0:T(8,128)(2,1)S(1)} %get-tuple-element.30), channel_id=1, source_target_pairs={{0,1},{1,0},{2,3},{3,2},{4,5},{5,4},{6,7},{7,6},{8,9},{9,8},{10,11... | collective-permute-start | bytes 3145736 | tf_op jit(solution)/shard_map/ppermute | solution.py:319
  190.7 13.2 %collective-permute-start.4 = (bf16[64,4096]{1,0:T(8,128)(2,1)S(1)}, bf16[64,4096]{1,0:T(8,128)(2,1)S(1)}, u32[]{:S(2)}, u32[]{:S(2)}) collective-permute-start(bf16[64,4096]{1,0:T(8,128)(2,1)S(1)} %get-tuple-element.32), channel_id=1, source_target_pairs={{0,2},{2,0},{4,6},{6,4},{1,3},{3,1},{5,7},{7,5},{8,10},{10,8},{12,... | collective-permute-start | bytes 1572872 | tf_op jit(solution)/shard_map/ppermute | solution.py:319
  204.0 14.7 %collective-permute-start.5 = (bf16[32,4096]{1,0:T(8,128)(2,1)S(1)}, bf16[32,4096]{1,0:T(8,128)(2,1)S(1)}, u32[]{:S(2)}, u32[]{:S(2)}) collective-permute-start(bf16[32,4096]{1,0:T(8,128)(2,1)S(1)} %add_convert_fusion.3), channel_id=1, source_target_pairs={{0,4},{2,6},{4,0},{6,2},{1,5},{3,7},{5,1},{7,3},{8,12},{10,14},{12... | collective-permute-start | bytes 786440 | tf_op jit(solution)/shard_map/ppermute | solution.py:319

commit v4 on v3

--- a/solution.py
+++ b/solution.py
@@ -88,8 +88,9 @@
     )(pick, pages)
 
 
-def attend_kernel(width, q_ref, kv_ref, out_ref, list_ref, key_ref, value_ref, s_ref, acc_ref):
-    sub = pl.program_id(0)
+def attend_kernel(width, first, q_ref, kv_ref, *refs):
+    out_ref, list_ref, key_ref, value_ref, s_ref, acc_ref = refs[-6:]
+    sub = pl.program_id(0) + first
     peers, span = kv_ref.shape[0], kv_ref.shape[1] // 4
     group, cap = q_ref.shape[0], q_ref.shape[1]
     key_at = pl.multiple_of(sub * 2 * span, 2 * span)
@@ -173,20 +174,22 @@
         out_ref[j, :, width:] = jnp.where(lane < 24, part, 0.0).astype(BF16)
 
 
-def attend(q, kv, name):
+def attend(q, kv, name, first, number, begun=None):
     peers, rows, width = q.shape
     group = 8
     span = kv.shape[1] // 4
     m = group * CAP * G
     return pl.pallas_call(
-        functools.partial(attend_kernel, width),
-        grid=(2, peers // group),
+        functools.partial(attend_kernel, width, first),
+        grid=(number, peers // group),
         out_shape=jax.ShapeDtypeStruct((peers, rows, width + HD), BF16),
         in_specs=[
-            pl.BlockSpec((group, CAP, width), lambda s, i: (i, s, 0)),
+            pl.BlockSpec((group, CAP, width), lambda s, i: (i, s + first, 0)),
             pl.BlockSpec(memory_space=pltpu.VMEM),
-        ],
-        out_specs=pl.BlockSpec((group, CAP, width + HD), lambda s, i: (i, s, 0)),
+        ]
+        + [pl.BlockSpec(memory_space=pl.ANY)] * (begun is not None),
+        out_specs=pl.BlockSpec((group, CAP, width + HD), lambda s, i: (i, s + first, 0)),
+        input_output_aliases={} if begun is None else {2: 0},
         scratch_shapes=[
             pltpu.SMEM((peers + 2,), jnp.int32),
             pltpu.VMEM((peers * span, HD), BF16),
@@ -194,30 +197,31 @@
             pltpu.VMEM((m, peers * span), F32),
             pltpu.VMEM((m, 2 * HD), F32),
         ],
-        compiler_params=pltpu.CompilerParams(vmem_limit_bytes=48 * 2**20),
+        compiler_params=pltpu.CompilerParams(vmem_limit_bytes=34 * 2**20),
         cost_estimate=pl.CostEstimate(
-            flops=4 * peers * rows * G * 8 * span * HD,
-            bytes_accessed=6 * 2**20,
-            transcendentals=peers * rows * G * 8 * span,
+            flops=2 * number * peers * rows * G * 8 * span * HD,
+            bytes_accessed=3 * number * 2**20,
+            transcendentals=number * peers * rows * G * 4 * span,
         ),
         name=name,
-    )(q, kv)
-
-
-def collect_kernel(col_ref, row_ref, replies_ref, out_ref):
+    )(*((q, kv) if begun is None else (q, kv, begun)))
+
+
+def collect_kernel(col_ref, row_ref, replies_ref, low_ref, high_ref):
     slot = slots_as_col(col_ref[...], row_ref[...])
     n, width = slot.shape[0], replies_ref.shape[1]
     pick = jnp.where(lax.broadcasted_iota(jnp.int32, (n, replies_ref.shape[0]), 1) == slot, 1.0, 0.0)
     rows = jnp.dot(pick.astype(BF16), replies_ref[...], preferred_element_type=F32).astype(BF16)
-    out_ref[:, :width] = rows[: n // 2]
-    out_ref[:, width:] = rows[n // 2 :]
+    for ref, at in ((low_ref, 0), (high_ref, n // 2)):
+        ref[:, :width] = rows[at : at + n // 4]
+        ref[:, width:] = rows[at + n // 4 : at + n // 2]
 
 
 def collect(ids_col, ids_row, replies):
     n = ids_col.shape[0]
     return pl.pallas_call(
         collect_kernel,
-        out_shape=jax.ShapeDtypeStruct((n // 2, 2 * replies.shape[1]), BF16),
+        out_shape=(jax.ShapeDtypeStruct((n // 4, 2 * replies.shape[1]), BF16),) * 2,
         compiler_params=pltpu.CompilerParams(vmem_limit_bytes=32 * 2**20),
         cost_estimate=pl.CostEstimate(
             flops=2 * n * replies.shape[0] * replies.shape[1], bytes_accessed=2**21, transcendentals=0
@@ -226,21 +230,39 @@
     )(ids_col, ids_row, replies)
 
 
-def merge_kernel(me_ref, col_ref, row_ref, own_ref, far_ref, suf_ref, suf_lse_ref, w_ref, send_ref, keep_ref, att_ref, w_buf, sem):
-    tile = w_ref.shape[1] // sem.shape[0]
+def fetch_weight(w_ref, w_buf, sem, first):
+    tile = w_buf.shape[1] // sem.shape[0]
     fetches = [
         pltpu.make_async_copy(
-            w_ref.at[:, pl.ds(t * tile, tile)], w_buf.at[:, pl.ds(t * tile, tile)], sem.at[t]
+            w_ref.at[:, pl.ds(first + t * tile, tile)], w_buf.at[:, pl.ds(t * tile, tile)], sem.at[t]
         )
         for t in range(sem.shape[0])
     ]
     for fetch in fetches:
         fetch.start()
+    return fetches
+
+
+def project(fetches, att_ref, w_buf, send_ref, keep_ref):
+    half = send_ref.shape[0]
+    tile = w_buf.shape[1] // len(fetches)
+    for t, fetch in enumerate(fetches):
+        fetch.wait()
+        out = jnp.dot(
+            att_ref[...], w_buf[:, t * tile : (t + 1) * tile], preferred_element_type=F32
+        ).astype(BF16)
+        send_ref[:, t * tile : (t + 1) * tile] = out[:half]
+        keep_ref[:, t * tile : (t + 1) * tile] = out[half:]
+
+
+def merge_kernel(me_ref, col_ref, row_ref, own_ref, low_ref, high_ref, suf_ref, suf_lse_ref, w_ref, att_ref, send_ref, keep_ref, plain_ref, w_buf, sem):
+    fetches = fetch_weight(w_ref, w_buf, sem, 0)
     n, width = suf_ref.shape
     slot = slots_as_col(col_ref[...], row_ref[...])
     pick = jnp.where(lax.broadcasted_iota(jnp.int32, (n, own_ref.shape[0]), 1) == slot, 1.0, 0.0)
     own = jnp.dot(pick.astype(BF16), own_ref[...], preferred_element_type=F32)
-    far = jnp.concatenate([far_ref[:, : width + HD], far_ref[:, width + HD :]], axis=0)
+    cut = width + HD
+    far = jnp.concatenate([low_ref[:, :cut], low_ref[:, cut:], high_ref[:, :cut], high_ref[:, cut:]], axis=0)
     i = lax.broadcasted_iota(jnp.int32, (HD, width), 0)
     c = lax.broadcasted_iota(jnp.int32, (HD, width), 1)
     spread = jnp.where((i < 24) & ((i & 7) == (c >> 7)), 1.0, 0.0).astype(BF16)
@@ -252,46 +274,51 @@
     b = jnp.exp(far_lse - top)
     s = jnp.exp(suf_lse - top)
     att = (a * own[:, :width] + b * far[:, :width].astype(F32) + s * suf_ref[...]) / (a + b + s)
-    att_ref[0] = att.astype(BF16)
+    plain_ref[...] = att.astype(BF16)
     me = me_ref[0]
     step = n // 8
     for q in range(8):
         flip = (1 - q // 4) + 2 * (1 - (q // 2) % 2) + 4 * (1 - q % 2)
         at = pl.multiple_of((me ^ flip) * step, step)
-        att_ref[1, q * step : (q + 1) * step] = att_ref[0, pl.ds(at, step), :]
-    half = send_ref.shape[0]
-    for t, fetch in enumerate(fetches):
-        fetch.wait()
-        out = jnp.dot(
-            att_ref[1], w_buf[:, t * tile : (t + 1) * tile], preferred_element_type=F32
-        ).astype(BF16)
-        send_ref[:, t * tile : (t + 1) * tile] = out[:half]
-        keep_ref[:, t * tile : (t + 1) * tile] = out[half:]
-
-
-def merge_project(me, ids_col, ids_row, own, far, suf, suf_lse, weight):
+        att_ref[q * step : (q + 1) * step] = plain_ref[pl.ds(at, step), :]
+    project(fetches, att_ref, w_buf, send_ref, keep_ref)
+
+
+def project_kernel(first, att_ref, w_ref, send_ref, keep_ref, w_buf, sem):
+    project(fetch_weight(w_ref, w_buf, sem, first), att_ref, w_buf, send_ref, keep_ref)
+
+
+def merge_project(me, ids_col, ids_row, own, low, high, suf, suf_lse, weight):
     n, width = suf.shape
-    columns = weight.shape[1]
+    columns = weight.shape[1] // 2
     whole = pl.BlockSpec(memory_space=pltpu.VMEM)
     shape = jax.ShapeDtypeStruct((n // 2, columns), BF16)
-    return pl.pallas_call(
+    scratch = [pltpu.VMEM((width, columns), BF16), pltpu.SemaphoreType.DMA((4,))]
+    params = pltpu.CompilerParams(vmem_limit_bytes=56 * 2**20)
+    cost = pl.CostEstimate(flops=2 * n * width * columns, bytes_accessed=8 * 2**20, transcendentals=n * width)
+    att, send_a, keep_a = pl.pallas_call(
         merge_kernel,
+        out_shape=(jax.ShapeDtypeStruct((n, width), BF16), shape, shape),
+        in_specs=[pl.BlockSpec(memory_space=pltpu.SMEM)]
+        + [whole] * 7
+        + [pl.BlockSpec(memory_space=pl.ANY)],
+        out_specs=(whole, whole, whole),
+        scratch_shapes=[pltpu.VMEM((n, width), BF16)] + scratch,
+        compiler_params=params,
+        cost_estimate=cost,
+        name="merge_project",
+    )(me, ids_col, ids_row, own, low, high, suf, suf_lse, weight)
+    send_b, keep_b = pl.pallas_call(
+        functools.partial(project_kernel, columns),
         out_shape=(shape, shape),
-        in_specs=[pl.BlockSpec(memory_space=pltpu.SMEM)]
-        + [whole] * 6
-        + [pl.BlockSpec(memory_space=pl.ANY)],
+        in_specs=[whole, pl.BlockSpec(memory_space=pl.ANY)],
         out_specs=(whole, whole),
-        scratch_shapes=[
-            pltpu.VMEM((2, n, width), BF16),
-            pltpu.VMEM(weight.shape, BF16),
-            pltpu.SemaphoreType.DMA((8,)),
-        ],
-        compiler_params=pltpu.CompilerParams(vmem_limit_bytes=48 * 2**20),
-        cost_estimate=pl.CostEstimate(
-            flops=2 * n * width * columns, bytes_accessed=16 * 2**20, transcendentals=3 * n * width
-        ),
-        name="merge_project",
-    )(me, ids_col, ids_row, own, far, suf, suf_lse, weight)
+        scratch_shapes=scratch,
+        compiler_params=params,
+        cost_estimate=cost,
+        name="project",
+    )(att, weight)
+    return (send_a, keep_a), (send_b, keep_b)
 
 
 def suffix_attend(queries, suffix_cache, suffix_len):
@@ -345,30 +372,35 @@
     suf, suf_lse = suffix_attend(later, suffix_cache, suffix_len)
     far_q, suf, suf_lse = lax.optimization_barrier((far_q, suf, suf_lse))
 
-    far_out = attend(far_q, kv, "attend_far")
+    far_out = attend(far_q, kv, "attend_far", 0, 2)
     far_out, own_q = lax.optimization_barrier((far_out, own_q))
     far_back = lax.all_to_all(far_out, PLANE, 0, 0, tiled=True)
-    own_out = attend(own_q, kv, "attend_own")
+    own_out = attend(own_q, kv, "attend_own", 0, 1)
     far_back, own_out = lax.optimization_barrier((far_back, own_out))
+    far_part = collect(far_col, far_row, far_back.reshape(plane * 2 * CAP, width + HD))
+    far_part, own_out = lax.optimization_barrier((far_part, own_out))
+    far_low = swap(far_part[0], "zh", 1)
+    far_high = swap(far_part[1], "zh", 1)
+    own_out = attend(own_q, kv, "attend_own", 1, 1, own_out)
+    far_low, own_out = lax.optimization_barrier((far_low, own_out))
     own_back = lax.all_to_all(own_out, PLANE, 0, 0, tiled=True)
-    far_part = collect(far_col, far_row, far_back.reshape(plane * 2 * CAP, width + HD))
-    far_part = swap(far_part, "zh", 1)
 
     me = (lax.axis_index("zl") * 2 + lax.axis_index("core")).astype(jnp.int32).reshape(1)
-    send, keep = merge_project(
-        me, ids_col, ids_row, own_back.reshape(plane * 2 * CAP, width + HD), far_part, suf, suf_lse, out_weight
+    halves = merge_project(
+        me, ids_col, ids_row, own_back.reshape(plane * 2 * CAP, width + HD), far_low, far_high, suf, suf_lse, out_weight
     )
 
     def add(a, b):
         return (a.astype(F32) + b.astype(F32)).astype(BF16)
 
-    got = swap(send, "core", 1)
-    half = seq // 4
-    send, keep = add(keep[:half], got[:half]), add(keep[half:], got[half:])
-    got = swap(send, "zl", 1)
-    half = seq // 8
-    send, keep = add(keep[:half], got[:half]), add(keep[half:], got[half:])
-    return add(keep, swap(send, "zl", 2))
+    def fold(send, keep, axis, bit):
+        got = swap(send, axis, bit)
+        half = keep.shape[0] // 2
+        return add(keep[:half], got[:half]), add(keep[half:], got[half:])
+
+    halves = [fold(send, keep, "core", 1) for send, keep in halves]
+    halves = [fold(send, keep, "zl", 1) for send, keep in halves]
+    return jnp.concatenate([add(keep, swap(send, "zl", 2)) for send, keep in halves], axis=1)
 
 
 def solution(mesh):

time: 218 us -> 212 us (0.972); the launches traced: 220 us -> 211 us
  starting transfers between devices: 83.9 us -> 69.8 us
  Pallas kernels: 43.4 us -> 54.5 us
  local copies, waits for them, and re-layouts: 18.4 us -> 11.7 us
    pallas_call x4 -> x6, Pallas kernels: 40.7 us -> 51.8 us  [the longest x3 39.2 us: attend(): pl.pallas_call(functools.partial(attend_kernel, width, first), grid=(numb...]
    ppermute x6 -> x10, waiting for transfers between devices: 56.8 us -> 47.7 us  [swap(): return lax.ppermute(value, axis, [(i, i ^ bit) for i in range(size)])]
    all_to_all x1, starting transfers between devices: 13.3 us -> 6.86 us  [local(): own_back = lax.all_to_all(own_out, PLANE, 0, 0, tiled=True)]
    ppermute x6 -> x10, starting transfers between devices: 44.6 us -> 40.4 us  [swap(): return lax.ppermute(value, axis, [(i, i ^ bit) for i in range(size)])]
    all_to_all x1, starting transfers between devices: 13.7 us -> 10.3 us  [local(): far_back = lax.all_to_all(far_out, PLANE, 0, 0, tiled=True)]
    all_to_all x1, waiting for transfers between devices: 0.01 us -> 3.31 us  [local(): own_back = lax.all_to_all(own_out, PLANE, 0, 0, tiled=True)]
    slice x1, local copies, waits for them, and re-layouts: 5.71 us -> 2.97 us  [suffix_attend(): suffix_cache[:, :, 0]]
    all_to_all x1, waiting for transfers between devices: 9.77 us -> 12.5 us  [local(): kv = lax.all_to_all(placed, PLANE, 0, 0, tiled=True)]
  transfers between devices with their start and end apart: 10 -> 14, of which waited for: 7 -> 9; matrix products, arithmetic and copies ran while one was open for 6% -> 5% of each run, Pallas kernels for 9% -> 13%
where the time goes in v4:
time: 212 us; the launch traced here: 211 us
  starting transfers between devices  69.8 us (33%)
  waiting for transfers between devices  69.8 us (33%)
  Pallas kernels  54.5 us (26%)
  local copies, waits for them, and re-layouts  11.7 us (6%)
  other arithmetic  3.13 us (1%)
    ppermute x10, waiting for transfers between devices, swap(): return lax.ppermute(value, axis, [(i, i ^ bit) for i in range(size)])  47.7 us
    ppermute x10, starting transfers between devices, swap(): return lax.ppermute(value, axis, [(i, i ^ bit) for i in range(size)])  40.4 us
    pallas_call x3, Pallas kernels, attend(): pl.pallas_call(functools.partial(attend_kernel, width, first), grid=(numb...  39.2 us
    all_to_all x1, waiting for transfers between devices, local(): kv = lax.all_to_all(placed, PLANE, 0, 0, tiled=True)  12.5 us
    all_to_all x1, starting transfers between devices, local(): far_back = lax.all_to_all(far_out, PLANE, 0, 0, tiled=True)  10.3 us
    all_to_all x1, starting transfers between devices, local(): own_q = lax.all_to_all(sent, PLANE, 0, 0, tiled=True)  7.58 us
    all_to_all x1, starting transfers between devices, local(): own_back = lax.all_to_all(own_out, PLANE, 0, 0, tiled=True)  6.86 us
    pallas_call x1, Pallas kernels, merge_project(): pl.pallas_call(merge_kernel, out_shape=(jax.ShapeDtypeStruct((n, width),...  6.7 us
  transfers between devices with their start and end apart: 14, of which 9 were waited for; matrix products, arithmetic and copies ran while one was open for 5% of the time, Pallas kernels for 13%

profile of v4, /device:TPU:1, one launch (start us, length us, event | category | flops | bytes accessed | tf_op | source)
XLA Modules:
  0.0 211.2 jit_solution(17538653369368977185)
XLA Ops:
  0.0 0.9 copy.25.col_ref
  0.9 1.1 copy-done.1
  2.0 0.7 copy-done.4
  2.7 1.5 dispatch.1
  4.2 7.6 %all-to-all-start = ((bf16[16,32,1024]{2,1,0:T(8,128)(2,1)}), bf16[16,32,1024]{2,1,0:T(8,128)(2,1)S(1)}, u32[]{:S(2)}, u32[]{:S(2)}) async-start(bf16[16,32,1024]{2,1,0:T(8,128)(2,1)} %bitcast.7), calls=%async_computation | async-start | bytes 2097152 | tf_op jit(solution)/shard_map/all_to_all | solution.py:358
  11.8 7.0 %collective-permute-start = (s32[1,256]{1,0:T(1,128)S(1)}, s32[1,256]{1,0:T(1,128)S(1)}, u32[]{:S(2)}, u32[]{:S(2)}) collective-permute-start(s32[1,256]{1,0:T(1,128)S(1)} %bitcast.36), channel_id=1, source_target_pairs={{0,32},{32,0},{1,33},{33,1},{2,34},{34,2},{3,35},{35,3},{4,36},{36... | collective-permute-start | bytes 3080 | tf_op jit(solution)/shard_map/ppermute | solution.py:346
  18.8 0.1 slice.57
  19.0 0.5 copy.20
  19.5 1.2 place.1
  20.7 2.0 copy-done
  22.8 4.5 %all-to-all-done.q_ref = bf16[16,32,1024]{2,1,0:T(8,128)(2,1)S(1)} async-done(((bf16[16,32,1024]{2,1,0:T(8,128)(2,1)}), bf16[16,32,1024]{2,1,0:T(8,128)(2,1)S(1)}, u32[]{:S(2)}, u32[]{:S(2)}) %all-to-all-start) | async-done | bytes 1048608 | tf_op jit(solution)/shard_map/all_to_all | solution.py:358
  27.3 4.7 %all-to-all-start.1 = ((bf16[16,1024,128]{2,1,0:T(8,128)(2,1)}), bf16[16,1024,128]{2,1,0:T(8,128)(2,1)}, u32[]{:S(2)}, u32[]{:S(2)}) async-start(bf16[16,1024,128]{2,1,0:T(8,128)(2,1)} %bitcast.30), calls=%async_computation.1 | async-start | bytes 8388608 | tf_op jit(solution)/shard_map/all_to_all | solution.py:369
  32.0 0.1 iota_compare_fusion
  32.1 3.0 %fusion.9 = (bf16[256,16,1,128]{3,2,1,0:T(2,128)(2,1)S(1)}, bf16[256,16,1,128]{3,2,1,0:T(2,128)(2,1)S(1)}) fusion(bf16[256,16,2,128]{3,2,1,0:T(2,128)(2,1)S(1)} %copy-done.6), kind=kLoop, calls=%fused_computation.36 | loop fusion | bytes 4194304 | tf_op jit(solution)/shard_map/slice | solution.py:329
  35.2 7.0 %collective-permute-start.1 = (bf16[16,32,1024]{2,1,0:T(8,128)(2,1)S(1)}, bf16[16,32,1024]{2,1,0:T(8,128)(2,1)S(1)}, u32[]{:S(2)}, u32[]{:S(2)}) collective-permute-start(bf16[16,32,1024]{2,1,0:T(8,128)(2,1)S(1)} %all-to-all-done.q_ref), channel_id=1, source_target_pairs={{0,32},{32,0},{1,33},{33,1},{2,34},{34,2},{3,35},{35,3},{4,36},{36... | collective-permute-start | bytes 3145736 | tf_op jit(solution)/shard_map/ppermute | solution.py:346
  42.2 0.7 fusion.10
  42.9 0.7 fusion.1
  43.7 1.2 convolution_divide_fusion
  44.9 0.3 broadcast_in_dim.49
  45.2 1.9 copy_bitcast_fusion
  47.1 20.0 %collective-permute-done.1.q_ref = bf16[16,32,1024]{2,1,0:T(8,128)(2,1)S(1)} collective-permute-done((bf16[16,32,1024]{2,1,0:T(8,128)(2,1)S(1)}, bf16[16,32,1024]{2,1,0:T(8,128)(2,1)S(1)}, u32[]{:S(2)}, u32[]{:S(2)}) %collective-permute-start.1) | collective-permute-done | bytes 1048608 | tf_op jit(solution)/shard_map/ppermute | solution.py:346
  67.1 12.5 %all-to-all-done.1.kv_ref = bf16[16,1024,128]{2,1,0:T(8,128)(2,1)} async-done(((bf16[16,1024,128]{2,1,0:T(8,128)(2,1)}), bf16[16,1024,128]{2,1,0:T(8,128)(2,1)}, u32[]{:S(2)}, u32[]{:S(2)}) %all-to-all-start.1) | async-done | bytes 4194336 | tf_op jit(solution)/shard_map/all_to_all | solution.py:369
  79.6 18.2 %attend_far.1 = bf16[16,32,1152]{2,1,0:T(8,128)(2,1)} custom-call(bf16[16,32,1024]{2,1,0:T(8,128)(2,1)S(1)} %collective-permute-done.1.q_ref, bf16[16,1024,128]{2,1,0:T(8,128)(2,1)} %all-to-all-done.1.kv_ref), custom_call_target="tpu_custom_call" | custom-call | flops 4294967296 | bytes 6291456 | tf_op jit(solution)/shard_map/attend_far/pallas_call | solution.py:182
  97.8 10.3 %all-to-all-start.2 = ((bf16[16,32,1152]{2,1,0:T(8,128)(2,1)}), bf16[16,32,1152]{2,1,0:T(8,128)(2,1)S(1)}, u32[]{:S(2)}, u32[]{:S(2)}) async-start(bf16[16,32,1152]{2,1,0:T(8,128)(2,1)} %attend_far.1), calls=%async_computation.2 | async-start | bytes 2359296 | tf_op jit(solution)/shard_map/all_to_all | solution.py:377
  108.1 0.1 copy.24.col_ref
  108.3 10.5 %attend_own.2.refs_0_ = bf16[16,32,1152]{2,1,0:T(8,128)(2,1)} custom-call(bf16[16,32,1024]{2,1,0:T(8,128)(2,1)S(1)} %all-to-all-done.q_ref, bf16[16,1024,128]{2,1,0:T(8,128)(2,1)} %all-to-all-done.1.kv_ref), custom_call_target="tpu_custom_call" | custom-call | flops 2147483648 | bytes 3145728 | tf_op jit(solution)/shard_map/attend_own/pallas_call | solution.py:182
  118.8 1.8 all-to-all-done.2
  120.6 0.8 collect.1
  121.4 9.6 %collective-permute-start.2 = (bf16[64,2304]{1,0:T(8,128)(2,1)S(1)}, bf16[64,2304]{1,0:T(8,128)(2,1)S(1)}, u32[]{:S(2)}, u32[]{:S(2)}) collective-permute-start(bf16[64,2304]{1,0:T(8,128)(2,1)S(1)} %get-tuple-element.39), channel_id=1, source_target_pairs={{0,32},{32,0},{1,33},{33,1},{2,34},{34,2},{3,35},{35,3},{4,36},{36... | collective-permute-start | bytes 884744 | tf_op jit(solution)/shard_map/ppermute | solution.py:346
  131.1 10.5 %attend_own.3 = bf16[16,32,1152]{2,1,0:T(8,128)(2,1)} custom-call(bf16[16,32,1024]{2,1,0:T(8,128)(2,1)S(1)} %all-to-all-done.q_ref, bf16[16,1024,128]{2,1,0:T(8,128)(2,1)} %all-to-all-done.1.kv_ref, bf16[16,32,1152]{2,1,0:T(8,128)(2,1)} %attend_own.2.refs_0_), custom_call_target="tpu_custom_call", output_to_operand_aliasing={{}: (2, {})} | custom-call | flops 2147483648 | bytes 3145728 | tf_op jit(solution)/shard_map/attend_own/pallas_call | solution.py:182
  141.6 6.9 %all-to-all-start.3 = ((bf16[16,32,1152]{2,1,0:T(8,128)(2,1)}), bf16[16,32,1152]{2,1,0:T(8,128)(2,1)S(1)}, u32[]{:S(2)}, u32[]{:S(2)}) async-start(bf16[16,32,1152]{2,1,0:T(8,128)(2,1)} %attend_own.3), calls=%async_computation.3 | async-start | bytes 2359296 | tf_op jit(solution)/shard_map/all_to_all | solution.py:386
  148.5 0.1 collective-permute-start.3
  148.6 9.4 %collective-permute-done.3.high_ref = bf16[64,2304]{1,0:T(8,128)(2,1)S(1)} collective-permute-done((bf16[64,2304]{1,0:T(8,128)(2,1)S(1)}, bf16[64,2304]{1,0:T(8,128)(2,1)S(1)}, u32[]{:S(2)}, u32[]{:S(2)}) %collective-permute-start.3) | collective-permute-done | bytes 294944 | tf_op jit(solution)/shard_map/ppermute | solution.py:346
  158.0 3.3 %all-to-all-done.3 = bf16[16,32,1152]{2,1,0:T(8,128)(2,1)S(1)} async-done(((bf16[16,32,1152]{2,1,0:T(8,128)(2,1)}), bf16[16,32,1152]{2,1,0:T(8,128)(2,1)S(1)}, u32[]{:S(2)}, u32[]{:S(2)}) %all-to-all-start.3) | async-done | bytes 1179680 | tf_op jit(solution)/shard_map/all_to_all | solution.py:386
  161.4 1.0 copy-done.7
  162.4 6.7 %merge_project.1 = (bf16[256,1024]{1,0:T(8,128)(2,1)}, bf16[128,2048]{1,0:T(8,128)(2,1)}, bf16[128,2048]{1,0:T(8,128)(2,1)}) custom-call(s32[1]{0:T(128)} %bitcast.me_ref, s32[256,1]{1,0:T(8,128)} %copy-done.3, s32[1,256]{1,0:T(1,128)} %bitcast.34, bf16[512,1152]{1,0:T(8,128)(2,1)} %bitcast.38, bf16[64,2304]{1,0:T(8,128)(2,1)} %copy-done.10, ...), custom_call_target="tpu_custom_call" | custom-call | flops 1073741824 | bytes 8388608 | tf_op jit(solution)/shard_map/merge_project/pallas_call | solution.py:299
  169.1 7.0 %collective-permute-start.4 = (bf16[128,2048]{1,0:T(8,128)(2,1)}, bf16[128,2048]{1,0:T(8,128)(2,1)S(1)}, u32[]{:S(2)}, u32[]{:S(2)}) collective-permute-start(bf16[128,2048]{1,0:T(8,128)(2,1)} %get-tuple-element.47), channel_id=1, source_target_pairs={{0,1},{1,0},{2,3},{3,2},{4,5},{5,4},{6,7},{7,6},{8,9},{9,8},{10,11... | collective-permute-start | bytes 1572872 | tf_op jit(solution)/shard_map/ppermute | solution.py:346
  176.1 5.1 %project.1 = (bf16[128,2048]{1,0:T(8,128)(2,1)}, bf16[128,2048]{1,0:T(8,128)(2,1)}) custom-call(bf16[256,1024]{1,0:T(8,128)(2,1)} %get-tuple-element.48.att_ref, bf16[1024,4096]{1,0:T(8,128)(2,1)} %w_ref.3), custom_call_target="tpu_custom_call" | custom-call | flops 1073741824 | bytes 8388608 | tf_op jit(solution)/shard_map/project/pallas_call | solution.py:311
  181.2 0.1 collective-permute-start.7
  181.3 0.1 add_convert_fusion.3
  181.4 5.5 %collective-permute-start.5 = (bf16[64,2048]{1,0:T(8,128)(2,1)S(1)}, bf16[64,2048]{1,0:T(8,128)(2,1)S(1)}, u32[]{:S(2)}, u32[]{:S(2)}) collective-permute-start(bf16[64,2048]{1,0:T(8,128)(2,1)S(1)} %get-tuple-element.54), channel_id=1, source_target_pairs={{0,2},{2,0},{4,6},{6,4},{1,3},{3,1},{5,7},{7,5},{8,10},{10,8},{12,... | collective-permute-start | bytes 786440 | tf_op jit(solution)/shard_map/ppermute | solution.py:346
  186.9 1.2 add_convert_fusion.1
  188.0 1.9 collective-permute-start.8
  190.0 3.1 %collective-permute-done.5 = bf16[64,2048]{1,0:T(8,128)(2,1)S(1)} collective-permute-done((bf16[64,2048]{1,0:T(8,128)(2,1)S(1)}, bf16[64,2048]{1,0:T(8,128)(2,1)S(1)}, u32[]{:S(2)}, u32[]{:S(2)}) %collective-permute-start.5) | collective-permute-done | bytes 262176 | tf_op jit(solution)/shard_map/ppermute | solution.py:346
  193.2 2.0 collective-permute-start.6
  195.2 6.4 %collective-permute-done.8 = bf16[64,2048]{1,0:T(8,128)(2,1)S(1)} collective-permute-done((bf16[64,2048]{1,0:T(8,128)(2,1)S(1)}, bf16[64,2048]{1,0:T(8,128)(2,1)S(1)}, u32[]{:S(2)}, u32[]{:S(2)}) %collective-permute-start.8) | collective-permute-done | bytes 262176 | tf_op jit(solution)/shard_map/ppermute | solution.py:346
  201.8 8.6 %collective-permute-done.9 = bf16[32,2048]{1,0:T(8,128)(2,1)S(1)} collective-permute-done((bf16[32,2048]{1,0:T(8,128)(2,1)S(1)}, bf16[32,2048]{1,0:T(8,128)(2,1)S(1)}, u32[]{:S(2)}, u32[]{:S(2)}) %collective-permute-start.9) | collective-permute-done | bytes 131104 | tf_op jit(solution)/shard_map/ppermute | solution.py:346
  210.4 0.7 pad_maximum_fusion
  (40 shorter events, 0.6 us)
Async XLA Ops:
  0.0 11.8 %copy-start.5 = (s32[256,1]{0,1:T(1,128)S(1)}, s32[256,1]{0,1:T(1,128)}, u32[]{:S(2)}) copy-start(s32[256,1]{0,1:T(1,128)} %param.12) | copy-start | bytes 3076
  0.0 18.8 %copy-start.13 = (s32[1,32]{1,0:T(1,128)S(1)}, s32[1,32]{1,0:T(1,128)}, u32[]{:S(2)}) copy-start(s32[1,32]{1,0:T(1,128)} %param.8) | copy-start | bytes 388
  0.9 18.6 %copy-start.3 = (s32[256,1]{1,0:T(8,128)}, s32[256,1]{1,0:T(8,128)S(1)}, u32[]{:S(2)}) copy-start(s32[256,1]{1,0:T(8,128)S(1)} %copy.25.col_ref) | copy-start | bytes 3076
  0.9 1.1 copy-start.1
  2.0 0.7 copy-start.4
  2.7 16.3 %copy-start.8 = (bf16[32,128,2,128]{3,2,1,0:T(2,128)(2,1)S(1)}, bf16[32,128,2,128]{3,2,1,0:T(2,128)(2,1)}, u32[]{:S(2)}) copy-start(bf16[32,128,2,128]{3,2,1,0:T(2,128)(2,1)} %param.7) | copy-start | bytes 6291460
  4.2 23.1 %all-to-all-start = ((bf16[16,32,1024]{2,1,0:T(8,128)(2,1)}), bf16[16,32,1024]{2,1,0:T(8,128)(2,1)S(1)}, u32[]{:S(2)}, u32[]{:S(2)}) async-start(bf16[16,32,1024]{2,1,0:T(8,128)(2,1)} %bitcast.7), calls=%async_computation | async-start | bytes 2097152 | tf_op jit(solution)/shard_map/all_to_all | solution.py:358
  11.8 11.0 %collective-permute-start = (s32[1,256]{1,0:T(1,128)S(1)}, s32[1,256]{1,0:T(1,128)S(1)}, u32[]{:S(2)}, u32[]{:S(2)}) collective-permute-start(s32[1,256]{1,0:T(1,128)S(1)} %bitcast.36), channel_id=1, source_target_pairs={{0,32},{32,0},{1,33},{33,1},{2,34},{34,2},{3,35},{35,3},{4,36},{36... | collective-permute-start | bytes 3080 | tf_op jit(solution)/shard_map/ppermute | solution.py:346
  20.7 2.0 copy-start
  27.3 4.7 %copy-start.12 = (s32[256]{0:T(256)S(1)}, s32[256]{0:T(256)}, u32[]{:S(2)}) copy-start(s32[256]{0:T(256)} %param.11) | copy-start | bytes 3076
  27.3 4.8 %copy-start.6 = (bf16[256,16,2,128]{3,2,1,0:T(2,128)(2,1)S(1)}, bf16[256,16,2,128]{3,2,1,0:T(2,128)(2,1)}, u32[]{:S(2)}) copy-start(bf16[256,16,2,128]{3,2,1,0:T(2,128)(2,1)} %param.10) | copy-start | bytes 6291460
  27.3 52.4 %all-to-all-start.1 = ((bf16[16,1024,128]{2,1,0:T(8,128)(2,1)}), bf16[16,1024,128]{2,1,0:T(8,128)(2,1)}, u32[]{:S(2)}, u32[]{:S(2)}) async-start(bf16[16,1024,128]{2,1,0:T(8,128)(2,1)} %bitcast.30), calls=%async_computation.1 | async-start | bytes 8388608 | tf_op jit(solution)/shard_map/all_to_all | solution.py:369
  32.1 3.0 %copy-start.2 = (bf16[256,1024]{1,0:T(8,128)(2,1)S(1)}, bf16[256,1024]{1,0:T(8,128)(2,1)}, u32[]{:S(2)}) copy-start(bf16[256,1024]{1,0:T(8,128)(2,1)} %q_ref.1) | copy-start | bytes 1572868
  35.2 31.9 %collective-permute-start.1 = (bf16[16,32,1024]{2,1,0:T(8,128)(2,1)S(1)}, bf16[16,32,1024]{2,1,0:T(8,128)(2,1)S(1)}, u32[]{:S(2)}, u32[]{:S(2)}) collective-permute-start(bf16[16,32,1024]{2,1,0:T(8,128)(2,1)S(1)} %all-to-all-done.q_ref), channel_id=1, source_target_pairs={{0,32},{32,0},{1,33},{33,1},{2,34},{34,2},{3,35},{35,3},{4,36},{36... | collective-permute-start | bytes 3145736 | tf_op jit(solution)/shard_map/ppermute | solution.py:346
  97.8 22.8 %all-to-all-start.2 = ((bf16[16,32,1152]{2,1,0:T(8,128)(2,1)}), bf16[16,32,1152]{2,1,0:T(8,128)(2,1)S(1)}, u32[]{:S(2)}, u32[]{:S(2)}) async-start(bf16[16,32,1152]{2,1,0:T(8,128)(2,1)} %attend_far.1), calls=%async_computation.2 | async-start | bytes 2359296 | tf_op jit(solution)/shard_map/all_to_all | solution.py:377
  121.4 20.2 %collective-permute-start.2 = (bf16[64,2304]{1,0:T(8,128)(2,1)S(1)}, bf16[64,2304]{1,0:T(8,128)(2,1)S(1)}, u32[]{:S(2)}, u32[]{:S(2)}) collective-permute-start(bf16[64,2304]{1,0:T(8,128)(2,1)S(1)} %get-tuple-element.39), channel_id=1, source_target_pairs={{0,32},{32,0},{1,33},{33,1},{2,34},{34,2},{3,35},{35,3},{4,36},{36... | collective-permute-start | bytes 884744 | tf_op jit(solution)/shard_map/ppermute | solution.py:346
  141.6 19.8 %copy-start.10 = (bf16[64,2304]{1,0:T(8,128)(2,1)}, bf16[64,2304]{1,0:T(8,128)(2,1)S(1)}, u32[]{:S(2)}) copy-start(bf16[64,2304]{1,0:T(8,128)(2,1)S(1)} %collective-permute-done.2.low_ref) | copy-start | bytes 884740
  141.6 19.8 %all-to-all-start.3 = ((bf16[16,32,1152]{2,1,0:T(8,128)(2,1)}), bf16[16,32,1152]{2,1,0:T(8,128)(2,1)S(1)}, u32[]{:S(2)}, u32[]{:S(2)}) async-start(bf16[16,32,1152]{2,1,0:T(8,128)(2,1)} %attend_own.3), calls=%async_computation.3 | async-start | bytes 2359296 | tf_op jit(solution)/shard_map/all_to_all | solution.py:386
  148.5 9.6 %collective-permute-start.3 = (bf16[64,2304]{1,0:T(8,128)(2,1)S(1)}, bf16[64,2304]{1,0:T(8,128)(2,1)S(1)}, u32[]{:S(2)}, u32[]{:S(2)}) collective-permute-start(bf16[64,2304]{1,0:T(8,128)(2,1)S(1)} %get-tuple-element.43), channel_id=1, source_target_pairs={{0,32},{32,0},{1,33},{33,1},{2,34},{34,2},{3,35},{35,3},{4,36},{36... | collective-permute-start | bytes 884744 | tf_op jit(solution)/shard_map/ppermute | solution.py:346
  158.0 3.3 %copy-start.11 = (bf16[64,2304]{1,0:T(8,128)(2,1)}, bf16[64,2304]{1,0:T(8,128)(2,1)S(1)}, u32[]{:S(2)}) copy-start(bf16[64,2304]{1,0:T(8,128)(2,1)S(1)} %collective-permute-done.3.high_ref) | copy-start | bytes 884740
  161.4 1.0 copy-start.7
  169.1 12.2 %collective-permute-start.4 = (bf16[128,2048]{1,0:T(8,128)(2,1)}, bf16[128,2048]{1,0:T(8,128)(2,1)S(1)}, u32[]{:S(2)}, u32[]{:S(2)}) collective-permute-start(bf16[128,2048]{1,0:T(8,128)(2,1)} %get-tuple-element.47), channel_id=1, source_target_pairs={{0,1},{1,0},{2,3},{3,2},{4,5},{5,4},{6,7},{7,6},{8,9},{9,8},{10,11... | collective-permute-start | bytes 1572872 | tf_op jit(solution)/shard_map/ppermute | solution.py:346
  176.1 5.2 %copy-start.9 = (bf16[128,2048]{1,0:T(8,128)(2,1)S(1)}, bf16[128,2048]{1,0:T(8,128)(2,1)}, u32[]{:S(2)}) copy-start(bf16[128,2048]{1,0:T(8,128)(2,1)} %get-tuple-element.46) | copy-start | bytes 1572868
  181.2 5.7 %collective-permute-start.7 = (bf16[128,2048]{1,0:T(8,128)(2,1)}, bf16[128,2048]{1,0:T(8,128)(2,1)S(1)}, u32[]{:S(2)}, u32[]{:S(2)}) collective-permute-start(bf16[128,2048]{1,0:T(8,128)(2,1)} %get-tuple-element.50), channel_id=1, source_target_pairs={{0,1},{1,0},{2,3},{3,2},{4,5},{5,4},{6,7},{7,6},{8,9},{9,8},{10,11... | collective-permute-start | bytes 1572872 | tf_op jit(solution)/shard_map/ppermute | solution.py:346
  181.4 11.7 %collective-permute-start.5 = (bf16[64,2048]{1,0:T(8,128)(2,1)S(1)}, bf16[64,2048]{1,0:T(8,128)(2,1)S(1)}, u32[]{:S(2)}, u32[]{:S(2)}) collective-permute-start(bf16[64,2048]{1,0:T(8,128)(2,1)S(1)} %get-tuple-element.54), channel_id=1, source_target_pairs={{0,2},{2,0},{4,6},{6,4},{1,3},{3,1},{5,7},{7,5},{8,10},{10,8},{12,... | collective-permute-start | bytes 786440 | tf_op jit(solution)/shard_map/ppermute | solution.py:346
  188.0 13.5 %collective-permute-start.8 = (bf16[64,2048]{1,0:T(8,128)(2,1)S(1)}, bf16[64,2048]{1,0:T(8,128)(2,1)S(1)}, u32[]{:S(2)}, u32[]{:S(2)}) collective-permute-start(bf16[64,2048]{1,0:T(8,128)(2,1)S(1)} %get-tuple-element.56), channel_id=1, source_target_pairs={{0,2},{2,0},{4,6},{6,4},{1,3},{3,1},{5,7},{7,5},{8,10},{10,8},{12,... | collective-permute-start | bytes 786440 | tf_op jit(solution)/shard_map/ppermute | solution.py:346
  193.2 8.5 %collective-permute-start.6 = (bf16[32,2048]{1,0:T(8,128)(2,1)S(1)}, bf16[32,2048]{1,0:T(8,128)(2,1)S(1)}, u32[]{:S(2)}, u32[]{:S(2)}) collective-permute-start(bf16[32,2048]{1,0:T(8,128)(2,1)S(1)} %add_convert_fusion.8), channel_id=1, source_target_pairs={{0,4},{2,6},{4,0},{6,2},{1,5},{3,7},{5,1},{7,3},{8,12},{10,14},{12... | collective-permute-start | bytes 393224 | tf_op jit(solution)/shard_map/ppermute | solution.py:346
  201.6 8.8 %collective-permute-start.9 = (bf16[32,2048]{1,0:T(8,128)(2,1)S(1)}, bf16[32,2048]{1,0:T(8,128)(2,1)S(1)}, u32[]{:S(2)}, u32[]{:S(2)}) collective-permute-start(bf16[32,2048]{1,0:T(8,128)(2,1)S(1)} %add_convert_fusion.5), channel_id=1, source_target_pairs={{0,4},{2,6},{4,0},{6,2},{1,5},{3,7},{5,1},{7,3},{8,12},{10,14},{12... | collective-permute-start | bytes 393224 | tf_op jit(solution)/shard_map/ppermute | solution.py:346

commit v5 on v3

--- a/solution.py
+++ b/solution.py
@@ -61,43 +61,44 @@
     )(ids_col, ids_row, queries)
 
 
-def place_kernel(pick_ref, pages_ref, out_ref):
-    def one(slot, carry):
-        src = pick_ref[slot]
-        out_ref[slot] = pages_ref[jnp.maximum(src, 0)]
-
-        @pl.when(src < 0)
-        def _():
-            out_ref[slot, :16, :] = jnp.full((16, HD), MARK, BF16)
-
-        return carry
-
-    lax.fori_loop(0, out_ref.shape[0], one, 0)
-
-
-def place(pick, pages, slots):
+def place_kernel(pick_ref, pages_ref, *out_refs):
+    for sub, out_ref in enumerate(out_refs):
+
+        def one(group, carry):
+            src = pick_ref[2 * group + sub]
+            out_ref[group] = pages_ref[jnp.maximum(src, 0)]
+
+            @pl.when(src < 0)
+            def _():
+                out_ref[group, :16, :] = jnp.full((16, HD), MARK, BF16)
+
+            return carry
+
+        lax.fori_loop(0, out_ref.shape[0], one, 0)
+
+
+def place(pick, pages, plane):
     whole = pl.BlockSpec(memory_space=pltpu.VMEM)
     return pl.pallas_call(
         place_kernel,
-        out_shape=jax.ShapeDtypeStruct((slots,) + pages.shape[1:], BF16),
+        out_shape=(jax.ShapeDtypeStruct((plane,) + pages.shape[1:], BF16),) * 2,
         in_specs=[pl.BlockSpec(memory_space=pltpu.SMEM), whole],
-        out_specs=whole,
+        out_specs=(whole, whole),
         compiler_params=pltpu.CompilerParams(vmem_limit_bytes=32 * 2**20),
         cost_estimate=pl.CostEstimate(flops=0, bytes_accessed=6 * 2**20, transcendentals=0),
         name="place",
     )(pick, pages)
 
 
-def attend_kernel(width, q_ref, kv_ref, out_ref, list_ref, key_ref, value_ref, s_ref, acc_ref):
-    sub = pl.program_id(0)
-    peers, span = kv_ref.shape[0], kv_ref.shape[1] // 4
+def attend_kernel(width, q_ref, kv_ref, *refs):
+    out_ref, list_ref, key_ref, value_ref, s_ref, acc_ref = refs[-6:]
+    peers, span = kv_ref.shape[0], kv_ref.shape[1] // 2
     group, cap = q_ref.shape[0], q_ref.shape[1]
-    key_at = pl.multiple_of(sub * 2 * span, 2 * span)
-
-    @pl.when(pl.program_id(1) == 0)
+
+    @pl.when(pl.program_id(0) == 0)
     def _():
         there = [
-            (jnp.max(kv_ref[src, pl.ds(key_at, 16), :].astype(F32)) < MARK / 2).astype(jnp.int32)
+            (jnp.max(kv_ref[src, :16, :].astype(F32)) < MARK / 2).astype(jnp.int32)
             for src in range(peers)
         ]
         count = jnp.int32(0)
@@ -112,8 +113,8 @@
             src = list_ref[n]
             at = pl.multiple_of(n * span, span)
             weight = jnp.where(n < count, 1.0, 0.0).astype(BF16)
-            key_ref[pl.ds(at, span), :] = kv_ref[src, pl.ds(key_at, span), :]
-            value_ref[pl.ds(at, span), :HD] = kv_ref[src, pl.ds(key_at + span, span), :] * weight
+            key_ref[pl.ds(at, span), :] = kv_ref[src, :span, :]
+            value_ref[pl.ds(at, span), :HD] = kv_ref[src, span:, :] * weight
             value_ref[pl.ds(at, span), HD:] = jnp.full((span, HD), 1.0, BF16) * weight
             return carry
 
@@ -173,20 +174,22 @@
         out_ref[j, :, width:] = jnp.where(lane < 24, part, 0.0).astype(BF16)
 
 
-def attend(q, kv, name):
+def attend(q, kv, name, sub, begun=None):
     peers, rows, width = q.shape
     group = 8
-    span = kv.shape[1] // 4
+    span = kv.shape[1] // 2
     m = group * CAP * G
     return pl.pallas_call(
         functools.partial(attend_kernel, width),
-        grid=(2, peers // group),
+        grid=(peers // group,),
         out_shape=jax.ShapeDtypeStruct((peers, rows, width + HD), BF16),
         in_specs=[
-            pl.BlockSpec((group, CAP, width), lambda s, i: (i, s, 0)),
+            pl.BlockSpec((group, CAP, width), lambda i: (i, sub, 0)),
             pl.BlockSpec(memory_space=pltpu.VMEM),
-        ],
-        out_specs=pl.BlockSpec((group, CAP, width + HD), lambda s, i: (i, s, 0)),
+        ]
+        + [pl.BlockSpec(memory_space=pl.ANY)] * (begun is not None),
+        out_specs=pl.BlockSpec((group, CAP, width + HD), lambda i: (i, sub, 0)),
+        input_output_aliases={} if begun is None else {2: 0},
         scratch_shapes=[
             pltpu.SMEM((peers + 2,), jnp.int32),
             pltpu.VMEM((peers * span, HD), BF16),
@@ -194,30 +197,36 @@
             pltpu.VMEM((m, peers * span), F32),
             pltpu.VMEM((m, 2 * HD), F32),
         ],
-        compiler_params=pltpu.CompilerParams(vmem_limit_bytes=48 * 2**20),
+        compiler_params=pltpu.CompilerParams(vmem_limit_bytes=32 * 2**20),
         cost_estimate=pl.CostEstimate(
-            flops=4 * peers * rows * G * 8 * span * HD,
-            bytes_accessed=6 * 2**20,
-            transcendentals=peers * rows * G * 8 * span,
+            flops=4 * peers * CAP * G * peers * span * HD,
+            bytes_accessed=32 * 2**20,
+            transcendentals=peers * CAP * G * peers * span,
         ),
         name=name,
-    )(q, kv)
-
-
-def collect_kernel(col_ref, row_ref, replies_ref, out_ref):
+    )(*((q, kv) if begun is None else (q, kv, begun)))
+
+
+def half_rows(rows, part):
+    step = rows.shape[0] // 8
+    half = step // 2
+    return jnp.concatenate([rows[b * step + part * half : b * step + (part + 1) * half] for b in range(8)], axis=0)
+
+
+def collect_kernel(col_ref, row_ref, replies_ref, low_ref, high_ref):
     slot = slots_as_col(col_ref[...], row_ref[...])
-    n, width = slot.shape[0], replies_ref.shape[1]
+    n = slot.shape[0]
     pick = jnp.where(lax.broadcasted_iota(jnp.int32, (n, replies_ref.shape[0]), 1) == slot, 1.0, 0.0)
     rows = jnp.dot(pick.astype(BF16), replies_ref[...], preferred_element_type=F32).astype(BF16)
-    out_ref[:, :width] = rows[: n // 2]
-    out_ref[:, width:] = rows[n // 2 :]
+    low_ref[...] = half_rows(rows, 0)
+    high_ref[...] = half_rows(rows, 1)
 
 
 def collect(ids_col, ids_row, replies):
     n = ids_col.shape[0]
     return pl.pallas_call(
         collect_kernel,
-        out_shape=jax.ShapeDtypeStruct((n // 2, 2 * replies.shape[1]), BF16),
+        out_shape=(jax.ShapeDtypeStruct((n // 2, replies.shape[1]), BF16),) * 2,
         compiler_params=pltpu.CompilerParams(vmem_limit_bytes=32 * 2**20),
         cost_estimate=pl.CostEstimate(
             flops=2 * n * replies.shape[0] * replies.shape[1], bytes_accessed=2**21, transcendentals=0
@@ -226,7 +235,7 @@
     )(ids_col, ids_row, replies)
 
 
-def merge_kernel(me_ref, col_ref, row_ref, own_ref, far_ref, suf_ref, suf_lse_ref, w_ref, send_ref, keep_ref, att_ref, w_buf, sem):
+def merge_kernel(part, me_ref, col_ref, row_ref, own_ref, far_ref, suf_ref, suf_lse_ref, w_ref, send_ref, keep_ref, att_ref, w_buf, sem):
     tile = w_ref.shape[1] // sem.shape[0]
     fetches = [
         pltpu.make_async_copy(
@@ -239,22 +248,23 @@
     n, width = suf_ref.shape
     slot = slots_as_col(col_ref[...], row_ref[...])
     pick = jnp.where(lax.broadcasted_iota(jnp.int32, (n, own_ref.shape[0]), 1) == slot, 1.0, 0.0)
-    own = jnp.dot(pick.astype(BF16), own_ref[...], preferred_element_type=F32)
-    far = jnp.concatenate([far_ref[:, : width + HD], far_ref[:, width + HD :]], axis=0)
+    pick = half_rows(pick.astype(BF16), part)
+    own = jnp.dot(pick, own_ref[...], preferred_element_type=F32)
+    far = far_ref[...]
     i = lax.broadcasted_iota(jnp.int32, (HD, width), 0)
     c = lax.broadcasted_iota(jnp.int32, (HD, width), 1)
     spread = jnp.where((i < 24) & ((i & 7) == (c >> 7)), 1.0, 0.0).astype(BF16)
     own_lse = jnp.dot(own[:, width:].astype(BF16), spread, preferred_element_type=F32)
     far_lse = jnp.dot(far[:, width:], spread, preferred_element_type=F32)
-    suf_lse = suf_lse_ref[...]
+    suf_lse = half_rows(suf_lse_ref, part)
     top = jnp.maximum(jnp.maximum(own_lse, far_lse), suf_lse)
     a = jnp.exp(own_lse - top)
     b = jnp.exp(far_lse - top)
     s = jnp.exp(suf_lse - top)
-    att = (a * own[:, :width] + b * far[:, :width].astype(F32) + s * suf_ref[...]) / (a + b + s)
-    att_ref[0] = att.astype(BF16)
+    att = a * own[:, :width] + b * far[:, :width].astype(F32) + s * half_rows(suf_ref, part)
+    att_ref[0] = (att / (a + b + s)).astype(BF16)
     me = me_ref[0]
-    step = n // 8
+    step = att_ref.shape[1] // 8
     for q in range(8):
         flip = (1 - q // 4) + 2 * (1 - (q // 2) % 2) + 4 * (1 - q % 2)
         at = pl.multiple_of((me ^ flip) * step, step)
@@ -269,26 +279,26 @@
         keep_ref[:, t * tile : (t + 1) * tile] = out[half:]
 
 
-def merge_project(me, ids_col, ids_row, own, far, suf, suf_lse, weight):
+def merge_project(part, me, ids_col, ids_row, own, far, suf, suf_lse, weight):
     n, width = suf.shape
     columns = weight.shape[1]
     whole = pl.BlockSpec(memory_space=pltpu.VMEM)
-    shape = jax.ShapeDtypeStruct((n // 2, columns), BF16)
+    shape = jax.ShapeDtypeStruct((n // 4, columns), BF16)
     return pl.pallas_call(
-        merge_kernel,
+        functools.partial(merge_kernel, part),
         out_shape=(shape, shape),
         in_specs=[pl.BlockSpec(memory_space=pltpu.SMEM)]
         + [whole] * 6
         + [pl.BlockSpec(memory_space=pl.ANY)],
         out_specs=(whole, whole),
         scratch_shapes=[
-            pltpu.VMEM((2, n, width), BF16),
-            pltpu.VMEM(weight.shape, BF16),
+            pltpu.VMEM((2, n // 2, width), BF16),
+            pltpu.VMEM((width, columns), BF16),
             pltpu.SemaphoreType.DMA((8,)),
         ],
-        compiler_params=pltpu.CompilerParams(vmem_limit_bytes=48 * 2**20),
+        compiler_params=pltpu.CompilerParams(vmem_limit_bytes=56 * 2**20),
         cost_estimate=pl.CostEstimate(
-            flops=2 * n * width * columns, bytes_accessed=16 * 2**20, transcendentals=3 * n * width
+            flops=8 * n * width * columns, bytes_accessed=24 * 2**20, transcendentals=2 * n * width
         ),
         name="merge_project",
     )(me, ids_col, ids_row, own, far, suf, suf_lse, weight)
@@ -336,39 +346,47 @@
     pick = jnp.sum(jnp.where(here, jnp.arange(pairs, dtype=jnp.int32)[None, :] + 1, 0), axis=1) - 1
     paired = jnp.swapaxes(prefill_pages.reshape(pairs, 2 * page, 2, HD), 1, 2)
     paired = paired.reshape(pairs, 4 * page, HD)
-    placed = place(pick, paired, 2 * plane).reshape(plane, 8 * page, HD)
-    placed, own_q, far_row, later = lax.optimization_barrier((placed, own_q, far_row, queries))
+    first, second = place(pick, paired, plane)
+    first, second, own_q, far_row = lax.optimization_barrier((first, second, own_q, far_row))
     far_col = far_row.reshape(seq, 1)
-    kv = lax.all_to_all(placed, PLANE, 0, 0, tiled=True)
     far_q = swap(own_q, "zh", 1)
-
+    first = lax.all_to_all(first, PLANE, 0, 0, tiled=True)
+    first, second = lax.optimization_barrier((first, second))
+    second = lax.all_to_all(second, PLANE, 0, 0, tiled=True)
+    own_out = attend(own_q, first, "attend_own", 0)
+    own_out, later, suffix_cache = lax.optimization_barrier((own_out, queries, suffix_cache))
     suf, suf_lse = suffix_attend(later, suffix_cache, suffix_len)
-    far_q, suf, suf_lse = lax.optimization_barrier((far_q, suf, suf_lse))
-
-    far_out = attend(far_q, kv, "attend_far")
+    far_q, own_out, suf, suf_lse = lax.optimization_barrier((far_q, own_out, suf, suf_lse))
+    far_out = attend(far_q, first, "attend_far", 0)
+    far_out = attend(far_q, second, "attend_far", 1, far_out)
     far_out, own_q = lax.optimization_barrier((far_out, own_q))
     far_back = lax.all_to_all(far_out, PLANE, 0, 0, tiled=True)
-    own_out = attend(own_q, kv, "attend_own")
+    own_out = attend(own_q, second, "attend_own", 1, own_out)
     far_back, own_out = lax.optimization_barrier((far_back, own_out))
+    far_part = collect(far_col, far_row, far_back.reshape(plane * 2 * CAP, width + HD))
+    far_part, own_out = lax.optimization_barrier((far_part, own_out))
+    far_low = swap(far_part[0], "zh", 1)
+    far_high = swap(far_part[1], "zh", 1)
     own_back = lax.all_to_all(own_out, PLANE, 0, 0, tiled=True)
-    far_part = collect(far_col, far_row, far_back.reshape(plane * 2 * CAP, width + HD))
-    far_part = swap(far_part, "zh", 1)
 
     me = (lax.axis_index("zl") * 2 + lax.axis_index("core")).astype(jnp.int32).reshape(1)
-    send, keep = merge_project(
-        me, ids_col, ids_row, own_back.reshape(plane * 2 * CAP, width + HD), far_part, suf, suf_lse, out_weight
-    )
+    own_back = own_back.reshape(plane * 2 * CAP, width + HD)
+    halves = [
+        merge_project(part, me, ids_col, ids_row, own_back, far, suf, suf_lse, out_weight)
+        for part, far in enumerate((far_low, far_high))
+    ]
 
     def add(a, b):
         return (a.astype(F32) + b.astype(F32)).astype(BF16)
 
-    got = swap(send, "core", 1)
-    half = seq // 4
-    send, keep = add(keep[:half], got[:half]), add(keep[half:], got[half:])
-    got = swap(send, "zl", 1)
-    half = seq // 8
-    send, keep = add(keep[:half], got[:half]), add(keep[half:], got[half:])
-    return add(keep, swap(send, "zl", 2))
+    def fold(send, keep, axis, bit):
+        got = swap(send, axis, bit)
+        half = keep.shape[0] // 2
+        return add(keep[:half], got[:half]), add(keep[half:], got[half:])
+
+    halves = [fold(send, keep, "core", 1) for send, keep in halves]
+    halves = [fold(send, keep, "zl", 1) for send, keep in halves]
+    return jnp.concatenate([add(keep, swap(send, "zl", 2)) for send, keep in halves], axis=0)
 
 
 def solution(mesh):

time: 218 us -> 201 us (0.922)
  waiting for transfers between devices: 69.6 us -> 52.7 us
  starting transfers between devices: 83.9 us -> 71.8 us
  Pallas kernels: 43.4 us -> 53 us
    ppermute x6 -> x10, waiting for transfers between devices: 56.8 us -> 22.3 us  [swap(): return lax.ppermute(value, axis, [(i, i ^ bit) for i in range(size)])]
    all_to_all x1 -> x2, waiting for transfers between devices: 9.77 us -> 21.3 us  [the longest x1 18.2 us: local(): first = lax.all_to_all(first, PLANE, 0, 0, tiled=True)]
    pallas_call x5 -> x8, Pallas kernels: 41.9 us -> 51.5 us  [the longest x4 34.3 us: attend(): pl.pallas_call(functools.partial(attend_kernel, width), grid=(peers // gr...]
    all_to_all x1, starting transfers between devices: 13.3 us -> 5.31 us  [local(): own_back = lax.all_to_all(own_out, PLANE, 0, 0, tiled=True)]
    unnamed x22 -> x48, local copies, waits for them, and re-layouts: 7.84 us -> 14.6 us
    all_to_all x1, starting transfers between devices: 13.7 us -> 7.56 us  [local(): far_back = lax.all_to_all(far_out, PLANE, 0, 0, tiled=True)]
    slice x1 -> x0, local copies, waits for them, and re-layouts: 5.71 us -> none  [suffix_attend(): suffix_cache[:, :, 0]]
    all_to_all x1 -> x2, starting transfers between devices: 4.67 us -> 10.4 us  [the longest x1 6.25 us: local(): second = lax.all_to_all(second, PLANE, 0, 0, tiled=True)]
  transfers between devices with their start and end apart: 10 -> 15, of which waited for: 7 -> 9; matrix products, arithmetic and copies ran while one was open for 6% -> 4% of each run, Pallas kernels for 9% -> 20%
where the time goes in v5:
time: 201 us
  starting transfers between devices  71.8 us (36%)
  Pallas kernels  53 us (26%)
  waiting for transfers between devices  52.7 us (26%)
  local copies, waits for them, and re-layouts  17.7 us (9%)
  other arithmetic  3.14 us (2%)
    ppermute x10, starting transfers between devices, swap(): return lax.ppermute(value, axis, [(i, i ^ bit) for i in range(size)])  41 us
    pallas_call x4, Pallas kernels, attend(): pl.pallas_call(functools.partial(attend_kernel, width), grid=(peers // gr...  34.3 us
    ppermute x10, waiting for transfers between devices, swap(): return lax.ppermute(value, axis, [(i, i ^ bit) for i in range(size)])  22.3 us
    all_to_all x1, waiting for transfers between devices, local(): first = lax.all_to_all(first, PLANE, 0, 0, tiled=True)  18.2 us
    unnamed x48, local copies, waits for them, and re-layouts  14.6 us
    pallas_call x2, Pallas kernels, merge_project(): pl.pallas_call(functools.partial(merge_kernel, part), out_shape=(shape, s...  13.8 us
    all_to_all x1, starting transfers between devices, local(): own_q = lax.all_to_all(sent, PLANE, 0, 0, tiled=True)  7.58 us
    all_to_all x1, starting transfers between devices, local(): far_back = lax.all_to_all(far_out, PLANE, 0, 0, tiled=True)  7.56 us
  transfers between devices with their start and end apart: 15, of which 9 were waited for; matrix products, arithmetic and copies ran while one was open for 4% of the time, Pallas kernels for 20%

profile of v5, /device:TPU:1, one launch (start us, length us, event | category | flops | bytes accessed | tf_op | source)
XLA Modules:
  0.0 200.7 jit_solution(2059467082812933019)
XLA Ops:
  0.0 0.9 copy.28.col_ref
  0.9 1.1 copy-done
  2.7 1.5 dispatch.1
  4.2 7.6 %all-to-all-start = ((bf16[16,32,1024]{2,1,0:T(8,128)(2,1)}), bf16[16,32,1024]{2,1,0:T(8,128)(2,1)S(1)}, u32[]{:S(2)}, u32[]{:S(2)}) async-start(bf16[16,32,1024]{2,1,0:T(8,128)(2,1)} %bitcast.6), calls=%async_computation | async-start | bytes 2097152 | tf_op jit(solution)/shard_map/all_to_all | solution.py:341
  11.8 7.0 %collective-permute-start = (s32[1,256]{1,0:T(1,128)S(1)}, s32[1,256]{1,0:T(1,128)S(1)}, u32[]{:S(2)}, u32[]{:S(2)}) collective-permute-start(s32[1,256]{1,0:T(1,128)S(1)} %bitcast.35), channel_id=1, source_target_pairs={{0,32},{32,0},{1,33},{33,1},{2,34},{34,2},{3,35},{35,3},{4,36},{36... | collective-permute-start | bytes 3080 | tf_op jit(solution)/shard_map/ppermute | solution.py:329
  19.6 2.6 %place.1 = (bf16[16,512,128]{2,1,0:T(8,128)(2,1)S(1)}, bf16[16,512,128]{2,1,0:T(8,128)(2,1)}) custom-call(s32[32]{0:T(128)S(1)} %broadcast_add_fusion.pick_ref, bf16[16,512,128]{2,1,0:T(8,128)(2,1)S(1)} %bitcast.29), custom_call_target="tpu_custom_call" | custom-call | bytes 6291456 | tf_op jit(solution)/shard_map/place/pallas_call | solution.py:82
  22.2 1.3 copy-done.5
  23.5 3.8 %all-to-all-done.q_ref = bf16[16,32,1024]{2,1,0:T(8,128)(2,1)S(1)} async-done(((bf16[16,32,1024]{2,1,0:T(8,128)(2,1)}), bf16[16,32,1024]{2,1,0:T(8,128)(2,1)S(1)}, u32[]{:S(2)}, u32[]{:S(2)}) %all-to-all-start) | async-done | bytes 1048608 | tf_op jit(solution)/shard_map/all_to_all | solution.py:341
  27.3 4.1 %all-to-all-start.1 = ((bf16[16,512,128]{2,1,0:T(8,128)(2,1)}), bf16[16,512,128]{2,1,0:T(8,128)(2,1)S(1)}, u32[]{:S(2)}, u32[]{:S(2)}) async-start(bf16[16,512,128]{2,1,0:T(8,128)(2,1)} %copy-done.5), calls=%async_computation.1 | async-start | bytes 4194304 | tf_op jit(solution)/shard_map/all_to_all | solution.py:353
  31.5 7.0 %collective-permute-start.1 = (bf16[16,32,1024]{2,1,0:T(8,128)(2,1)S(1)}, bf16[16,32,1024]{2,1,0:T(8,128)(2,1)}, u32[]{:S(2)}, u32[]{:S(2)}) collective-permute-start(bf16[16,32,1024]{2,1,0:T(8,128)(2,1)S(1)} %all-to-all-done.q_ref), channel_id=1, source_target_pairs={{0,32},{32,0},{1,33},{33,1},{2,34},{34,2},{3,35},{35,3},{4,36},{36... | collective-permute-start | bytes 3145736 | tf_op jit(solution)/shard_map/ppermute | solution.py:329
  38.5 18.2 %all-to-all-done.1.kv_ref = bf16[16,512,128]{2,1,0:T(8,128)(2,1)S(1)} async-done(((bf16[16,512,128]{2,1,0:T(8,128)(2,1)}), bf16[16,512,128]{2,1,0:T(8,128)(2,1)S(1)}, u32[]{:S(2)}, u32[]{:S(2)}) %all-to-all-start.1) | async-done | bytes 2097184 | tf_op jit(solution)/shard_map/all_to_all | solution.py:353
  56.8 1.3 copy-done.2
  58.1 6.2 %all-to-all-start.2 = ((bf16[16,512,128]{2,1,0:T(8,128)(2,1)}), bf16[16,512,128]{2,1,0:T(8,128)(2,1)S(1)}, u32[]{:S(2)}, u32[]{:S(2)}) async-start(bf16[16,512,128]{2,1,0:T(8,128)(2,1)} %get-tuple-element.44), calls=%async_computation.2 | async-start | bytes 4194304 | tf_op jit(solution)/shard_map/all_to_all | solution.py:355
  64.4 1.6 copy-done.3
  66.0 6.6 %attend_own.2.refs_0_ = bf16[16,32,1152]{2,1,0:T(8,128)(2,1)S(1)} custom-call(bf16[16,32,1024]{2,1,0:T(8,128)(2,1)S(1)} %all-to-all-done.q_ref, bf16[16,512,128]{2,1,0:T(8,128)(2,1)S(1)} %copy-done.3), custom_call_target="tpu_custom_call" | custom-call | flops 4294967296 | bytes 33554432 | tf_op jit(solution)/shard_map/attend_own/pallas_call | solution.py:182
  72.9 0.8 copy-done.6
  74.1 0.7 fusion.9
  74.8 0.7 fusion.1
  75.6 1.2 convolution_divide_fusion
  77.1 1.8 copy_bitcast_fusion
  79.1 7.5 %attend_far.2.refs_0_ = bf16[16,32,1152]{2,1,0:T(8,128)(2,1)S(1)} custom-call(bf16[16,32,1024]{2,1,0:T(8,128)(2,1)} %collective-permute-done.1.q_ref, bf16[16,512,128]{2,1,0:T(8,128)(2,1)S(1)} %copy-done.4), custom_call_target="tpu_custom_call" | custom-call | flops 4294967296 | bytes 33554432 | tf_op jit(solution)/shard_map/attend_far/pallas_call | solution.py:182
  86.5 3.1 %all-to-all-done.2.kv_ref = bf16[16,512,128]{2,1,0:T(8,128)(2,1)S(1)} async-done(((bf16[16,512,128]{2,1,0:T(8,128)(2,1)}), bf16[16,512,128]{2,1,0:T(8,128)(2,1)S(1)}, u32[]{:S(2)}, u32[]{:S(2)}) %all-to-all-start.2) | async-done | bytes 2097184 | tf_op jit(solution)/shard_map/all_to_all | solution.py:355
  89.7 10.6 %attend_far.3 = bf16[16,32,1152]{2,1,0:T(8,128)(2,1)S(1)} custom-call(bf16[16,32,1024]{2,1,0:T(8,128)(2,1)} %collective-permute-done.1.q_ref, bf16[16,512,128]{2,1,0:T(8,128)(2,1)S(1)} %all-to-all-done.2.kv_ref, bf16[16,32,1152]{2,1,0:T(8,128)(2,1)S(1)} %attend_far.2.refs_0_), custom_call_target="tpu_custom_call", output_to_operand_aliasing={{}: (2, {})} | custom-call | flops 4294967296 | bytes 33554432 | tf_op jit(solution)/shard_map/attend_far/pallas_call | solution.py:182
  100.2 1.0 copy-done.9
  101.2 7.6 %all-to-all-start.3 = ((bf16[16,32,1152]{2,1,0:T(8,128)(2,1)}), bf16[16,32,1152]{2,1,0:T(8,128)(2,1)S(1)}, u32[]{:S(2)}, u32[]{:S(2)}) async-start(bf16[16,32,1152]{2,1,0:T(8,128)(2,1)} %copy-done.9), calls=%async_computation.3 | async-start | bytes 2359296 | tf_op jit(solution)/shard_map/all_to_all | solution.py:363
  109.0 1.3 copy-done.7
  110.2 1.2 copy-done.11
  111.4 9.7 %attend_own.3 = bf16[16,32,1152]{2,1,0:T(8,128)(2,1)S(1)} custom-call(bf16[16,32,1024]{2,1,0:T(8,128)(2,1)S(1)} %copy-done.11, bf16[16,512,128]{2,1,0:T(8,128)(2,1)S(1)} %all-to-all-done.2.kv_ref, bf16[16,32,1152]{2,1,0:T(8,128)(2,1)S(1)} %copy-done.7), custom_call_target="tpu_custom_call", output_to_operand_aliasing={{}: (2, {})} | custom-call | flops 4294967296 | bytes 33554432 | tf_op jit(solution)/shard_map/attend_own/pallas_call | solution.py:182
  121.1 1.0 copy-done.8
  122.2 2.0 all-to-all-done.3
  124.2 0.8 collect.1
  125.0 5.3 %all-to-all-start.4 = ((bf16[16,32,1152]{2,1,0:T(8,128)(2,1)}), bf16[16,32,1152]{2,1,0:T(8,128)(2,1)S(1)}, u32[]{:S(2)}, u32[]{:S(2)}) async-start(bf16[16,32,1152]{2,1,0:T(8,128)(2,1)} %copy-done.8), calls=%async_computation.4 | async-start | bytes 2359296 | tf_op jit(solution)/shard_map/all_to_all | solution.py:370
  130.3 7.9 %collective-permute-start.2 = (bf16[128,1152]{1,0:T(8,128)(2,1)S(1)}, bf16[128,1152]{1,0:T(8,128)(2,1)S(1)}, u32[]{:S(2)}, u32[]{:S(2)}) collective-permute-start(bf16[128,1152]{1,0:T(8,128)(2,1)S(1)} %get-tuple-element.53), channel_id=1, source_target_pairs={{0,32},{32,0},{1,33},{33,1},{2,34},{34,2},{3,35},{35,3},{4,36},{36... | collective-permute-start | bytes 884744 | tf_op jit(solution)/shard_map/ppermute | solution.py:329
  138.3 4.3 %collective-permute-done.2.far_ref = bf16[128,1152]{1,0:T(8,128)(2,1)S(1)} collective-permute-done((bf16[128,1152]{1,0:T(8,128)(2,1)S(1)}, bf16[128,1152]{1,0:T(8,128)(2,1)S(1)}, u32[]{:S(2)}, u32[]{:S(2)}) %collective-permute-start.2) | collective-permute-done | bytes 294944 | tf_op jit(solution)/shard_map/ppermute | solution.py:329
  142.6 3.2 %all-to-all-done.4 = bf16[16,32,1152]{2,1,0:T(8,128)(2,1)S(1)} async-done(((bf16[16,32,1152]{2,1,0:T(8,128)(2,1)}), bf16[16,32,1152]{2,1,0:T(8,128)(2,1)S(1)}, u32[]{:S(2)}, u32[]{:S(2)}) %all-to-all-start.4) | async-done | bytes 1179680 | tf_op jit(solution)/shard_map/all_to_all | solution.py:370
  145.8 1.0 copy-done.17
  146.9 6.9 %merge_project.2 = (bf16[64,4096]{1,0:T(8,128)(2,1)}, bf16[64,4096]{1,0:T(8,128)(2,1)}) custom-call(s32[1]{0:T(128)} %bitcast.me_ref, s32[256,1]{1,0:T(8,128)} %copy-done.12, s32[1,256]{1,0:T(1,128)} %bitcast.32, bf16[512,1152]{1,0:T(8,128)(2,1)} %bitcast.40, bf16[128,1152]{1,0:T(8,128)(2,1)} %copy-done.20, f32[256,1024]{1,0:T(8,128)} %get-tuple-element.54.suf_ref, ...), custom_call_target="tpu_custom_call" | custom-call | flops 8589934592 | bytes 25165824 | tf_op jit(solution)/shard_map/merge_project/pallas_call | solution.py:287
  153.8 5.7 %collective-permute-start.3 = (bf16[64,4096]{1,0:T(8,128)(2,1)}, bf16[64,4096]{1,0:T(8,128)(2,1)S(1)}, u32[]{:S(2)}, u32[]{:S(2)}) collective-permute-start(bf16[64,4096]{1,0:T(8,128)(2,1)} %get-tuple-element.57), channel_id=1, source_target_pairs={{0,1},{1,0},{2,3},{3,2},{4,5},{5,4},{6,7},{7,6},{8,9},{9,8},{10,11... | collective-permute-start | bytes 1572872 | tf_op jit(solution)/shard_map/ppermute | solution.py:329
  159.5 0.7 copy-done.21
  160.3 6.9 %merge_project.3 = (bf16[64,4096]{1,0:T(8,128)(2,1)}, bf16[64,4096]{1,0:T(8,128)(2,1)}) custom-call(s32[1]{0:T(128)} %bitcast.me_ref, s32[256,1]{1,0:T(8,128)} %copy-done.12, s32[1,256]{1,0:T(1,128)} %bitcast.33, bf16[512,1152]{1,0:T(8,128)(2,1)} %bitcast.41, bf16[128,1152]{1,0:T(8,128)(2,1)} %copy-done.21, f32[256,1024]{1,0:T(8,128)} %get-tuple-element.54.suf_ref, ...), custom_call_target="tpu_custom_call" | custom-call | flops 8589934592 | bytes 25165824 | tf_op jit(solution)/shard_map/merge_project/pallas_call | solution.py:287
  167.4 9.6 %collective-permute-start.4 = (bf16[32,4096]{1,0:T(8,128)(2,1)S(1)}, bf16[32,4096]{1,0:T(8,128)(2,1)S(1)}, u32[]{:S(2)}, u32[]{:S(2)}) collective-permute-start(bf16[32,4096]{1,0:T(8,128)(2,1)S(1)} %get-tuple-element.62), channel_id=1, source_target_pairs={{0,2},{2,0},{4,6},{6,4},{1,3},{3,1},{5,7},{7,5},{8,10},{10,8},{12,... | collective-permute-start | bytes 786440 | tf_op jit(solution)/shard_map/ppermute | solution.py:329
  177.0 1.2 add_convert_fusion.1
  178.2 2.0 collective-permute-start.8
  180.2 3.1 %collective-permute-done.4 = bf16[32,4096]{1,0:T(8,128)(2,1)S(1)} collective-permute-done((bf16[32,4096]{1,0:T(8,128)(2,1)S(1)}, bf16[32,4096]{1,0:T(8,128)(2,1)S(1)}, u32[]{:S(2)}, u32[]{:S(2)}) %collective-permute-start.4) | collective-permute-done | bytes 262176 | tf_op jit(solution)/shard_map/ppermute | solution.py:329
  183.3 1.5 collective-permute-start.5
  184.8 6.9 %collective-permute-done.8 = bf16[32,4096]{1,0:T(8,128)(2,1)S(1)} collective-permute-done((bf16[32,4096]{1,0:T(8,128)(2,1)S(1)}, bf16[32,4096]{1,0:T(8,128)(2,1)S(1)}, u32[]{:S(2)}, u32[]{:S(2)}) %collective-permute-start.8) | collective-permute-done | bytes 262176 | tf_op jit(solution)/shard_map/ppermute | solution.py:329
  191.9 8.0 %collective-permute-done.9 = bf16[16,4096]{1,0:T(8,128)(2,1)S(1)} collective-permute-done((bf16[16,4096]{1,0:T(8,128)(2,1)S(1)}, bf16[16,4096]{1,0:T(8,128)(2,1)S(1)}, u32[]{:S(2)}, u32[]{:S(2)}) %collective-permute-start.9) | collective-permute-done | bytes 131104 | tf_op jit(solution)/shard_map/ppermute | solution.py:329
  200.0 0.7 pad_maximum_fusion
  (61 shorter events, 3.5 us)
Async XLA Ops:
  0.0 11.8 %copy-start.14 = (s32[256,1]{0,1:T(1,128)S(1)}, s32[256,1]{0,1:T(1,128)}, u32[]{:S(2)}) copy-start(s32[256,1]{0,1:T(1,128)} %param.12) | copy-start | bytes 3076
  0.0 18.8 %copy-start.22 = (s32[1,32]{1,0:T(1,128)S(1)}, s32[1,32]{1,0:T(1,128)}, u32[]{:S(2)}) copy-start(s32[1,32]{1,0:T(1,128)} %param.8) | copy-start | bytes 388
  0.9 18.7 %copy-start.12 = (s32[256,1]{1,0:T(8,128)}, s32[256,1]{1,0:T(8,128)S(1)}, u32[]{:S(2)}) copy-start(s32[256,1]{1,0:T(8,128)S(1)} %copy.28.col_ref) | copy-start | bytes 3076
  0.9 1.1 copy-start
  2.0 0.7 copy-start.13
  2.7 16.4 %copy-start.15 = (bf16[32,128,2,128]{3,2,1,0:T(2,128)(2,1)S(1)}, bf16[32,128,2,128]{3,2,1,0:T(2,128)(2,1)}, u32[]{:S(2)}) copy-start(bf16[32,128,2,128]{3,2,1,0:T(2,128)(2,1)} %param.7) | copy-start | bytes 6291460
  4.2 23.1 %all-to-all-start = ((bf16[16,32,1024]{2,1,0:T(8,128)(2,1)}), bf16[16,32,1024]{2,1,0:T(8,128)(2,1)S(1)}, u32[]{:S(2)}, u32[]{:S(2)}) async-start(bf16[16,32,1024]{2,1,0:T(8,128)(2,1)} %bitcast.6), calls=%async_computation | async-start | bytes 2097152 | tf_op jit(solution)/shard_map/all_to_all | solution.py:341
  11.8 11.7 %collective-permute-start = (s32[1,256]{1,0:T(1,128)S(1)}, s32[1,256]{1,0:T(1,128)S(1)}, u32[]{:S(2)}, u32[]{:S(2)}) collective-permute-start(s32[1,256]{1,0:T(1,128)S(1)} %bitcast.35), channel_id=1, source_target_pairs={{0,32},{32,0},{1,33},{33,1},{2,34},{34,2},{3,35},{35,3},{4,36},{36... | collective-permute-start | bytes 3080 | tf_op jit(solution)/shard_map/ppermute | solution.py:329
  22.1 1.3 copy-start.5
  27.3 37.0 %copy-start.10 = (bf16[16,32,1024]{2,1,0:T(8,128)(2,1)}, bf16[16,32,1024]{2,1,0:T(8,128)(2,1)S(1)}, u32[]{:S(2)}) copy-start(bf16[16,32,1024]{2,1,0:T(8,128)(2,1)S(1)} %all-to-all-done.q_ref) | copy-start | bytes 3145732
  27.3 4.1 %copy-start.19 = (s32[256]{0:T(256)S(1)}, s32[256]{0:T(256)}, u32[]{:S(2)}) copy-start(s32[256]{0:T(256)} %param.11) | copy-start | bytes 3076
  27.3 29.4 %all-to-all-start.1 = ((bf16[16,512,128]{2,1,0:T(8,128)(2,1)}), bf16[16,512,128]{2,1,0:T(8,128)(2,1)S(1)}, u32[]{:S(2)}, u32[]{:S(2)}) async-start(bf16[16,512,128]{2,1,0:T(8,128)(2,1)} %copy-done.5), calls=%async_computation.1 | async-start | bytes 4194304 | tf_op jit(solution)/shard_map/all_to_all | solution.py:353
  31.5 47.4 %collective-permute-start.1 = (bf16[16,32,1024]{2,1,0:T(8,128)(2,1)S(1)}, bf16[16,32,1024]{2,1,0:T(8,128)(2,1)}, u32[]{:S(2)}, u32[]{:S(2)}) collective-permute-start(bf16[16,32,1024]{2,1,0:T(8,128)(2,1)S(1)} %all-to-all-done.q_ref), channel_id=1, source_target_pairs={{0,32},{32,0},{1,33},{33,1},{2,34},{34,2},{3,35},{35,3},{4,36},{36... | collective-permute-start | bytes 3145736 | tf_op jit(solution)/shard_map/ppermute | solution.py:329
  56.8 1.3 copy-start.2
  58.1 31.6 %all-to-all-start.2 = ((bf16[16,512,128]{2,1,0:T(8,128)(2,1)}), bf16[16,512,128]{2,1,0:T(8,128)(2,1)S(1)}, u32[]{:S(2)}, u32[]{:S(2)}) async-start(bf16[16,512,128]{2,1,0:T(8,128)(2,1)} %get-tuple-element.44), calls=%async_computation.2 | async-start | bytes 4194304 | tf_op jit(solution)/shard_map/all_to_all | solution.py:355
  64.4 1.6 copy-start.3
  66.0 6.6 %copy-start.16 = (bf16[256,16,2,128]{3,2,1,0:T(2,128)(2,1)S(1)}, bf16[256,16,2,128]{3,2,1,0:T(2,128)(2,1)}, u32[]{:S(2)}) copy-start(bf16[256,16,2,128]{3,2,1,0:T(2,128)(2,1)} %param.10) | copy-start | bytes 6291460
  72.5 1.1 copy-start.6
  72.6 1.4 copy-start.1
  77.1 2.0 copy-start.4
  100.2 1.0 copy-start.9
  101.2 22.9 %all-to-all-start.3 = ((bf16[16,32,1152]{2,1,0:T(8,128)(2,1)}), bf16[16,32,1152]{2,1,0:T(8,128)(2,1)S(1)}, u32[]{:S(2)}, u32[]{:S(2)}) async-start(bf16[16,32,1152]{2,1,0:T(8,128)(2,1)} %copy-done.9), calls=%async_computation.3 | async-start | bytes 2359296 | tf_op jit(solution)/shard_map/all_to_all | solution.py:363
  108.9 1.3 copy-start.7
  110.2 1.2 copy-start.11
  121.1 1.0 copy-start.8
  125.0 20.8 %all-to-all-start.4 = ((bf16[16,32,1152]{2,1,0:T(8,128)(2,1)}), bf16[16,32,1152]{2,1,0:T(8,128)(2,1)S(1)}, u32[]{:S(2)}, u32[]{:S(2)}) async-start(bf16[16,32,1152]{2,1,0:T(8,128)(2,1)} %copy-done.8), calls=%async_computation.4 | async-start | bytes 2359296 | tf_op jit(solution)/shard_map/all_to_all | solution.py:370
  130.3 12.3 %collective-permute-start.2 = (bf16[128,1152]{1,0:T(8,128)(2,1)S(1)}, bf16[128,1152]{1,0:T(8,128)(2,1)S(1)}, u32[]{:S(2)}, u32[]{:S(2)}) collective-permute-start(bf16[128,1152]{1,0:T(8,128)(2,1)S(1)} %get-tuple-element.53), channel_id=1, source_target_pairs={{0,32},{32,0},{1,33},{33,1},{2,34},{34,2},{3,35},{35,3},{4,36},{36... | collective-permute-start | bytes 884744 | tf_op jit(solution)/shard_map/ppermute | solution.py:329
  138.2 21.3 %collective-permute-start.6 = (bf16[128,1152]{1,0:T(8,128)(2,1)S(1)}, bf16[128,1152]{1,0:T(8,128)(2,1)S(1)}, u32[]{:S(2)}, u32[]{:S(2)}) collective-permute-start(bf16[128,1152]{1,0:T(8,128)(2,1)S(1)} %get-tuple-element.58), channel_id=1, source_target_pairs={{0,32},{32,0},{1,33},{33,1},{2,34},{34,2},{3,35},{35,3},{4,36},{36... | collective-permute-start | bytes 884744 | tf_op jit(solution)/shard_map/ppermute | solution.py:329
  142.6 3.2 %copy-start.20 = (bf16[128,1152]{1,0:T(8,128)(2,1)}, bf16[128,1152]{1,0:T(8,128)(2,1)S(1)}, u32[]{:S(2)}) copy-start(bf16[128,1152]{1,0:T(8,128)(2,1)S(1)} %collective-permute-done.2.far_ref) | copy-start | bytes 884740
  145.8 1.0 copy-start.17
  153.8 13.5 %copy-start.18 = (bf16[64,4096]{1,0:T(8,128)(2,1)S(1)}, bf16[64,4096]{1,0:T(8,128)(2,1)}, u32[]{:S(2)}) copy-start(bf16[64,4096]{1,0:T(8,128)(2,1)} %get-tuple-element.56) | copy-start | bytes 1572868
  153.8 13.5 %collective-permute-start.3 = (bf16[64,4096]{1,0:T(8,128)(2,1)}, bf16[64,4096]{1,0:T(8,128)(2,1)S(1)}, u32[]{:S(2)}, u32[]{:S(2)}) collective-permute-start(bf16[64,4096]{1,0:T(8,128)(2,1)} %get-tuple-element.57), channel_id=1, source_target_pairs={{0,1},{1,0},{2,3},{3,2},{4,5},{5,4},{6,7},{7,6},{8,9},{9,8},{10,11... | collective-permute-start | bytes 1572872 | tf_op jit(solution)/shard_map/ppermute | solution.py:329
  159.5 0.7 copy-start.21
  167.2 9.9 %collective-permute-start.7 = (bf16[64,4096]{1,0:T(8,128)(2,1)}, bf16[64,4096]{1,0:T(8,128)(2,1)S(1)}, u32[]{:S(2)}, u32[]{:S(2)}) collective-permute-start(bf16[64,4096]{1,0:T(8,128)(2,1)} %get-tuple-element.60), channel_id=1, source_target_pairs={{0,1},{1,0},{2,3},{3,2},{4,5},{5,4},{6,7},{7,6},{8,9},{9,8},{10,11... | collective-permute-start | bytes 1572872 | tf_op jit(solution)/shard_map/ppermute | solution.py:329
  167.4 15.9 %collective-permute-start.4 = (bf16[32,4096]{1,0:T(8,128)(2,1)S(1)}, bf16[32,4096]{1,0:T(8,128)(2,1)S(1)}, u32[]{:S(2)}, u32[]{:S(2)}) collective-permute-start(bf16[32,4096]{1,0:T(8,128)(2,1)S(1)} %get-tuple-element.62), channel_id=1, source_target_pairs={{0,2},{2,0},{4,6},{6,4},{1,3},{3,1},{5,7},{7,5},{8,10},{10,8},{12,... | collective-permute-start | bytes 786440 | tf_op jit(solution)/shard_map/ppermute | solution.py:329
  178.2 13.5 %collective-permute-start.8 = (bf16[32,4096]{1,0:T(8,128)(2,1)S(1)}, bf16[32,4096]{1,0:T(8,128)(2,1)S(1)}, u32[]{:S(2)}, u32[]{:S(2)}) collective-permute-start(bf16[32,4096]{1,0:T(8,128)(2,1)S(1)} %get-tuple-element.64), channel_id=1, source_target_pairs={{0,2},{2,0},{4,6},{6,4},{1,3},{3,1},{5,7},{7,5},{8,10},{10,8},{12,... | collective-permute-start | bytes 786440 | tf_op jit(solution)/shard_map/ppermute | solution.py:329
  183.3 8.5 %collective-permute-start.5 = (bf16[16,4096]{1,0:T(8,128)(2,1)S(1)}, bf16[16,4096]{1,0:T(8,128)(2,1)S(1)}, u32[]{:S(2)}, u32[]{:S(2)}) collective-permute-start(bf16[16,4096]{1,0:T(8,128)(2,1)S(1)} %add_convert_fusion.8), channel_id=1, source_target_pairs={{0,4},{2,6},{4,0},{6,2},{1,5},{3,7},{5,1},{7,3},{8,12},{10,14},{12... | collective-permute-start | bytes 393224 | tf_op jit(solution)/shard_map/ppermute | solution.py:329
  191.8 8.2 %collective-permute-start.9 = (bf16[16,4096]{1,0:T(8,128)(2,1)S(1)}, bf16[16,4096]{1,0:T(8,128)(2,1)S(1)}, u32[]{:S(2)}, u32[]{:S(2)}) collective-permute-start(bf16[16,4096]{1,0:T(8,128)(2,1)S(1)} %add_convert_fusion.5), channel_id=1, source_target_pairs={{0,4},{2,6},{4,0},{6,2},{1,5},{3,7},{5,1},{7,3},{8,12},{10,14},{12... | collective-permute-start | bytes 393224 | tf_op jit(solution)/shard_map/ppermute | solution.py:329

commit v6 on v5

--- a/solution.py
+++ b/solution.py
@@ -24,15 +24,6 @@
     return (((ids >> 3) * 4 + (ids & 3)) * 2 + ((ids >> 2) & 1)) * CAP
 
 
-def slots_as_row(ids_col, ids_row):
-    n = ids_row.shape[1]
-    i = lax.broadcasted_iota(jnp.int32, (n, n), 0)
-    j = lax.broadcasted_iota(jnp.int32, (n, n), 1)
-    earlier = jnp.where((ids_col == ids_row) & (i < j), 1.0, 0.0)
-    rank = jnp.sum(earlier, axis=0, keepdims=True).astype(jnp.int32)
-    return slot_base(ids_row) + rank
-
-
 def slots_as_col(ids_col, ids_row):
     n = ids_row.shape[1]
     i = lax.broadcasted_iota(jnp.int32, (n, n), 0)
@@ -42,14 +33,21 @@
     return slot_base(ids_col) + rank
 
 
-def dispatch_kernel(col_ref, row_ref, q_ref, out_ref):
-    slot = slots_as_row(col_ref[...], row_ref[...])
-    rows, n = out_ref.shape[0], slot.shape[1]
+def dispatch_kernel(row_ref, q_ref, out_ref):
+    ids = row_ref[...]
+    rows, n = out_ref.shape[0], ids.shape[1]
+    named = lax.broadcasted_iota(jnp.int32, (rows // CAP, n), 0) == ids
+    i = lax.broadcasted_iota(jnp.int32, (n, n), 0)
+    j = lax.broadcasted_iota(jnp.int32, (n, n), 1)
+    ahead = jnp.where(i < j, 1.0, 0.0).astype(BF16)
+    earlier = jnp.dot(jnp.where(named, 1.0, 0.0).astype(BF16), ahead, preferred_element_type=F32)
+    rank = jnp.sum(jnp.where(named, earlier, 0.0), axis=0, keepdims=True).astype(jnp.int32)
+    slot = slot_base(ids) + rank
     pick = jnp.where(lax.broadcasted_iota(jnp.int32, (rows, n), 0) == slot, 1.0, 0.0)
     out_ref[...] = jnp.dot(pick.astype(BF16), q_ref[...], preferred_element_type=F32).astype(BF16)
 
 
-def dispatch(ids_col, ids_row, queries, rows):
+def dispatch(ids_row, queries, rows):
     return pl.pallas_call(
         dispatch_kernel,
         out_shape=jax.ShapeDtypeStruct((rows, queries.shape[1]), BF16),
@@ -58,7 +56,7 @@
             flops=2 * rows * queries.shape[0] * queries.shape[1], bytes_accessed=2**21, transcendentals=0
         ),
         name="dispatch",
-    )(ids_col, ids_row, queries)
+    )(ids_row, queries)
 
 
 def place_kernel(pick_ref, pages_ref, *out_refs):
@@ -337,7 +335,7 @@
     ids_col, ids_row = prefix_id, prefix_id.reshape(1, seq)
     far_row = swap(ids_row, "zh", 1)
 
-    sent = dispatch(ids_col, ids_row, queries, plane * 2 * CAP).reshape(plane, 2 * CAP, width)
+    sent = dispatch(ids_row, queries, plane * 2 * CAP).reshape(plane, 2 * CAP, width)
     own_q = lax.all_to_all(sent, PLANE, 0, 0, tiled=True)
 
     owner = page_owner[0, ::2]
@@ -379,14 +377,17 @@
     def add(a, b):
         return (a.astype(F32) + b.astype(F32)).astype(BF16)
 
-    def fold(send, keep, axis, bit):
-        got = swap(send, axis, bit)
-        half = keep.shape[0] // 2
-        return add(keep[:half], got[:half]), add(keep[half:], got[half:])
-
-    halves = [fold(send, keep, "core", 1) for send, keep in halves]
-    halves = [fold(send, keep, "zl", 1) for send, keep in halves]
-    return jnp.concatenate([add(keep, swap(send, "zl", 2)) for send, keep in halves], axis=0)
+    def spread(send, keep):
+        got = swap(send, "core", 1)
+        step = keep.shape[0] // 4
+        blocks = [add(keep[q * step : (q + 1) * step], got[q * step : (q + 1) * step]) for q in range(4)]
+        parts = [swap(blocks[q], "zl", bit) for q, bit in ((0, 3), (2, 2), (1, 1))]
+        total = blocks[3].astype(F32)
+        for part in parts:
+            total = total + part.astype(F32)
+        return total.astype(BF16)
+
+    return jnp.concatenate([spread(*half) for half in halves], axis=0)
 
 
 def solution(mesh):

time: 201 us -> 202 us (level); the launches traced: 201 us -> 199 us
  waiting for transfers between devices: 52.7 us -> 47.2 us
  starting transfers between devices: 71.8 us -> 76.7 us
    ppermute x10 -> x12, waiting for transfers between devices: 22.3 us -> 14.5 us  [swap(): return lax.ppermute(value, axis, [(i, i ^ bit) for i in range(size)])]
    all_to_all x1, starting transfers between devices: 7.56 us -> 11.4 us  [local(): far_back = lax.all_to_all(far_out, PLANE, 0, 0, tiled=True)]
    all_to_all x1, waiting for transfers between devices: 3.21 us -> 5.68 us  [local(): own_back = lax.all_to_all(own_out, PLANE, 0, 0, tiled=True)]
    all_to_all x1, waiting for transfers between devices: 3.11 us -> 0.96 us  [local(): second = lax.all_to_all(second, PLANE, 0, 0, tiled=True)]
    ppermute x10 -> x12, starting transfers between devices: 41 us -> 42 us  [swap(): return lax.ppermute(value, axis, [(i, i ^ bit) for i in range(size)])]
    unnamed x48 -> x46, local copies, waits for them, and re-layouts: 14.6 us -> 14.5 us
  transfers between devices with their start and end apart: 15 -> 17, of which waited for: 9 -> 9; matrix products, arithmetic and copies ran while one was open for 4% -> 4% of each run, Pallas kernels for 20% -> 20%
where the time goes in v6:
time: 202 us; the launch traced here: 199 us
  starting transfers between devices  76.7 us (38%)
  Pallas kernels  51.2 us (25%)
  waiting for transfers between devices  47.2 us (23%)
  local copies, waits for them, and re-layouts  17.6 us (9%)
  other arithmetic  3.99 us (2%)
    ppermute x12, starting transfers between devices, swap(): return lax.ppermute(value, axis, [(i, i ^ bit) for i in range(size)])  42 us
    pallas_call x4, Pallas kernels, attend(): pl.pallas_call(functools.partial(attend_kernel, width), grid=(peers // gr...  32.4 us
    all_to_all x1, waiting for transfers between devices, local(): first = lax.all_to_all(first, PLANE, 0, 0, tiled=True)  18.2 us
    ppermute x12, waiting for transfers between devices, swap(): return lax.ppermute(value, axis, [(i, i ^ bit) for i in range(size)])  14.5 us
    unnamed x46, local copies, waits for them, and re-layouts  14.5 us
    pallas_call x2, Pallas kernels, merge_project(): pl.pallas_call(functools.partial(merge_kernel, part), out_shape=(shape, s...  13.8 us
    all_to_all x1, starting transfers between devices, local(): far_back = lax.all_to_all(far_out, PLANE, 0, 0, tiled=True)  11.4 us
    all_to_all x1, starting transfers between devices, local(): own_q = lax.all_to_all(sent, PLANE, 0, 0, tiled=True)  7.59 us
  transfers between devices with their start and end apart: 17, of which 9 were waited for; matrix products, arithmetic and copies ran while one was open for 4% of the time, Pallas kernels for 20%

profile of v6, /device:TPU:1, one launch (start us, length us, event | category | flops | bytes accessed | tf_op | source)
XLA Modules:
  0.0 198.9 jit_solution(7279670869977055083)
XLA Ops:
  0.0 1.1 copy-done.4
  1.8 1.6 dispatch.1
  3.3 7.6 %all-to-all-start = ((bf16[16,32,1024]{2,1,0:T(8,128)(2,1)}), bf16[16,32,1024]{2,1,0:T(8,128)(2,1)S(1)}, u32[]{:S(2)}, u32[]{:S(2)}) async-start(bf16[16,32,1024]{2,1,0:T(8,128)(2,1)} %bitcast.6), calls=%async_computation | async-start | bytes 2097152 | tf_op jit(solution)/shard_map/all_to_all | solution.py:339
  11.0 7.0 %collective-permute-start = (s32[1,256]{1,0:T(1,128)S(1)}, s32[1,256]{1,0:T(1,128)S(1)}, u32[]{:S(2)}, u32[]{:S(2)}) collective-permute-start(s32[1,256]{1,0:T(1,128)S(1)} %bitcast.35), channel_id=1, source_target_pairs={{0,32},{32,0},{1,33},{33,1},{2,34},{34,2},{3,35},{35,3},{4,36},{36... | collective-permute-start | bytes 3080 | tf_op jit(solution)/shard_map/ppermute | solution.py:327
  18.7 2.6 %place.1 = (bf16[16,512,128]{2,1,0:T(8,128)(2,1)S(1)}, bf16[16,512,128]{2,1,0:T(8,128)(2,1)}) custom-call(s32[32]{0:T(128)S(1)} %broadcast_add_fusion.pick_ref, bf16[16,512,128]{2,1,0:T(8,128)(2,1)S(1)} %bitcast.29), custom_call_target="tpu_custom_call" | custom-call | bytes 6291456 | tf_op jit(solution)/shard_map/place/pallas_call | solution.py:80
  21.3 1.3 copy-done.3
  22.6 3.8 %all-to-all-done.q_ref = bf16[16,32,1024]{2,1,0:T(8,128)(2,1)S(1)} async-done(((bf16[16,32,1024]{2,1,0:T(8,128)(2,1)}), bf16[16,32,1024]{2,1,0:T(8,128)(2,1)S(1)}, u32[]{:S(2)}, u32[]{:S(2)}) %all-to-all-start) | async-done | bytes 1048608 | tf_op jit(solution)/shard_map/all_to_all | solution.py:339
  26.5 4.1 %all-to-all-start.1 = ((bf16[16,512,128]{2,1,0:T(8,128)(2,1)}), bf16[16,512,128]{2,1,0:T(8,128)(2,1)S(1)}, u32[]{:S(2)}, u32[]{:S(2)}) async-start(bf16[16,512,128]{2,1,0:T(8,128)(2,1)} %copy-done.3), calls=%async_computation.1 | async-start | bytes 4194304 | tf_op jit(solution)/shard_map/all_to_all | solution.py:351
  30.7 7.0 %collective-permute-start.1 = (bf16[16,32,1024]{2,1,0:T(8,128)(2,1)S(1)}, bf16[16,32,1024]{2,1,0:T(8,128)(2,1)}, u32[]{:S(2)}, u32[]{:S(2)}) collective-permute-start(bf16[16,32,1024]{2,1,0:T(8,128)(2,1)S(1)} %all-to-all-done.q_ref), channel_id=1, source_target_pairs={{0,32},{32,0},{1,33},{33,1},{2,34},{34,2},{3,35},{35,3},{4,36},{36... | collective-permute-start | bytes 3145736 | tf_op jit(solution)/shard_map/ppermute | solution.py:327
  37.7 18.2 %all-to-all-done.1.kv_ref = bf16[16,512,128]{2,1,0:T(8,128)(2,1)S(1)} async-done(((bf16[16,512,128]{2,1,0:T(8,128)(2,1)}), bf16[16,512,128]{2,1,0:T(8,128)(2,1)S(1)}, u32[]{:S(2)}, u32[]{:S(2)}) %all-to-all-start.1) | async-done | bytes 2097184 | tf_op jit(solution)/shard_map/all_to_all | solution.py:351
  55.9 1.3 copy-done
  57.2 6.2 %all-to-all-start.2 = ((bf16[16,512,128]{2,1,0:T(8,128)(2,1)}), bf16[16,512,128]{2,1,0:T(8,128)(2,1)S(1)}, u32[]{:S(2)}, u32[]{:S(2)}) async-start(bf16[16,512,128]{2,1,0:T(8,128)(2,1)} %get-tuple-element.44), calls=%async_computation.2 | async-start | bytes 4194304 | tf_op jit(solution)/shard_map/all_to_all | solution.py:353
  63.5 1.6 copy-done.1
  65.1 7.6 %attend_own.2.refs_0_ = bf16[16,32,1152]{2,1,0:T(8,128)(2,1)S(1)} custom-call(bf16[16,32,1024]{2,1,0:T(8,128)(2,1)S(1)} %all-to-all-done.q_ref, bf16[16,512,128]{2,1,0:T(8,128)(2,1)S(1)} %copy-done.1), custom_call_target="tpu_custom_call" | custom-call | flops 4294967296 | bytes 33554432 | tf_op jit(solution)/shard_map/attend_own/pallas_call | solution.py:180
  73.1 0.8 copy-done.6
  74.3 0.7 fusion.9
  75.0 0.7 fusion.1
  75.8 1.2 convolution_divide_fusion
  77.3 1.8 copy_bitcast_fusion
  79.3 8.5 %attend_far.2.refs_0_ = bf16[16,32,1152]{2,1,0:T(8,128)(2,1)S(1)} custom-call(bf16[16,32,1024]{2,1,0:T(8,128)(2,1)} %collective-permute-done.1.q_ref, bf16[16,512,128]{2,1,0:T(8,128)(2,1)S(1)} %copy-done.2), custom_call_target="tpu_custom_call" | custom-call | flops 4294967296 | bytes 33554432 | tf_op jit(solution)/shard_map/attend_far/pallas_call | solution.py:180
  87.8 1.0 all-to-all-done.2.kv_ref
  88.8 8.5 %attend_far.3 = bf16[16,32,1152]{2,1,0:T(8,128)(2,1)S(1)} custom-call(bf16[16,32,1024]{2,1,0:T(8,128)(2,1)} %collective-permute-done.1.q_ref, bf16[16,512,128]{2,1,0:T(8,128)(2,1)S(1)} %all-to-all-done.2.kv_ref, bf16[16,32,1152]{2,1,0:T(8,128)(2,1)S(1)} %attend_far.2.refs_0_), custom_call_target="tpu_custom_call", output_to_operand_aliasing={{}: (2, {})} | custom-call | flops 4294967296 | bytes 33554432 | tf_op jit(solution)/shard_map/attend_far/pallas_call | solution.py:180
  97.3 1.0 copy-done.9
  98.4 11.4 %all-to-all-start.3 = ((bf16[16,32,1152]{2,1,0:T(8,128)(2,1)}), bf16[16,32,1152]{2,1,0:T(8,128)(2,1)S(1)}, u32[]{:S(2)}, u32[]{:S(2)}) async-start(bf16[16,32,1152]{2,1,0:T(8,128)(2,1)} %copy-done.9), calls=%async_computation.3 | async-start | bytes 2359296 | tf_op jit(solution)/shard_map/all_to_all | solution.py:361
  109.9 1.3 copy-done.7
  111.2 1.2 copy-done.11
  112.4 7.6 %attend_own.3 = bf16[16,32,1152]{2,1,0:T(8,128)(2,1)S(1)} custom-call(bf16[16,32,1024]{2,1,0:T(8,128)(2,1)S(1)} %copy-done.11, bf16[16,512,128]{2,1,0:T(8,128)(2,1)S(1)} %all-to-all-done.2.kv_ref, bf16[16,32,1152]{2,1,0:T(8,128)(2,1)S(1)} %copy-done.7), custom_call_target="tpu_custom_call", output_to_operand_aliasing={{}: (2, {})} | custom-call | flops 4294967296 | bytes 33554432 | tf_op jit(solution)/shard_map/attend_own/pallas_call | solution.py:180
  120.1 1.0 copy-done.8
  121.1 4.0 %all-to-all-done.3 = bf16[16,32,1152]{2,1,0:T(8,128)(2,1)S(1)} async-done(((bf16[16,32,1152]{2,1,0:T(8,128)(2,1)}), bf16[16,32,1152]{2,1,0:T(8,128)(2,1)S(1)}, u32[]{:S(2)}, u32[]{:S(2)}) %all-to-all-start.3) | async-done | bytes 1179680 | tf_op jit(solution)/shard_map/all_to_all | solution.py:361
  125.1 0.8 collect.1
  125.9 5.3 %all-to-all-start.4 = ((bf16[16,32,1152]{2,1,0:T(8,128)(2,1)}), bf16[16,32,1152]{2,1,0:T(8,128)(2,1)S(1)}, u32[]{:S(2)}, u32[]{:S(2)}) async-start(bf16[16,32,1152]{2,1,0:T(8,128)(2,1)} %copy-done.8), calls=%async_computation.4 | async-start | bytes 2359296 | tf_op jit(solution)/shard_map/all_to_all | solution.py:368
  131.3 5.5 %collective-permute-start.2 = (bf16[128,1152]{1,0:T(8,128)(2,1)S(1)}, bf16[128,1152]{1,0:T(8,128)(2,1)S(1)}, u32[]{:S(2)}, u32[]{:S(2)}) collective-permute-start(bf16[128,1152]{1,0:T(8,128)(2,1)S(1)} %get-tuple-element.53), channel_id=1, source_target_pairs={{0,32},{32,0},{1,33},{33,1},{2,34},{34,2},{3,35},{35,3},{4,36},{36... | collective-permute-start | bytes 884744 | tf_op jit(solution)/shard_map/ppermute | solution.py:327
  136.8 0.8 copy.25.col_ref
  137.6 3.4 %collective-permute-done.2.far_ref = bf16[128,1152]{1,0:T(8,128)(2,1)S(1)} collective-permute-done((bf16[128,1152]{1,0:T(8,128)(2,1)S(1)}, bf16[128,1152]{1,0:T(8,128)(2,1)S(1)}, u32[]{:S(2)}, u32[]{:S(2)}) %collective-permute-start.2) | collective-permute-done | bytes 294944 | tf_op jit(solution)/shard_map/ppermute | solution.py:327
  141.0 5.7 %all-to-all-done.4 = bf16[16,32,1152]{2,1,0:T(8,128)(2,1)S(1)} async-done(((bf16[16,32,1152]{2,1,0:T(8,128)(2,1)}), bf16[16,32,1152]{2,1,0:T(8,128)(2,1)S(1)}, u32[]{:S(2)}, u32[]{:S(2)}) %all-to-all-start.4) | async-done | bytes 1179680 | tf_op jit(solution)/shard_map/all_to_all | solution.py:368
  146.7 1.0 copy-done.16
  147.7 6.9 %merge_project.2 = (bf16[64,4096]{1,0:T(8,128)(2,1)}, bf16[64,4096]{1,0:T(8,128)(2,1)}) custom-call(s32[1]{0:T(128)} %bitcast.me_ref, s32[256,1]{1,0:T(8,128)} %copy.25.col_ref, s32[1,256]{1,0:T(1,128)} %bitcast.32, bf16[512,1152]{1,0:T(8,128)(2,1)} %bitcast.40, bf16[128,1152]{1,0:T(8,128)(2,1)} %copy-done.19, f32[256,1024]{1,0:T(8,128)} %get-tuple-element.54.suf_ref, ...), custom_call_target="tpu_custom_call" | custom-call | flops 8589934592 | bytes 25165824 | tf_op jit(solution)/shard_map/merge_project/pallas_call | solution.py:285
  154.6 4.7 %collective-permute-start.3 = (bf16[64,4096]{1,0:T(8,128)(2,1)}, bf16[64,4096]{1,0:T(8,128)(2,1)S(1)}, u32[]{:S(2)}, u32[]{:S(2)}) collective-permute-start(bf16[64,4096]{1,0:T(8,128)(2,1)} %get-tuple-element.57), channel_id=1, source_target_pairs={{0,1},{1,0},{2,3},{3,2},{4,5},{5,4},{6,7},{7,6},{8,9},{9,8},{10,11... | collective-permute-start | bytes 1572872 | tf_op jit(solution)/shard_map/ppermute | solution.py:327
  160.1 6.9 %merge_project.3 = (bf16[64,4096]{1,0:T(8,128)(2,1)}, bf16[64,4096]{1,0:T(8,128)(2,1)}) custom-call(s32[1]{0:T(128)} %bitcast.me_ref, s32[256,1]{1,0:T(8,128)} %copy.25.col_ref, s32[1,256]{1,0:T(1,128)} %bitcast.33, bf16[512,1152]{1,0:T(8,128)(2,1)} %bitcast.41, bf16[128,1152]{1,0:T(8,128)(2,1)} %copy-done.20, f32[256,1024]{1,0:T(8,128)} %get-tuple-element.54.suf_ref, ...), custom_call_target="tpu_custom_call" | custom-call | flops 8589934592 | bytes 25165824 | tf_op jit(solution)/shard_map/merge_project/pallas_call | solution.py:285
  167.2 12.4 %collective-permute-start.4 = (bf16[16,4096]{1,0:T(8,128)(2,1)S(1)}, bf16[16,4096]{1,0:T(8,128)(2,1)S(1)}, u32[]{:S(2)}, u32[]{:S(2)}) collective-permute-start(bf16[16,4096]{1,0:T(8,128)(2,1)S(1)} %get-tuple-element.61), channel_id=1, source_target_pairs={{0,6},{2,4},{4,2},{6,0},{1,7},{3,5},{5,3},{7,1},{8,14},{10,12},{12... | collective-permute-start | bytes 393224 | tf_op jit(solution)/shard_map/ppermute | solution.py:327
  179.9 1.1 add_convert_fusion.3
  181.1 2.1 %collective-permute-start.10 = (bf16[16,4096]{1,0:T(8,128)(2,1)S(1)}, bf16[16,4096]{1,0:T(8,128)(2,1)S(1)}, u32[]{:S(2)}, u32[]{:S(2)}) collective-permute-start(bf16[16,4096]{1,0:T(8,128)(2,1)S(1)} %get-tuple-element.66), channel_id=1, source_target_pairs={{0,4},{2,6},{4,0},{6,2},{1,5},{3,7},{5,1},{7,3},{8,12},{10,14},{12... | collective-permute-start | bytes 393224 | tf_op jit(solution)/shard_map/ppermute | solution.py:327
  183.1 1.5 collective-permute-start.11
  184.6 1.4 collective-permute-start.9
  186.0 4.0 %collective-permute-done.5 = bf16[16,4096]{1,0:T(8,128)(2,1)S(1)} collective-permute-done((bf16[16,4096]{1,0:T(8,128)(2,1)S(1)}, bf16[16,4096]{1,0:T(8,128)(2,1)S(1)}, u32[]{:S(2)}, u32[]{:S(2)}) %collective-permute-start.5) | collective-permute-done | bytes 131104 | tf_op jit(solution)/shard_map/ppermute | solution.py:327
  190.1 5.5 %collective-permute-done.10 = bf16[16,4096]{1,0:T(8,128)(2,1)S(1)} collective-permute-done((bf16[16,4096]{1,0:T(8,128)(2,1)S(1)}, bf16[16,4096]{1,0:T(8,128)(2,1)S(1)}, u32[]{:S(2)}, u32[]{:S(2)}) %collective-permute-start.10) | collective-permute-done | bytes 131104 | tf_op jit(solution)/shard_map/ppermute | solution.py:327
  195.6 1.6 collective-permute-done.9
  197.2 1.0 add_convert_fusion
  (61 shorter events, 5.1 us)
Async XLA Ops:
  0.0 10.9 %copy-start.13 = (s32[256,1]{0,1:T(1,128)S(1)}, s32[256,1]{0,1:T(1,128)}, u32[]{:S(2)}) copy-start(s32[256,1]{0,1:T(1,128)} %param.12) | copy-start | bytes 3076
  0.0 17.9 %copy-start.21 = (s32[1,32]{1,0:T(1,128)S(1)}, s32[1,32]{1,0:T(1,128)}, u32[]{:S(2)}) copy-start(s32[1,32]{1,0:T(1,128)} %param.8) | copy-start | bytes 388
  0.0 1.1 copy-start.4
  1.1 0.7 copy-start.12
  1.8 16.4 %copy-start.14 = (bf16[32,128,2,128]{3,2,1,0:T(2,128)(2,1)S(1)}, bf16[32,128,2,128]{3,2,1,0:T(2,128)(2,1)}, u32[]{:S(2)}) copy-start(bf16[32,128,2,128]{3,2,1,0:T(2,128)(2,1)} %param.7) | copy-start | bytes 6291460
  3.3 23.1 %all-to-all-start = ((bf16[16,32,1024]{2,1,0:T(8,128)(2,1)}), bf16[16,32,1024]{2,1,0:T(8,128)(2,1)S(1)}, u32[]{:S(2)}, u32[]{:S(2)}) async-start(bf16[16,32,1024]{2,1,0:T(8,128)(2,1)} %bitcast.6), calls=%async_computation | async-start | bytes 2097152 | tf_op jit(solution)/shard_map/all_to_all | solution.py:339
  11.0 11.6 %collective-permute-start = (s32[1,256]{1,0:T(1,128)S(1)}, s32[1,256]{1,0:T(1,128)S(1)}, u32[]{:S(2)}, u32[]{:S(2)}) collective-permute-start(s32[1,256]{1,0:T(1,128)S(1)} %bitcast.35), channel_id=1, source_target_pairs={{0,32},{32,0},{1,33},{33,1},{2,34},{34,2},{3,35},{35,3},{4,36},{36... | collective-permute-start | bytes 3080 | tf_op jit(solution)/shard_map/ppermute | solution.py:327
  21.3 1.3 copy-start.3
  26.5 37.0 %copy-start.10 = (bf16[16,32,1024]{2,1,0:T(8,128)(2,1)}, bf16[16,32,1024]{2,1,0:T(8,128)(2,1)S(1)}, u32[]{:S(2)}) copy-start(bf16[16,32,1024]{2,1,0:T(8,128)(2,1)S(1)} %all-to-all-done.q_ref) | copy-start | bytes 3145732
  26.5 4.1 %copy-start.18 = (s32[256]{0:T(256)S(1)}, s32[256]{0:T(256)}, u32[]{:S(2)}) copy-start(s32[256]{0:T(256)} %param.11) | copy-start | bytes 3076
  26.5 29.4 %all-to-all-start.1 = ((bf16[16,512,128]{2,1,0:T(8,128)(2,1)}), bf16[16,512,128]{2,1,0:T(8,128)(2,1)S(1)}, u32[]{:S(2)}, u32[]{:S(2)}) async-start(bf16[16,512,128]{2,1,0:T(8,128)(2,1)} %copy-done.3), calls=%async_computation.1 | async-start | bytes 4194304 | tf_op jit(solution)/shard_map/all_to_all | solution.py:351
  30.7 48.4 %collective-permute-start.1 = (bf16[16,32,1024]{2,1,0:T(8,128)(2,1)S(1)}, bf16[16,32,1024]{2,1,0:T(8,128)(2,1)}, u32[]{:S(2)}, u32[]{:S(2)}) collective-permute-start(bf16[16,32,1024]{2,1,0:T(8,128)(2,1)S(1)} %all-to-all-done.q_ref), channel_id=1, source_target_pairs={{0,32},{32,0},{1,33},{33,1},{2,34},{34,2},{3,35},{35,3},{4,36},{36... | collective-permute-start | bytes 3145736 | tf_op jit(solution)/shard_map/ppermute | solution.py:327
  55.9 1.3 copy-start
  57.2 31.5 %all-to-all-start.2 = ((bf16[16,512,128]{2,1,0:T(8,128)(2,1)}), bf16[16,512,128]{2,1,0:T(8,128)(2,1)S(1)}, u32[]{:S(2)}, u32[]{:S(2)}) async-start(bf16[16,512,128]{2,1,0:T(8,128)(2,1)} %get-tuple-element.44), calls=%async_computation.2 | async-start | bytes 4194304 | tf_op jit(solution)/shard_map/all_to_all | solution.py:353
  63.5 1.6 copy-start.1
  65.1 7.7 %copy-start.15 = (bf16[256,16,2,128]{3,2,1,0:T(2,128)(2,1)S(1)}, bf16[256,16,2,128]{3,2,1,0:T(2,128)(2,1)}, u32[]{:S(2)}) copy-start(bf16[256,16,2,128]{3,2,1,0:T(2,128)(2,1)} %param.10) | copy-start | bytes 6291460
  72.8 1.1 copy-start.6
  72.8 1.4 copy-start.5
  77.3 2.0 copy-start.2
  97.3 1.0 copy-start.9
  98.4 26.7 %all-to-all-start.3 = ((bf16[16,32,1152]{2,1,0:T(8,128)(2,1)}), bf16[16,32,1152]{2,1,0:T(8,128)(2,1)S(1)}, u32[]{:S(2)}, u32[]{:S(2)}) async-start(bf16[16,32,1152]{2,1,0:T(8,128)(2,1)} %copy-done.9), calls=%async_computation.3 | async-start | bytes 2359296 | tf_op jit(solution)/shard_map/all_to_all | solution.py:361
  109.9 1.3 copy-start.7
  111.2 1.2 copy-start.11
  120.1 1.0 copy-start.8
  125.9 20.8 %all-to-all-start.4 = ((bf16[16,32,1152]{2,1,0:T(8,128)(2,1)}), bf16[16,32,1152]{2,1,0:T(8,128)(2,1)S(1)}, u32[]{:S(2)}, u32[]{:S(2)}) async-start(bf16[16,32,1152]{2,1,0:T(8,128)(2,1)} %copy-done.8), calls=%async_computation.4 | async-start | bytes 2359296 | tf_op jit(solution)/shard_map/all_to_all | solution.py:368
  131.3 9.7 %collective-permute-start.2 = (bf16[128,1152]{1,0:T(8,128)(2,1)S(1)}, bf16[128,1152]{1,0:T(8,128)(2,1)S(1)}, u32[]{:S(2)}, u32[]{:S(2)}) collective-permute-start(bf16[128,1152]{1,0:T(8,128)(2,1)S(1)} %get-tuple-element.53), channel_id=1, source_target_pairs={{0,32},{32,0},{1,33},{33,1},{2,34},{34,2},{3,35},{35,3},{4,36},{36... | collective-permute-start | bytes 884744 | tf_op jit(solution)/shard_map/ppermute | solution.py:327
  137.6 21.8 %collective-permute-start.7 = (bf16[128,1152]{1,0:T(8,128)(2,1)S(1)}, bf16[128,1152]{1,0:T(8,128)(2,1)S(1)}, u32[]{:S(2)}, u32[]{:S(2)}) collective-permute-start(bf16[128,1152]{1,0:T(8,128)(2,1)S(1)} %get-tuple-element.58), channel_id=1, source_target_pairs={{0,32},{32,0},{1,33},{33,1},{2,34},{34,2},{3,35},{35,3},{4,36},{36... | collective-permute-start | bytes 884744 | tf_op jit(solution)/shard_map/ppermute | solution.py:327
  141.0 5.7 %copy-start.19 = (bf16[128,1152]{1,0:T(8,128)(2,1)}, bf16[128,1152]{1,0:T(8,128)(2,1)S(1)}, u32[]{:S(2)}) copy-start(bf16[128,1152]{1,0:T(8,128)(2,1)S(1)} %collective-permute-done.2.far_ref) | copy-start | bytes 884740
  146.7 1.0 copy-start.16
  154.6 12.4 %copy-start.17 = (bf16[64,4096]{1,0:T(8,128)(2,1)S(1)}, bf16[64,4096]{1,0:T(8,128)(2,1)}, u32[]{:S(2)}) copy-start(bf16[64,4096]{1,0:T(8,128)(2,1)} %get-tuple-element.56) | copy-start | bytes 1572868
  154.6 12.4 %collective-permute-start.3 = (bf16[64,4096]{1,0:T(8,128)(2,1)}, bf16[64,4096]{1,0:T(8,128)(2,1)S(1)}, u32[]{:S(2)}, u32[]{:S(2)}) collective-permute-start(bf16[64,4096]{1,0:T(8,128)(2,1)} %get-tuple-element.57), channel_id=1, source_target_pairs={{0,1},{1,0},{2,3},{3,2},{4,5},{5,4},{6,7},{7,6},{8,9},{9,8},{10,11... | collective-permute-start | bytes 1572872 | tf_op jit(solution)/shard_map/ppermute | solution.py:327
  159.3 0.7 copy-start.20
  166.9 13.0 %collective-permute-start.8 = (bf16[64,4096]{1,0:T(8,128)(2,1)}, bf16[64,4096]{1,0:T(8,128)(2,1)S(1)}, u32[]{:S(2)}, u32[]{:S(2)}) collective-permute-start(bf16[64,4096]{1,0:T(8,128)(2,1)} %get-tuple-element.60), channel_id=1, source_target_pairs={{0,1},{1,0},{2,3},{3,2},{4,5},{5,4},{6,7},{7,6},{8,9},{9,8},{10,11... | collective-permute-start | bytes 1572872 | tf_op jit(solution)/shard_map/ppermute | solution.py:327
  167.2 17.4 %collective-permute-start.4 = (bf16[16,4096]{1,0:T(8,128)(2,1)S(1)}, bf16[16,4096]{1,0:T(8,128)(2,1)S(1)}, u32[]{:S(2)}, u32[]{:S(2)}) collective-permute-start(bf16[16,4096]{1,0:T(8,128)(2,1)S(1)} %get-tuple-element.61), channel_id=1, source_target_pairs={{0,6},{2,4},{4,2},{6,0},{1,7},{3,5},{5,3},{7,1},{8,14},{10,12},{12... | collective-permute-start | bytes 393224 | tf_op jit(solution)/shard_map/ppermute | solution.py:327
  179.6 10.4 %collective-permute-start.5 = (bf16[16,4096]{1,0:T(8,128)(2,1)S(1)}, bf16[16,4096]{1,0:T(8,128)(2,1)S(1)}, u32[]{:S(2)}, u32[]{:S(2)}) collective-permute-start(bf16[16,4096]{1,0:T(8,128)(2,1)S(1)} %get-tuple-element.63), channel_id=1, source_target_pairs={{0,4},{2,6},{4,0},{6,2},{1,5},{3,7},{5,1},{7,3},{8,12},{10,14},{12... | collective-permute-start | bytes 393224 | tf_op jit(solution)/shard_map/ppermute | solution.py:327
  179.6 10.4 %collective-permute-start.6 = (bf16[16,4096]{1,0:T(8,128)(2,1)S(1)}, bf16[16,4096]{1,0:T(8,128)(2,1)S(1)}, u32[]{:S(2)}, u32[]{:S(2)}) collective-permute-start(bf16[16,4096]{1,0:T(8,128)(2,1)S(1)} %get-tuple-element.62), channel_id=1, source_target_pairs={{0,2},{2,0},{4,6},{6,4},{1,3},{3,1},{5,7},{7,5},{8,10},{10,8},{12,... | collective-permute-start | bytes 393224 | tf_op jit(solution)/shard_map/ppermute | solution.py:327
  181.1 14.5 %collective-permute-start.10 = (bf16[16,4096]{1,0:T(8,128)(2,1)S(1)}, bf16[16,4096]{1,0:T(8,128)(2,1)S(1)}, u32[]{:S(2)}, u32[]{:S(2)}) collective-permute-start(bf16[16,4096]{1,0:T(8,128)(2,1)S(1)} %get-tuple-element.66), channel_id=1, source_target_pairs={{0,4},{2,6},{4,0},{6,2},{1,5},{3,7},{5,1},{7,3},{8,12},{10,14},{12... | collective-permute-start | bytes 393224 | tf_op jit(solution)/shard_map/ppermute | solution.py:327
  183.1 12.5 %collective-permute-start.11 = (bf16[16,4096]{1,0:T(8,128)(2,1)S(1)}, bf16[16,4096]{1,0:T(8,128)(2,1)S(1)}, u32[]{:S(2)}, u32[]{:S(2)}) collective-permute-start(bf16[16,4096]{1,0:T(8,128)(2,1)S(1)} %get-tuple-element.65), channel_id=1, source_target_pairs={{0,2},{2,0},{4,6},{6,4},{1,3},{3,1},{5,7},{7,5},{8,10},{10,8},{12,... | collective-permute-start | bytes 393224 | tf_op jit(solution)/shard_map/ppermute | solution.py:327
  184.6 12.6 %collective-permute-start.9 = (bf16[16,4096]{1,0:T(8,128)(2,1)S(1)}, bf16[16,4096]{1,0:T(8,128)(2,1)S(1)}, u32[]{:S(2)}, u32[]{:S(2)}) collective-permute-start(bf16[16,4096]{1,0:T(8,128)(2,1)S(1)} %get-tuple-element.64), channel_id=1, source_target_pairs={{0,6},{2,4},{4,2},{6,0},{1,7},{3,5},{5,3},{7,1},{8,14},{10,12},{12... | collective-permute-start | bytes 393224 | tf_op jit(solution)/shard_map/ppermute | solution.py:327

commit v7 on v6

--- a/solution.py
+++ b/solution.py
@@ -377,17 +377,18 @@
     def add(a, b):
         return (a.astype(F32) + b.astype(F32)).astype(BF16)
 
-    def spread(send, keep):
-        got = swap(send, "core", 1)
-        step = keep.shape[0] // 4
-        blocks = [add(keep[q * step : (q + 1) * step], got[q * step : (q + 1) * step]) for q in range(4)]
-        parts = [swap(blocks[q], "zl", bit) for q, bit in ((0, 3), (2, 2), (1, 1))]
-        total = blocks[3].astype(F32)
-        for part in parts:
-            total = total + part.astype(F32)
-        return total.astype(BF16)
-
-    return jnp.concatenate([spread(*half) for half in halves], axis=0)
+    got = [swap(send, "core", 1) for send, _ in halves]
+    step = halves[0][1].shape[0] // 4
+
+    def block(q):
+        rows = slice(q * step, (q + 1) * step)
+        return jnp.concatenate([add(keep[rows], g[rows]) for (_, keep), g in zip(halves, got)], axis=0)
+
+    parts = [swap(block(q), "zl", bit) for q, bit in ((0, 3), (2, 2), (1, 1))]
+    total = block(3).astype(F32)
+    for part in parts:
+        total = total + part.astype(F32)
+    return total.astype(BF16)
 
 
 def solution(mesh):

time: 202 us -> 204 us (level)
  waiting for transfers between devices: 47.2 us -> 60.6 us
  starting transfers between devices: 76.7 us -> 67.8 us
    ppermute x12 -> x9, waiting for transfers between devices: 14.5 us -> 28.8 us  [swap(): return lax.ppermute(value, axis, [(i, i ^ bit) for i in range(size)])]
    ppermute x12 -> x9, starting transfers between devices: 42 us -> 34.5 us  [swap(): return lax.ppermute(value, axis, [(i, i ^ bit) for i in range(size)])]
  transfers between devices with their start and end apart: 17 -> 14, of which waited for: 9 -> 9; matrix products, arithmetic and copies ran while one was open for 4% -> 3% of each run, Pallas kernels for 20% -> 20%
where the time goes in v7:
time: 204 us; the launch traced here: 203 us
  starting transfers between devices  67.8 us (33%)
  waiting for transfers between devices  60.6 us (30%)
  Pallas kernels  51.2 us (25%)
  local copies, waits for them, and re-layouts  17.6 us (9%)
  other arithmetic  3.2 us (2%)
    ppermute x9, starting transfers between devices, swap(): return lax.ppermute(value, axis, [(i, i ^ bit) for i in range(size)])  34.5 us
    pallas_call x4, Pallas kernels, attend(): pl.pallas_call(functools.partial(attend_kernel, width), grid=(peers // gr...  32.4 us
    ppermute x9, waiting for transfers between devices, swap(): return lax.ppermute(value, axis, [(i, i ^ bit) for i in range(size)])  28.8 us
    all_to_all x1, waiting for transfers between devices, local(): first = lax.all_to_all(first, PLANE, 0, 0, tiled=True)  18.2 us
    unnamed x46, local copies, waits for them, and re-layouts  14.5 us
    pallas_call x2, Pallas kernels, merge_project(): pl.pallas_call(functools.partial(merge_kernel, part), out_shape=(shape, s...  13.8 us
    all_to_all x1, starting transfers between devices, local(): far_back = lax.all_to_all(far_out, PLANE, 0, 0, tiled=True)  9.96 us
    all_to_all x1, starting transfers between devices, local(): own_q = lax.all_to_all(sent, PLANE, 0, 0, tiled=True)  7.59 us
  transfers between devices with their start and end apart: 14, of which 9 were waited for; matrix products, arithmetic and copies ran while one was open for 3% of the time, Pallas kernels for 20%

profile of v7, /device:TPU:1, one launch (start us, length us, event | category | flops | bytes accessed | tf_op | source)
XLA Modules:
  0.0 202.6 jit_solution(17032253653589710055)
XLA Ops:
  0.0 1.1 copy-done.4
  1.1 0.7 copy-done.12
  1.8 1.6 dispatch.1
  3.4 7.6 %all-to-all-start = ((bf16[16,32,1024]{2,1,0:T(8,128)(2,1)}), bf16[16,32,1024]{2,1,0:T(8,128)(2,1)S(1)}, u32[]{:S(2)}, u32[]{:S(2)}) async-start(bf16[16,32,1024]{2,1,0:T(8,128)(2,1)} %bitcast.6), calls=%async_computation | async-start | bytes 2097152 | tf_op jit(solution)/shard_map/all_to_all | solution.py:339
  11.0 7.0 %collective-permute-start = (s32[1,256]{1,0:T(1,128)S(1)}, s32[1,256]{1,0:T(1,128)S(1)}, u32[]{:S(2)}, u32[]{:S(2)}) collective-permute-start(s32[1,256]{1,0:T(1,128)S(1)} %bitcast.35), channel_id=1, source_target_pairs={{0,32},{32,0},{1,33},{33,1},{2,34},{34,2},{3,35},{35,3},{4,36},{36... | collective-permute-start | bytes 3080 | tf_op jit(solution)/shard_map/ppermute | solution.py:327
  18.2 0.5 copy.21
  18.7 2.6 %place.1 = (bf16[16,512,128]{2,1,0:T(8,128)(2,1)S(1)}, bf16[16,512,128]{2,1,0:T(8,128)(2,1)}) custom-call(s32[32]{0:T(128)S(1)} %broadcast_add_fusion.pick_ref, bf16[16,512,128]{2,1,0:T(8,128)(2,1)S(1)} %bitcast.29), custom_call_target="tpu_custom_call" | custom-call | bytes 6291456 | tf_op jit(solution)/shard_map/place/pallas_call | solution.py:80
  21.3 1.3 copy-done.3
  22.6 3.8 %all-to-all-done.q_ref = bf16[16,32,1024]{2,1,0:T(8,128)(2,1)S(1)} async-done(((bf16[16,32,1024]{2,1,0:T(8,128)(2,1)}), bf16[16,32,1024]{2,1,0:T(8,128)(2,1)S(1)}, u32[]{:S(2)}, u32[]{:S(2)}) %all-to-all-start) | async-done | bytes 1048608 | tf_op jit(solution)/shard_map/all_to_all | solution.py:339
  26.5 4.1 %all-to-all-start.1 = ((bf16[16,512,128]{2,1,0:T(8,128)(2,1)}), bf16[16,512,128]{2,1,0:T(8,128)(2,1)S(1)}, u32[]{:S(2)}, u32[]{:S(2)}) async-start(bf16[16,512,128]{2,1,0:T(8,128)(2,1)} %copy-done.3), calls=%async_computation.1 | async-start | bytes 4194304 | tf_op jit(solution)/shard_map/all_to_all | solution.py:351
  30.7 7.0 %collective-permute-start.1 = (bf16[16,32,1024]{2,1,0:T(8,128)(2,1)S(1)}, bf16[16,32,1024]{2,1,0:T(8,128)(2,1)}, u32[]{:S(2)}, u32[]{:S(2)}) collective-permute-start(bf16[16,32,1024]{2,1,0:T(8,128)(2,1)S(1)} %all-to-all-done.q_ref), channel_id=1, source_target_pairs={{0,32},{32,0},{1,33},{33,1},{2,34},{34,2},{3,35},{35,3},{4,36},{36... | collective-permute-start | bytes 3145736 | tf_op jit(solution)/shard_map/ppermute | solution.py:327
  37.7 18.2 %all-to-all-done.1.kv_ref = bf16[16,512,128]{2,1,0:T(8,128)(2,1)S(1)} async-done(((bf16[16,512,128]{2,1,0:T(8,128)(2,1)}), bf16[16,512,128]{2,1,0:T(8,128)(2,1)S(1)}, u32[]{:S(2)}, u32[]{:S(2)}) %all-to-all-start.1) | async-done | bytes 2097184 | tf_op jit(solution)/shard_map/all_to_all | solution.py:351
  55.9 1.3 copy-done
  57.3 6.2 %all-to-all-start.2 = ((bf16[16,512,128]{2,1,0:T(8,128)(2,1)}), bf16[16,512,128]{2,1,0:T(8,128)(2,1)S(1)}, u32[]{:S(2)}, u32[]{:S(2)}) async-start(bf16[16,512,128]{2,1,0:T(8,128)(2,1)} %get-tuple-element.44), calls=%async_computation.2 | async-start | bytes 4194304 | tf_op jit(solution)/shard_map/all_to_all | solution.py:353
  63.5 1.6 copy-done.1
  65.1 7.6 %attend_own.2.refs_0_ = bf16[16,32,1152]{2,1,0:T(8,128)(2,1)S(1)} custom-call(bf16[16,32,1024]{2,1,0:T(8,128)(2,1)S(1)} %all-to-all-done.q_ref, bf16[16,512,128]{2,1,0:T(8,128)(2,1)S(1)} %copy-done.1), custom_call_target="tpu_custom_call" | custom-call | flops 4294967296 | bytes 33554432 | tf_op jit(solution)/shard_map/attend_own/pallas_call | solution.py:180
  73.1 0.8 copy-done.6
  74.3 0.7 fusion.9
  75.1 0.7 fusion.1
  75.8 1.2 convolution_divide_fusion
  77.3 1.8 copy_bitcast_fusion
  79.3 8.5 %attend_far.2.refs_0_ = bf16[16,32,1152]{2,1,0:T(8,128)(2,1)S(1)} custom-call(bf16[16,32,1024]{2,1,0:T(8,128)(2,1)} %collective-permute-done.1.q_ref, bf16[16,512,128]{2,1,0:T(8,128)(2,1)S(1)} %copy-done.2), custom_call_target="tpu_custom_call" | custom-call | flops 4294967296 | bytes 33554432 | tf_op jit(solution)/shard_map/attend_far/pallas_call | solution.py:180
  87.8 1.0 all-to-all-done.2.kv_ref
  88.8 8.5 %attend_far.3 = bf16[16,32,1152]{2,1,0:T(8,128)(2,1)S(1)} custom-call(bf16[16,32,1024]{2,1,0:T(8,128)(2,1)} %collective-permute-done.1.q_ref, bf16[16,512,128]{2,1,0:T(8,128)(2,1)S(1)} %all-to-all-done.2.kv_ref, bf16[16,32,1152]{2,1,0:T(8,128)(2,1)S(1)} %attend_far.2.refs_0_), custom_call_target="tpu_custom_call", output_to_operand_aliasing={{}: (2, {})} | custom-call | flops 4294967296 | bytes 33554432 | tf_op jit(solution)/shard_map/attend_far/pallas_call | solution.py:180
  97.4 1.0 copy-done.9
  98.4 10.0 %all-to-all-start.3 = ((bf16[16,32,1152]{2,1,0:T(8,128)(2,1)}), bf16[16,32,1152]{2,1,0:T(8,128)(2,1)S(1)}, u32[]{:S(2)}, u32[]{:S(2)}) async-start(bf16[16,32,1152]{2,1,0:T(8,128)(2,1)} %copy-done.9), calls=%async_computation.3 | async-start | bytes 2359296 | tf_op jit(solution)/shard_map/all_to_all | solution.py:361
  108.5 1.3 copy-done.7
  109.8 1.2 copy-done.11
  111.0 7.6 %attend_own.3 = bf16[16,32,1152]{2,1,0:T(8,128)(2,1)S(1)} custom-call(bf16[16,32,1024]{2,1,0:T(8,128)(2,1)S(1)} %copy-done.11, bf16[16,512,128]{2,1,0:T(8,128)(2,1)S(1)} %all-to-all-done.2.kv_ref, bf16[16,32,1152]{2,1,0:T(8,128)(2,1)S(1)} %copy-done.7), custom_call_target="tpu_custom_call", output_to_operand_aliasing={{}: (2, {})} | custom-call | flops 4294967296 | bytes 33554432 | tf_op jit(solution)/shard_map/attend_own/pallas_call | solution.py:180
  118.7 1.0 copy-done.8
  119.7 4.0 %all-to-all-done.3 = bf16[16,32,1152]{2,1,0:T(8,128)(2,1)S(1)} async-done(((bf16[16,32,1152]{2,1,0:T(8,128)(2,1)}), bf16[16,32,1152]{2,1,0:T(8,128)(2,1)S(1)}, u32[]{:S(2)}, u32[]{:S(2)}) %all-to-all-start.3) | async-done | bytes 1179680 | tf_op jit(solution)/shard_map/all_to_all | solution.py:361
  123.7 0.8 collect.1
  124.5 5.3 %all-to-all-start.4 = ((bf16[16,32,1152]{2,1,0:T(8,128)(2,1)}), bf16[16,32,1152]{2,1,0:T(8,128)(2,1)S(1)}, u32[]{:S(2)}, u32[]{:S(2)}) async-start(bf16[16,32,1152]{2,1,0:T(8,128)(2,1)} %copy-done.8), calls=%async_computation.4 | async-start | bytes 2359296 | tf_op jit(solution)/shard_map/all_to_all | solution.py:368
  129.8 6.2 %collective-permute-start.2 = (bf16[128,1152]{1,0:T(8,128)(2,1)S(1)}, bf16[128,1152]{1,0:T(8,128)(2,1)S(1)}, u32[]{:S(2)}, u32[]{:S(2)}) collective-permute-start(bf16[128,1152]{1,0:T(8,128)(2,1)S(1)} %get-tuple-element.53), channel_id=1, source_target_pairs={{0,32},{32,0},{1,33},{33,1},{2,34},{34,2},{3,35},{35,3},{4,36},{36... | collective-permute-start | bytes 884744 | tf_op jit(solution)/shard_map/ppermute | solution.py:327
  136.0 0.8 copy.25.col_ref
  136.8 3.8 %collective-permute-done.2.far_ref = bf16[128,1152]{1,0:T(8,128)(2,1)S(1)} collective-permute-done((bf16[128,1152]{1,0:T(8,128)(2,1)S(1)}, bf16[128,1152]{1,0:T(8,128)(2,1)S(1)}, u32[]{:S(2)}, u32[]{:S(2)}) %collective-permute-start.2) | collective-permute-done | bytes 294944 | tf_op jit(solution)/shard_map/ppermute | solution.py:327
  140.7 4.8 %all-to-all-done.4 = bf16[16,32,1152]{2,1,0:T(8,128)(2,1)S(1)} async-done(((bf16[16,32,1152]{2,1,0:T(8,128)(2,1)}), bf16[16,32,1152]{2,1,0:T(8,128)(2,1)S(1)}, u32[]{:S(2)}, u32[]{:S(2)}) %all-to-all-start.4) | async-done | bytes 1179680 | tf_op jit(solution)/shard_map/all_to_all | solution.py:368
  145.4 1.0 copy-done.16
  146.5 6.9 %merge_project.2 = (bf16[64,4096]{1,0:T(8,128)(2,1)}, bf16[64,4096]{1,0:T(8,128)(2,1)}) custom-call(s32[1]{0:T(128)} %bitcast.me_ref, s32[256,1]{1,0:T(8,128)} %copy.25.col_ref, s32[1,256]{1,0:T(1,128)} %bitcast.32, bf16[512,1152]{1,0:T(8,128)(2,1)} %bitcast.40, bf16[128,1152]{1,0:T(8,128)(2,1)} %copy-done.19, f32[256,1024]{1,0:T(8,128)} %get-tuple-element.54.suf_ref, ...), custom_call_target="tpu_custom_call" | custom-call | flops 8589934592 | bytes 25165824 | tf_op jit(solution)/shard_map/merge_project/pallas_call | solution.py:285
  153.4 4.0 %collective-permute-start.3 = (bf16[64,4096]{1,0:T(8,128)(2,1)}, bf16[64,4096]{1,0:T(8,128)(2,1)S(1)}, u32[]{:S(2)}, u32[]{:S(2)}) collective-permute-start(bf16[64,4096]{1,0:T(8,128)(2,1)} %get-tuple-element.57), channel_id=1, source_target_pairs={{0,1},{1,0},{2,3},{3,2},{4,5},{5,4},{6,7},{7,6},{8,9},{9,8},{10,11... | collective-permute-start | bytes 1572872 | tf_op jit(solution)/shard_map/ppermute | solution.py:327
  157.4 0.7 copy-done.20
  158.1 6.9 %merge_project.3 = (bf16[64,4096]{1,0:T(8,128)(2,1)}, bf16[64,4096]{1,0:T(8,128)(2,1)}) custom-call(s32[1]{0:T(128)} %bitcast.me_ref, s32[256,1]{1,0:T(8,128)} %copy.25.col_ref, s32[1,256]{1,0:T(1,128)} %bitcast.33, bf16[512,1152]{1,0:T(8,128)(2,1)} %bitcast.41, bf16[128,1152]{1,0:T(8,128)(2,1)} %copy-done.20, f32[256,1024]{1,0:T(8,128)} %get-tuple-element.54.suf_ref, ...), custom_call_target="tpu_custom_call" | custom-call | flops 8589934592 | bytes 25165824 | tf_op jit(solution)/shard_map/merge_project/pallas_call | solution.py:285
  165.3 2.0 collective-permute-done.5
  167.2 1.2 add_convert_fusion.7
  168.5 9.6 %collective-permute-start.6 = (bf16[32,4096]{1,0:T(8,128)(2,1)S(1)}, bf16[32,4096]{1,0:T(8,128)(2,1)S(1)}, u32[]{:S(2)}, u32[]{:S(2)}) collective-permute-start(bf16[32,4096]{1,0:T(8,128)(2,1)S(1)} %pad_maximum_fusion), channel_id=1, source_target_pairs={{0,6},{2,4},{4,2},{6,0},{1,7},{3,5},{5,3},{7,1},{8,14},{10,12},{12... | collective-permute-start | bytes 786440 | tf_op jit(solution)/shard_map/ppermute | solution.py:327
  178.8 5.9 %collective-permute-done.6 = bf16[32,4096]{1,0:T(8,128)(2,1)S(1)} collective-permute-done((bf16[32,4096]{1,0:T(8,128)(2,1)S(1)}, bf16[32,4096]{1,0:T(8,128)(2,1)S(1)}, u32[]{:S(2)}, u32[]{:S(2)}) %collective-permute-start.6) | collective-permute-done | bytes 262176 | tf_op jit(solution)/shard_map/ppermute | solution.py:327
  184.7 17.1 %collective-permute-done.7 = bf16[32,4096]{1,0:T(8,128)(2,1)S(1)} collective-permute-done((bf16[32,4096]{1,0:T(8,128)(2,1)S(1)}, bf16[32,4096]{1,0:T(8,128)(2,1)S(1)}, u32[]{:S(2)}, u32[]{:S(2)}) %collective-permute-start.7) | collective-permute-done | bytes 262176 | tf_op jit(solution)/shard_map/ppermute | solution.py:327
  201.8 0.8 add_convert_fusion
  (56 shorter events, 2.7 us)
Async XLA Ops:
  0.0 11.0 %copy-start.13 = (s32[256,1]{0,1:T(1,128)S(1)}, s32[256,1]{0,1:T(1,128)}, u32[]{:S(2)}) copy-start(s32[256,1]{0,1:T(1,128)} %param.12) | copy-start | bytes 3076
  0.0 18.0 %copy-start.21 = (s32[1,32]{1,0:T(1,128)S(1)}, s32[1,32]{1,0:T(1,128)}, u32[]{:S(2)}) copy-start(s32[1,32]{1,0:T(1,128)} %param.8) | copy-start | bytes 388
  0.0 1.1 copy-start.4
  1.1 0.7 copy-start.12
  1.8 16.4 %copy-start.14 = (bf16[32,128,2,128]{3,2,1,0:T(2,128)(2,1)S(1)}, bf16[32,128,2,128]{3,2,1,0:T(2,128)(2,1)}, u32[]{:S(2)}) copy-start(bf16[32,128,2,128]{3,2,1,0:T(2,128)(2,1)} %param.7) | copy-start | bytes 6291460
  3.4 23.1 %all-to-all-start = ((bf16[16,32,1024]{2,1,0:T(8,128)(2,1)}), bf16[16,32,1024]{2,1,0:T(8,128)(2,1)S(1)}, u32[]{:S(2)}, u32[]{:S(2)}) async-start(bf16[16,32,1024]{2,1,0:T(8,128)(2,1)} %bitcast.6), calls=%async_computation | async-start | bytes 2097152 | tf_op jit(solution)/shard_map/all_to_all | solution.py:339
  11.0 11.7 %collective-permute-start = (s32[1,256]{1,0:T(1,128)S(1)}, s32[1,256]{1,0:T(1,128)S(1)}, u32[]{:S(2)}, u32[]{:S(2)}) collective-permute-start(s32[1,256]{1,0:T(1,128)S(1)} %bitcast.35), channel_id=1, source_target_pairs={{0,32},{32,0},{1,33},{33,1},{2,34},{34,2},{3,35},{35,3},{4,36},{36... | collective-permute-start | bytes 3080 | tf_op jit(solution)/shard_map/ppermute | solution.py:327
  21.3 1.3 copy-start.3
  26.5 37.1 %copy-start.10 = (bf16[16,32,1024]{2,1,0:T(8,128)(2,1)}, bf16[16,32,1024]{2,1,0:T(8,128)(2,1)S(1)}, u32[]{:S(2)}) copy-start(bf16[16,32,1024]{2,1,0:T(8,128)(2,1)S(1)} %all-to-all-done.q_ref) | copy-start | bytes 3145732
  26.5 4.1 %copy-start.18 = (s32[256]{0:T(256)S(1)}, s32[256]{0:T(256)}, u32[]{:S(2)}) copy-start(s32[256]{0:T(256)} %param.11) | copy-start | bytes 3076
  26.5 29.4 %all-to-all-start.1 = ((bf16[16,512,128]{2,1,0:T(8,128)(2,1)}), bf16[16,512,128]{2,1,0:T(8,128)(2,1)S(1)}, u32[]{:S(2)}, u32[]{:S(2)}) async-start(bf16[16,512,128]{2,1,0:T(8,128)(2,1)} %copy-done.3), calls=%async_computation.1 | async-start | bytes 4194304 | tf_op jit(solution)/shard_map/all_to_all | solution.py:351
  30.7 48.4 %collective-permute-start.1 = (bf16[16,32,1024]{2,1,0:T(8,128)(2,1)S(1)}, bf16[16,32,1024]{2,1,0:T(8,128)(2,1)}, u32[]{:S(2)}, u32[]{:S(2)}) collective-permute-start(bf16[16,32,1024]{2,1,0:T(8,128)(2,1)S(1)} %all-to-all-done.q_ref), channel_id=1, source_target_pairs={{0,32},{32,0},{1,33},{33,1},{2,34},{34,2},{3,35},{35,3},{4,36},{36... | collective-permute-start | bytes 3145736 | tf_op jit(solution)/shard_map/ppermute | solution.py:327
  55.9 1.3 copy-start
  57.3 31.5 %all-to-all-start.2 = ((bf16[16,512,128]{2,1,0:T(8,128)(2,1)}), bf16[16,512,128]{2,1,0:T(8,128)(2,1)S(1)}, u32[]{:S(2)}, u32[]{:S(2)}) async-start(bf16[16,512,128]{2,1,0:T(8,128)(2,1)} %get-tuple-element.44), calls=%async_computation.2 | async-start | bytes 4194304 | tf_op jit(solution)/shard_map/all_to_all | solution.py:353
  63.5 1.6 copy-start.1
  65.1 7.7 %copy-start.15 = (bf16[256,16,2,128]{3,2,1,0:T(2,128)(2,1)S(1)}, bf16[256,16,2,128]{3,2,1,0:T(2,128)(2,1)}, u32[]{:S(2)}) copy-start(bf16[256,16,2,128]{3,2,1,0:T(2,128)(2,1)} %param.10) | copy-start | bytes 6291460
  72.8 1.1 copy-start.6
  72.8 1.4 copy-start.5
  77.3 2.0 copy-start.2
  97.4 1.0 copy-start.9
  98.4 25.3 %all-to-all-start.3 = ((bf16[16,32,1152]{2,1,0:T(8,128)(2,1)}), bf16[16,32,1152]{2,1,0:T(8,128)(2,1)S(1)}, u32[]{:S(2)}, u32[]{:S(2)}) async-start(bf16[16,32,1152]{2,1,0:T(8,128)(2,1)} %copy-done.9), calls=%async_computation.3 | async-start | bytes 2359296 | tf_op jit(solution)/shard_map/all_to_all | solution.py:361
  108.5 1.3 copy-start.7
  109.8 1.2 copy-start.11
  118.7 1.0 copy-start.8
  124.5 20.9 %all-to-all-start.4 = ((bf16[16,32,1152]{2,1,0:T(8,128)(2,1)}), bf16[16,32,1152]{2,1,0:T(8,128)(2,1)S(1)}, u32[]{:S(2)}, u32[]{:S(2)}) async-start(bf16[16,32,1152]{2,1,0:T(8,128)(2,1)} %copy-done.8), calls=%async_computation.4 | async-start | bytes 2359296 | tf_op jit(solution)/shard_map/all_to_all | solution.py:368
  129.8 10.8 %collective-permute-start.2 = (bf16[128,1152]{1,0:T(8,128)(2,1)S(1)}, bf16[128,1152]{1,0:T(8,128)(2,1)S(1)}, u32[]{:S(2)}, u32[]{:S(2)}) collective-permute-start(bf16[128,1152]{1,0:T(8,128)(2,1)S(1)} %get-tuple-element.53), channel_id=1, source_target_pairs={{0,32},{32,0},{1,33},{33,1},{2,34},{34,2},{3,35},{35,3},{4,36},{36... | collective-permute-start | bytes 884744 | tf_op jit(solution)/shard_map/ppermute | solution.py:327
  136.8 20.6 %collective-permute-start.4 = (bf16[128,1152]{1,0:T(8,128)(2,1)S(1)}, bf16[128,1152]{1,0:T(8,128)(2,1)S(1)}, u32[]{:S(2)}, u32[]{:S(2)}) collective-permute-start(bf16[128,1152]{1,0:T(8,128)(2,1)S(1)} %get-tuple-element.58), channel_id=1, source_target_pairs={{0,32},{32,0},{1,33},{33,1},{2,34},{34,2},{3,35},{35,3},{4,36},{36... | collective-permute-start | bytes 884744 | tf_op jit(solution)/shard_map/ppermute | solution.py:327
  140.7 4.8 %copy-start.19 = (bf16[128,1152]{1,0:T(8,128)(2,1)}, bf16[128,1152]{1,0:T(8,128)(2,1)S(1)}, u32[]{:S(2)}) copy-start(bf16[128,1152]{1,0:T(8,128)(2,1)S(1)} %collective-permute-done.2.far_ref) | copy-start | bytes 884740
  145.4 1.0 copy-start.16
  153.4 11.7 %copy-start.17 = (bf16[64,4096]{1,0:T(8,128)(2,1)S(1)}, bf16[64,4096]{1,0:T(8,128)(2,1)}, u32[]{:S(2)}) copy-start(bf16[64,4096]{1,0:T(8,128)(2,1)} %get-tuple-element.56) | copy-start | bytes 1572868
  153.4 11.7 %collective-permute-start.3 = (bf16[64,4096]{1,0:T(8,128)(2,1)}, bf16[64,4096]{1,0:T(8,128)(2,1)S(1)}, u32[]{:S(2)}, u32[]{:S(2)}) collective-permute-start(bf16[64,4096]{1,0:T(8,128)(2,1)} %get-tuple-element.57), channel_id=1, source_target_pairs={{0,1},{1,0},{2,3},{3,2},{4,5},{5,4},{6,7},{7,6},{8,9},{9,8},{10,11... | collective-permute-start | bytes 1572872 | tf_op jit(solution)/shard_map/ppermute | solution.py:327
  157.4 0.7 copy-start.20
  165.0 2.2 %collective-permute-start.5 = (bf16[64,4096]{1,0:T(8,128)(2,1)}, bf16[64,4096]{1,0:T(8,128)(2,1)S(1)}, u32[]{:S(2)}, u32[]{:S(2)}) collective-permute-start(bf16[64,4096]{1,0:T(8,128)(2,1)} %get-tuple-element.60), channel_id=1, source_target_pairs={{0,1},{1,0},{2,3},{3,2},{4,5},{5,4},{6,7},{7,6},{8,9},{9,8},{10,11... | collective-permute-start | bytes 1572872 | tf_op jit(solution)/shard_map/ppermute | solution.py:327
  168.5 16.2 %collective-permute-start.6 = (bf16[32,4096]{1,0:T(8,128)(2,1)S(1)}, bf16[32,4096]{1,0:T(8,128)(2,1)S(1)}, u32[]{:S(2)}, u32[]{:S(2)}) collective-permute-start(bf16[32,4096]{1,0:T(8,128)(2,1)S(1)} %pad_maximum_fusion), channel_id=1, source_target_pairs={{0,6},{2,4},{4,2},{6,0},{1,7},{3,5},{5,3},{7,1},{8,14},{10,12},{12... | collective-permute-start | bytes 786440 | tf_op jit(solution)/shard_map/ppermute | solution.py:327
  178.1 23.7 %collective-permute-start.7 = (bf16[32,4096]{1,0:T(8,128)(2,1)S(1)}, bf16[32,4096]{1,0:T(8,128)(2,1)S(1)}, u32[]{:S(2)}, u32[]{:S(2)}) collective-permute-start(bf16[32,4096]{1,0:T(8,128)(2,1)S(1)} %pad_maximum_fusion.1), channel_id=1, source_target_pairs={{0,4},{2,6},{4,0},{6,2},{1,5},{3,7},{5,1},{7,3},{8,12},{10,14},{12... | collective-permute-start | bytes 786440 | tf_op jit(solution)/shard_map/ppermute | solution.py:327
  178.4 23.4 %collective-permute-start.8 = (bf16[32,4096]{1,0:T(8,128)(2,1)S(1)}, bf16[32,4096]{1,0:T(8,128)(2,1)S(1)}, u32[]{:S(2)}, u32[]{:S(2)}) collective-permute-start(bf16[32,4096]{1,0:T(8,128)(2,1)S(1)} %pad_maximum_fusion.2), channel_id=1, source_target_pairs={{0,2},{2,0},{4,6},{6,4},{1,3},{3,1},{5,7},{7,5},{8,10},{10,8},{12,... | collective-permute-start | bytes 786440 | tf_op jit(solution)/shard_map/ppermute | solution.py:327
